TPU v7x, 128 devices: a whole 4x4x4 slice. The times are simulated.
128 devices in a mesh: gx: 8 (over x, core), gy: 16 (over y, z).
Axes of the slice: x: 4, y: 4, z: 4, core: 2. Of those that a mesh axis runs over, the one named last changes fastest.
Arguments:
- part_data: bfloat16 [16, 64, 16, 4, 128], P('gx', 'gy'), may hold values from 0 to 1
- tile_cells: int32 [16, 64, 16, 128], P('gx', 'gy'), may hold values from 0 to 511
- tile_counts: int32 [16, 64, 16], P('gx', 'gy'), may hold values from 32 to 128
- ghost_data: bfloat16 [128, 9, 16, 4, 2048], P(('gx', 'gy')), may hold values from 0 to 1
- halo_refined_cells: int32 [128, 9, 16, 2048], P(('gx', 'gy')), may hold values from 0 to 3822, as said below
- ghost_counts: int32 [128, 9, 16], P(('gx', 'gy')), may hold values from 0 to 2048
- virt_data: bfloat16 [128, 9, 4, 512], P(('gx', 'gy')), may hold values from 0 to 1
- virt_cells: int32 [128, 9, 512], P(('gx', 'gy')), may hold values from 0 to 61311, as said below
- phantom_slot_counts: int32 [128, 9], P(('gx', 'gy')), may hold values from 0 to 512
Outputs:
- base_mass: float32 [128, 512, 128], P('gx', 'gy')
- fine_mass: float32 [2048, 4096], P(('gx', 'gy'))
Inputs may be any that keep to these rules, and one draw needn't show every extreme that they name: `halo_refined_cells`: each of the three coordinates (c // 256, c // 16 mod 16, c mod 16) is at most 14. `virt_cells`: the first coordinate is at most 14 and the second at most 30.
All inputs are finite; a program needn't handle non-finite values.
Results may differ from a plain program's by a relative error of at most 0.004.
Values may be sent and summed in bfloat16 or wider, within the bound.
No kernel may reach another device: no remote copies, remote signals or barrier semaphores. Data moves between devices by JAX's collectives and lax.ppermute only.
A program may use at most 128 MiB of HBM per device.

v0:
```python
import functools

import jax
import jax.numpy as jnp
from jax import lax
from jax.experimental import pallas as pl
from jax.experimental.pallas import tpu as pltpu
from jax.sharding import PartitionSpec as P

BF16 = jnp.bfloat16
F32 = jnp.float32
I32 = jnp.int32
NT = (((1,), (1,)), ((), ()))
LANES = 256
UNROLL = 16
PATCHES = 48
VMEM_LIMIT = 56 * 2**20


def shift(x, axis, by):
    devices = lax.axis_size(axis)
    return lax.ppermute(x, axis, [(i, (i + by) % devices) for i in range(devices)])


def sublane(rows, lanes):
    return lax.broadcasted_iota(I32, (rows, lanes), 0).astype(F32)


def dot_nt(a, b):
    return lax.dot_general(a, b, NT, preferred_element_type=F32)


def row8(ref, row):
    return ref[pl.ds(row, 8, stride=0), :]


def row16(ref, row):
    return jnp.concatenate([row8(ref, row)] * 2, 0).astype(BF16)


def fine_kernel(base_group, counts, data, cells, out, total, fields, partial):
    total[...] = jnp.zeros_like(total)
    partial[...] = jnp.zeros_like(partial)

    def chunks(group):
        return jnp.maximum((counts[base_group + group] + (LANES - 1)) >> 8, 1)

    work = lax.fori_loop(
        0, PATCHES, lambda group, t: t + chunks(group), jnp.int32(0), unroll=8
    )
    steps = lax.div(work + (UNROLL - 1), UNROLL)
    lane = lax.broadcasted_iota(I32, (1, LANES), 1)
    here = sublane(16, LANES).astype(BF16)
    before = (sublane(16, LANES) - 1.0).astype(BF16)
    rows = sublane(8, LANES)
    zero = jnp.zeros((16, LANES), BF16)

    def deposit(unit, group, chunk):
        patch = jnp.minimum(group, PATCHES - 1)
        live = jnp.where(group < PATCHES, counts[base_group + patch], 0)
        start = pl.multiple_of(chunk * LANES, LANES)
        high = data[patch, :, pl.ds(start, LANES)].astype(F32)
        cell = cells[pl.ds(patch, 1), pl.ds(start, LANES)]
        low = 1.0 - high
        mass = jnp.where(lane < live - start, high[0:1], 0.0)
        f = fields.at[unit]
        f[0:4, :] = high
        f[4:8, :] = low
        f[8:9, :] = high[3:4] * mass
        f[9:10, :] = low[3:4] * mass
        f[10:11, :] = (cell >> 8).astype(F32)
        f[11:12, :] = (cell & 15).astype(F32)
        f[12:13, :] = ((cell >> 4) & 3).astype(F32)
        f[13:14, :] = ((cell >> 6) & 3).astype(F32)
        inner = row8(f, 12)
        f[16:24, :] = jnp.where(
            rows == inner, row8(f, 6), jnp.where(rows - 1.0 == inner, row8(f, 2), 0.0)
        )
        x, outer, z = row16(f, 10), row16(f, 13), row16(f, 11)
        along_x = jnp.where(here == x, row16(f, 5), jnp.where(before == x, row16(f, 1), zero))
        along_z = jnp.where(here == z, row16(f, 9), jnp.where(before == z, row16(f, 8), zero))
        left = jnp.concatenate(
            [jnp.where(outer == BF16(k), along_x, zero) for k in range(4)], 0
        )
        right = jnp.concatenate([row16(f, 16 + k) * along_z for k in range(5)], 0)
        partial[unit, :, 0:80] = dot_nt(left, right)
        last = chunk + 1 >= chunks(patch)
        return patch, jnp.where(last, group + 1, group), jnp.where(last, 0, chunk + 1)

    def body(_, carry):
        group, chunk, *old = carry
        new = []
        for unit in range(UNROLL):
            total[old[unit]] += partial[unit]
            patch, group, chunk = deposit(unit, group, chunk)
            new.append(patch)
        return (group, chunk, *new)

    carry = lax.fori_loop(0, steps, body, (jnp.int32(0),) * (UNROLL + 2))
    for unit in range(UNROLL):
        total[carry[2 + unit]] += partial[unit]
    lane = lax.broadcasted_iota(I32, (16, 128), 1)

    def fold(group, _):
        for half in range(2):
            at = 32 * half
            even = total[group, at : at + 16]
            odd = total[group, at + 16 : at + 32]
            prior = total[group, at - 16 : at] if half else jnp.zeros((16, 128), F32)
            swapped = pltpu.roll(jnp.where(lane < 64, odd, prior), 64, 1)
            out[group, 16 * half : 16 * half + 16] = (even + swapped).astype(BF16)
        return 0

    lax.fori_loop(0, PATCHES, fold, 0, unroll=8)


def fine_part(part, counts, data, cells):
    slots = data.shape[2]
    return pl.pallas_call(
        functools.partial(fine_kernel, PATCHES * part),
        grid_spec=pltpu.PrefetchScalarGridSpec(
            num_scalar_prefetch=1,
            grid=(1,),
            in_specs=[
                pl.BlockSpec((PATCHES, 4, slots), lambda i, c: (part, 0, 0)),
                pl.BlockSpec((PATCHES, slots), lambda i, c: (part, 0)),
            ],
            out_specs=pl.BlockSpec((PATCHES, 32, 128), lambda i, c: (0, 0, 0)),
            scratch_shapes=[
                pltpu.VMEM((PATCHES, 64, 128), F32),
                pltpu.VMEM((UNROLL, 24, LANES), F32),
                pltpu.VMEM((UNROLL, 64, 128), F32),
            ],
        ),
        out_shape=jax.ShapeDtypeStruct((PATCHES, 32, 128), BF16),
        compiler_params=pltpu.CompilerParams(vmem_limit_bytes=VMEM_LIMIT),
        cost_estimate=pl.CostEstimate(
            flops=2 * PATCHES * slots * 64 * 128, bytes_accessed=1600000, transcendentals=0
        ),
        name="fine",
    )(counts, data, cells)


def tile_kernel(
    counts, vcounts, data, cells, vdata, vcells, core, face_x, face_y, *rest
):
    packs, (grid, fields) = rest[:3], rest[3:]
    grid[...] = jnp.zeros_like(grid)
    lane = lax.broadcasted_iota(I32, (1, 512), 1)
    for offset in range(9):
        high = vdata[offset].astype(F32)
        pack = packs[offset // 3].at[offset % 3]
        pack[0:1, :] = jnp.where(lane < vcounts[offset], high[0:1], 0.0)
        pack[1:4, :] = high[1:4]
        pack[4:5, :] = vcells[offset : offset + 1, :].astype(F32)
        pack[5:8, :] = jnp.zeros((3, 512), F32)
    lane = lax.broadcasted_iota(I32, (1, 128), 1)
    here = sublane(16, LANES).astype(BF16)
    before = (sublane(16, LANES) - 1.0).astype(BF16)
    fifteen = (sublane(16, LANES) + 15.0).astype(BF16)
    rows = sublane(16, LANES)
    zero = jnp.zeros((16, LANES), BF16)

    def column(col, _):
        acc = jnp.zeros((144, 128), F32)
        for pair in range(8):
            tile = col * 16 + 2 * pair
            f = fields.at[pair]
            high = jnp.concatenate(
                [data[tile].astype(F32), data[tile + 1].astype(F32)], 1
            )
            low = 1.0 - high
            live = jnp.concatenate(
                [jnp.where(lane < counts[tile], 1.0, 0.0),
                 jnp.where(lane < counts[tile + 1], 1.0, 0.0)], 1
            )
            cell = jnp.concatenate(
                [cells[pl.ds(tile, 1), :], cells[pl.ds(tile + 1, 1), :] + 1024], 1
            )
            mass = high[0:1] * live
            f[0:4, :] = high
            f[4:8, :] = low
            f[8:9, :] = high[3:4] * mass
            f[9:10, :] = low[3:4] * mass
            f[10:11, :] = ((cell >> 6) & 7).astype(F32)
            f[11:12, :] = ((cell >> 3) & 7).astype(F32)
            f[12:13, :] = ((cell & 7) + ((cell >> 10) << 3)).astype(F32)
            x = jnp.concatenate([row8(f, 10)] * 2, 0)
            low_x = jnp.concatenate([row8(f, 5)] * 2, 0)
            high_x = jnp.concatenate([row8(f, 1)] * 2, 0)
            f[16:32, :] = jnp.where(
                rows == x, low_x, jnp.where(rows - 1.0 == x, high_x, 0.0)
            )
            y, z = row16(f, 11), row16(f, 12)
            c0, c1 = row16(f, 9), row16(f, 8)
            along_y = jnp.where(
                here == y, row16(f, 6), jnp.where(before == y, row16(f, 2), zero)
            )
            along_z = jnp.concatenate(
                [jnp.where(here == z, c0, jnp.where(before == z, c1, zero)),
                 jnp.where(fifteen == z, c1, zero)], 0
            )
            left = jnp.concatenate([row16(f, 16 + k) * along_y for k in range(9)], 0)
            part = jnp.concatenate(
                [dot_nt(left, along_z), jnp.zeros((144, 96), F32)], 1
            )
            acc = acc + (pltpu.roll(part, 16 * pair, 1) if pair else part)
        tx = col >> 2
        ty = col & 3
        for k in range(9):
            grid[8 * tx + k, pl.ds(pl.multiple_of(8 * ty, 8), 16), :] += acc[
                16 * k : 16 * k + 16
            ]
        return 0

    lax.fori_loop(0, 8, column, 0)
    core[...] = grid[0:16, 0:32, :]
    face_x[...] = grid[16]
    face_y[...] = grid[0:16, 32, :]


def tile_part(counts, vcounts, data, cells, vdata, vcells):
    full = pl.BlockSpec(memory_space=pltpu.VMEM)
    smem = pl.BlockSpec(memory_space=pltpu.SMEM)
    return pl.pallas_call(
        tile_kernel,
        in_specs=[smem, smem, full, full, full, full],
        out_specs=[full] * 6,
        out_shape=[
            jax.ShapeDtypeStruct((16, 32, 128), F32),
            jax.ShapeDtypeStruct((40, 128), F32),
            jax.ShapeDtypeStruct((16, 128), F32),
        ]
        + [jax.ShapeDtypeStruct((3, 8, 512), F32)] * 3,
        scratch_shapes=[
            pltpu.VMEM((17, 40, 128), F32),
            pltpu.VMEM((8, 32, LANES), F32),
        ],
        compiler_params=pltpu.CompilerParams(vmem_limit_bytes=VMEM_LIMIT),
        name="tiles",
    )(counts, vcounts, data, cells, vdata, vcells)


def base_kernel(pack_own, pack_up, pack_down, core, from_x, from_y, out, fields):
    out[...] = core[...].reshape(512, 128)
    out[0:32, :] += from_x[0:32, :]
    for x in range(16):
        out[32 * x : 32 * x + 1, :] += from_y[x : x + 1, :]
    lanes = 512
    rows = sublane(16, lanes)
    zero = jnp.zeros((16, lanes), BF16)

    def place(at):
        return (rows + float(at)).astype(BF16)

    def one(source, index):
        f = fields
        high = source[index, 0:4, :]
        low = 1.0 - high
        cell = source[index, 4:5, :].astype(I32)
        mass = high[0:1]
        f[0:4, :] = high
        f[4:8, :] = low
        f[8:9, :] = high[3:4] * mass
        f[9:10, :] = low[3:4] * mass
        f[10:11, :] = (cell >> 12).astype(F32)
        f[11:12, :] = ((cell >> 7) & 31).astype(F32)
        f[12:13, :] = (cell & 127).astype(F32)
        f[13:14, :] = ((cell + 1) & 127).astype(F32)
        x = jnp.concatenate([row8(f, 10)] * 2, 0)
        low_x = jnp.concatenate([row8(f, 5)] * 2, 0)
        high_x = jnp.concatenate([row8(f, 1)] * 2, 0)
        f[16:32, :] = jnp.where(
            rows == x, low_x, jnp.where(rows - 1.0 == x, high_x, 0.0)
        )
        y, z, z_next = row16(f, 11), row16(f, 12), row16(f, 13)
        c0, c1 = row16(f, 9), row16(f, 8)
        y0, y1 = row16(f, 6), row16(f, 2)
        along_y = [
            jnp.where(place(16 * h) == y, y0, jnp.where(place(16 * h - 1) == y, y1, zero))
            for h in range(2)
        ]
        along_z = jnp.concatenate(
            [
                jnp.where(
                    place(16 * k) == z, c0, jnp.where(place(16 * k) == z_next, c1, zero)
                )
                for k in range(8)
            ],
            0,
        )
        left = []
        for k in range(16):
            w = row16(f, 16 + k)
            left += [w * along_y[0], w * along_y[1]]
        out[...] += dot_nt(jnp.concatenate(left, 0), along_z)

    for source in (pack_own, pack_up, pack_down):
        def body(index, _, source=source):
            one(source, index)
            return 0
        lax.fori_loop(0, 3, body, 0)


def base_part(*args):
    full = pl.BlockSpec(memory_space=pltpu.VMEM)
    return pl.pallas_call(
        base_kernel,
        in_specs=[full] * 6,
        out_specs=full,
        out_shape=jax.ShapeDtypeStruct((512, 128), F32),
        scratch_shapes=[pltpu.VMEM((32, 512), F32)],
        compiler_params=pltpu.CompilerParams(vmem_limit_bytes=VMEM_LIMIT),
        cost_estimate=pl.CostEstimate(
            flops=2 * 9 * 512 * 512 * 128, bytes_accessed=1000000, transcendentals=0
        ),
        name="base",
    )(*args)


def sum_kernel(own, left, right, up, down, out, lines):
    for patch in range(16):
        mass = (
            (own[patch].astype(F32) + left[patch].astype(F32))
            + (right[patch].astype(F32) + up[patch].astype(F32))
        ) + down[patch].astype(F32)
        lines[32 * patch : 32 * patch + 32, :] = mass
    for group in range(2):
        for half in range(2):
            for x in range(16):
                block = lines[pl.ds(256 * group + 16 * half + x, 8, stride=32), :]
                at = 128 * (2 * x + half)
                out[8 * group : 8 * group + 8, at : at + 128] = block


def sum_part(own, left, right, up, down):
    part = pl.BlockSpec((16, 32, 128), lambda i: (1, 0, 0))
    full = pl.BlockSpec((16, 32, 128), lambda i: (0, 0, 0))
    return pl.pallas_call(
        sum_kernel,
        grid=(1,),
        in_specs=[part, part, part, full, full],
        out_specs=pl.BlockSpec((16, 4096), lambda i: (0, 0)),
        out_shape=jax.ShapeDtypeStruct((16, 4096), F32),
        scratch_shapes=[pltpu.VMEM((512, 128), F32)],
        compiler_params=pltpu.CompilerParams(vmem_limit_bytes=VMEM_LIMIT),
        name="patches",
    )(own, left, right, up, down)


def on_device(
    part_data,
    tile_cells,
    tile_counts,
    ghost_data,
    halo_refined_cells,
    ghost_counts,
    virt_data,
    virt_cells,
    phantom_slot_counts,
):
    core, face_x, face_y, pack_m, pack_0, pack_p = tile_part(
        tile_counts.reshape(128),
        phantom_slot_counts.reshape(9),
        part_data.reshape(128, 4, 128),
        tile_cells.reshape(128, 128),
        virt_data.reshape(9, 4, 512),
        virt_cells.reshape(9, 512),
    )
    counts = ghost_counts.reshape(144)
    data = ghost_data.reshape(144, 4, 2048)
    cells = halo_refined_cells.reshape(144, 2048)

    pack_r = shift(pack_m, "gx", -1)
    pack_l = shift(pack_p, "gx", 1)
    from_x = shift(face_x, "gx", 1)
    fine_m = fine_part(0, counts, data, cells)
    fine_r = shift(fine_m, "gx", -1)

    pack_all = jnp.stack([pack_0, pack_r, pack_l])
    pack_up = shift(pack_all[:, 0], "gy", -1)
    pack_down = shift(pack_all[:, 2], "gy", 1)
    from_y = shift(face_y.at[0].add(from_x[32]), "gy", 1)
    fine_p = fine_part(2, counts, data, cells)
    fine_l = shift(fine_p, "gx", 1)
    fine_0 = fine_part(1, counts, data, cells)

    def joint(at):
        part = slice(16 * at, 16 * at + 16)
        return (
            fine_0[part].astype(F32) + fine_r[part].astype(F32) + fine_l[part].astype(F32)
        ).astype(BF16)

    up = shift(joint(0), "gy", -1)
    down = shift(joint(2), "gy", 1)
    base = base_part(pack_all[:, 1], pack_up, pack_down, core, from_x, from_y)
    fine_mass = sum_part(fine_0, fine_r, fine_l, up, down)
    return base.reshape(16, 32, 128), fine_mass


def solution(mesh):
    return jax.shard_map(
        on_device,
        mesh=mesh,
        in_specs=(
            P("gx", "gy", None, None, None),
            P("gx", "gy", None, None),
            P("gx", "gy", None),
            P(("gx", "gy"), None, None, None, None),
            P(("gx", "gy"), None, None, None),
            P(("gx", "gy"), None, None),
            P(("gx", "gy"), None, None, None),
            P(("gx", "gy"), None, None),
            P(("gx", "gy"), None),
        ),
        out_specs=(P("gx", "gy", None), P(("gx", "gy"), None)),
        check_vma=False,
    )
```

profile of v0, /device:TPU:0, one launch (start us, length us, event | category | flops | bytes accessed | tf_op | source)
XLA Modules:
  0.0 74.2 jit_solution(4587952186473033041)
XLA Ops:
  0.6 0.7 reduce.2
  1.3 0.7 reshape.66.counts
  2.0 10.6 %fine.4 = bf16[48,32,128]{2,1,0:T(8,128)(2,1)} custom-call(s32[144]{0:T(256)} %reshape.66.counts, bf16[144,4,2048]{2,1,0:T(4,128)(2,1)} %bitcast.27, s32[144,2048]{1,0:T(8,128)} %bitcast.30), custom_call_target="tpu_custom_call" | custom-call | flops 1610612736 | bytes 1600000 | tf_op jit(solution)/shard_map/fine/pallas_call | solution.py:119
  12.6 0.0 copy-start.6
  12.6 0.0 copy-start.5
  12.6 1.4 %collective-permute-start.6 = (bf16[48,32,128]{2,1,0:T(8,128)(2,1)}, bf16[48,32,128]{2,1,0:T(8,128)(2,1)S(1)}, u32[]{:S(2)}, u32[]{:S(2)}) collective-permute-start(bf16[48,32,128]{2,1,0:T(8,128)(2,1)} %fine.4), channel_id=1, source_target_pairs={{0,112},{16,0},{32,16},{48,32},{64,48},{80,64},{96,80},{112,96},{1... | collective-permute-start | bytes 1179656 | tf_op jit(solution)/shard_map/ppermute | solution.py:22
  14.0 10.1 %fine.5 = bf16[48,32,128]{2,1,0:T(8,128)(2,1)} custom-call(s32[144]{0:T(256)} %reshape.66.counts, bf16[144,4,2048]{2,1,0:T(4,128)(2,1)} %bitcast.28, s32[144,2048]{1,0:T(8,128)} %bitcast.31), custom_call_target="tpu_custom_call" | custom-call | flops 1610612736 | bytes 1600000 | tf_op jit(solution)/shard_map/fine/pallas_call | solution.py:119
  24.1 0.0 collective-permute-start.7
  24.1 0.0 copy-done.6
  24.1 0.6 reshape.59.counts
  24.7 0.0 copy-done.5
  24.7 0.6 copy.13
  25.3 5.1 %tiles.1 = (f32[16,32,128]{2,1,0:T(8,128)}, f32[40,128]{1,0:T(8,128)}, f32[16,128]{1,0:T(8,128)}, f32[3,8,512]{2,1,0:T(8,128)}, f32[3,8,512]{2,1,0:T(8,128)}, /*index=5*/f32[3,8,512]{2,1,0:T(8,128)}) custom-call(s32[128]{0:T(128)} %reshape.59.counts, s32[9]{0:T(128)} %bitcast.26, bf16[128,4,128]{2,1,0:T(4,128)(2,1)} %bitcast.19, s32[128,128]{1,0:T(8,128)} %bitcast.21, ...), custom_call_target="tpu_custom_call" | custom-call | tf_op jit(solution)/shard_map/tiles/pallas_call | solution.py:225
  30.4 0.0 collective-permute-start.4
  30.4 3.0 %collective-permute-start = (f32[3,8,512]{2,1,0:T(8,128)}, f32[3,8,512]{2,1,0:T(8,128)S(1)}, u32[]{:S(2)}, u32[]{:S(2)}) collective-permute-start(f32[3,8,512]{2,1,0:T(8,128)} %get-tuple-element.21), channel_id=1, source_target_pairs={{0,112},{16,0},{32,16},{48,32},{64,48},{80,64},{96,80},{112,96},{1... | collective-permute-start | bytes 147464 | tf_op jit(solution)/shard_map/ppermute | solution.py:22
  33.4 0.0 copy-start.4
  33.4 0.0 copy-start.10
  33.4 0.0 collective-permute-start.1
  33.4 11.2 %fine.3.own = bf16[48,32,128]{2,1,0:T(8,128)(2,1)} custom-call(s32[144]{0:T(256)} %reshape.66.counts, bf16[144,4,2048]{2,1,0:T(4,128)(2,1)} %bitcast.29, s32[144,2048]{1,0:T(8,128)} %bitcast.32), custom_call_target="tpu_custom_call" | custom-call | flops 1610612736 | bytes 1600000 | tf_op jit(solution)/shard_map/fine/pallas_call | solution.py:119
  44.5 0.0 collective-permute-done
  44.5 0.0 collective-permute-done.1
  44.5 0.0 copy-done.4
  44.6 0.6 slice_bitcast_fusion
  45.2 0.5 collective-permute-start.3
  45.7 6.0 %collective-permute-start.2 = (f32[3,8,512]{2,1,0:T(8,128)S(1)}, f32[3,8,512]{2,1,0:T(8,128)S(1)}, u32[]{:S(2)}, u32[]{:S(2)}) collective-permute-start(f32[3,8,512]{2,1,0:T(8,128)S(1)} %get-tuple-element.29), channel_id=1, source_target_pairs={{0,15},{1,0},{2,1},{3,2},{4,3},{5,4},{6,5},{7,6},{8,7},{9,8},{10,9... | collective-permute-start | bytes 147464 | tf_op jit(solution)/shard_map/ppermute | solution.py:22
  51.7 0.0 collective-permute-done.6.left
  51.7 0.0 copy-start
  51.7 0.0 collective-permute-done.7.right
  51.7 0.0 copy-start.1
  51.7 1.4 %add_convert_fusion = (bf16[16,32,128]{2,1,0:T(8,128)(2,1)S(1)}, bf16[16,32,128]{2,1,0:T(8,128)(2,1)S(1)}) fusion(bf16[48,32,128]{2,1,0:T(8,128)(2,1)S(1)} %collective-permute-done.7.right, bf16[48,32,128]{2,1,0:T(8,128)(2,1)S(1)} %collective-permute-done.6.left, bf16[48,32,128]{2,1,0:T(8,128)(2,1)} %fine.3.own), kind=kLoop, calls=%fused_computation | loop fusion | flops 786432 | bytes 1048576 | tf_op jit(solution)/shard_map/convert_element_type | solution.py:392
  53.1 0.1 collective-permute-start.9
  53.2 5.3 %collective-permute-start.8 = (bf16[16,32,128]{2,1,0:T(8,128)(2,1)S(1)}, bf16[16,32,128]{2,1,0:T(8,128)(2,1)S(1)}, u32[]{:S(2)}, u32[]{:S(2)}) collective-permute-start(bf16[16,32,128]{2,1,0:T(8,128)(2,1)S(1)} %get-tuple-element.27), channel_id=1, source_target_pairs={{0,15},{1,0},{2,1},{3,2},{4,3},{5,4},{6,5},{7,6},{8,7},{9,8},{10,9... | collective-permute-start | bytes 393224 | tf_op jit(solution)/shard_map/ppermute | solution.py:22
  58.5 0.0 collective-permute-done.4.from_x
  58.5 0.0 copy-start.9
  58.5 0.0 copy-done.10
  58.5 0.1 collective-permute-start.5
  58.6 7.0 %collective-permute-done.5.from_y = f32[16,128]{1,0:T(8,128)S(1)} collective-permute-done((f32[16,128]{1,0:T(8,128)S(1)}, f32[16,128]{1,0:T(8,128)S(1)}, u32[]{:S(2)}, u32[]{:S(2)}) %collective-permute-start.5) | collective-permute-done | bytes 8224 | tf_op jit(solution)/shard_map/ppermute | solution.py:22
  65.6 0.0 copy-start.11
  65.6 0.0 collective-permute-done.3.pack_down
  65.6 0.0 copy-start.7
  65.6 0.0 collective-permute-done.2.pack_up
  65.6 0.0 copy-start.8
  65.6 0.0 copy-done.9
  65.6 0.6 copy-done.11
  66.2 0.0 copy-done.7
  66.2 0.0 copy-done.8
  66.2 4.6 %base.1 = f32[512,128]{1,0:T(8,128)} custom-call(f32[3,8,512]{2,1,0:T(8,128)} %get-tuple-element.30.pack_own, f32[3,8,512]{2,1,0:T(8,128)} %copy-done.8, f32[3,8,512]{2,1,0:T(8,128)} %copy-done.7, f32[16,32,128]{2,1,0:T(8,128)} %get-tuple-element.23.core, f32[40,128]{1,0:T(8,128)} %copy-done.9, f32[16,128]{1,0:T(8,128)} %copy-done.11), custom_call_target="tpu_custom_call" | custom-call | flops 603979776 | bytes 1000000 | tf_op jit(solution)/shard_map/base/pallas_call | solution.py:307
  70.8 0.0 collective-permute-done.9.down
  70.8 0.0 copy-start.2
  70.8 0.0 collective-permute-done.8.up
  70.8 0.0 copy-done
  70.8 0.0 copy-done.1
  70.8 0.6 copy-done.2
  71.5 0.0 copy-start.3
  71.5 0.6 copy-done.3
  72.1 2.1 %patches.1 = f32[16,4096]{1,0:T(8,128)} custom-call(bf16[48,32,128]{2,1,0:T(8,128)(2,1)} %fine.3.own, bf16[48,32,128]{2,1,0:T(8,128)(2,1)} %copy-done, bf16[48,32,128]{2,1,0:T(8,128)(2,1)} %copy-done.1, bf16[16,32,128]{2,1,0:T(8,128)(2,1)} %copy-done.3, bf16[16,32,128]{2,1,0:T(8,128)(2,1)} %copy-done.2), custom_call_target="tpu_custom_call" | custom-call | tf_op jit(solution)/shard_map/patches/pallas_call | solution.py:339
  (3 shorter events, 0.1 us)
Async XLA Ops:
  12.6 11.5 %copy-start.6 = (s32[2,4,16]{2,1,0:T(4,128)S(1)}, s32[2,4,16]{2,1,0:T(4,128)}, u32[]{:S(2)}) copy-start(s32[2,4,16]{2,1,0:T(4,128)} %param.13) | copy-start | bytes 1540
  12.6 12.1 %copy-start.5 = (s32[1,9,512]{2,0,1:T(1,128)S(1)}, s32[1,9,512]{2,0,1:T(1,128)}, u32[]{:S(2)}) copy-start(s32[1,9,512]{2,0,1:T(1,128)} %param.18) | copy-start | bytes 55300
  12.6 39.1 %collective-permute-start.6 = (bf16[48,32,128]{2,1,0:T(8,128)(2,1)}, bf16[48,32,128]{2,1,0:T(8,128)(2,1)S(1)}, u32[]{:S(2)}, u32[]{:S(2)}) collective-permute-start(bf16[48,32,128]{2,1,0:T(8,128)(2,1)} %fine.4), channel_id=1, source_target_pairs={{0,112},{16,0},{32,16},{48,32},{64,48},{80,64},{96,80},{112,96},{1... | collective-permute-start | bytes 1179656 | tf_op jit(solution)/shard_map/ppermute | solution.py:22
  24.1 27.6 %collective-permute-start.7 = (bf16[48,32,128]{2,1,0:T(8,128)(2,1)}, bf16[48,32,128]{2,1,0:T(8,128)(2,1)S(1)}, u32[]{:S(2)}, u32[]{:S(2)}) collective-permute-start(bf16[48,32,128]{2,1,0:T(8,128)(2,1)} %fine.5), channel_id=1, source_target_pairs={{0,16},{16,32},{32,48},{48,64},{64,80},{80,96},{96,112},{112,0},{1... | collective-permute-start | bytes 1179656 | tf_op jit(solution)/shard_map/ppermute | solution.py:22
  30.4 28.1 %collective-permute-start.4 = (f32[40,128]{1,0:T(8,128)}, f32[40,128]{1,0:T(8,128)S(1)}, u32[]{:S(2)}, u32[]{:S(2)}) collective-permute-start(f32[40,128]{1,0:T(8,128)} %get-tuple-element.24), channel_id=1, source_target_pairs={{0,16},{16,32},{32,48},{48,64},{64,80},{80,96},{96,112},{112,0},{1... | collective-permute-start | bytes 61448 | tf_op jit(solution)/shard_map/ppermute | solution.py:22
  30.4 14.1 %collective-permute-start = (f32[3,8,512]{2,1,0:T(8,128)}, f32[3,8,512]{2,1,0:T(8,128)S(1)}, u32[]{:S(2)}, u32[]{:S(2)}) collective-permute-start(f32[3,8,512]{2,1,0:T(8,128)} %get-tuple-element.21), channel_id=1, source_target_pairs={{0,112},{16,0},{32,16},{48,32},{64,48},{80,64},{96,80},{112,96},{1... | collective-permute-start | bytes 147464 | tf_op jit(solution)/shard_map/ppermute | solution.py:22
  33.4 11.2 %copy-start.4 = (f32[3,8,512]{2,1,0:T(8,128)S(1)}, f32[3,8,512]{2,1,0:T(8,128)}, u32[]{:S(2)}) copy-start(f32[3,8,512]{2,1,0:T(8,128)} %get-tuple-element.20) | copy-start | bytes 147460
  33.4 25.1 %copy-start.10 = (f32[16,128]{1,0:T(8,128)S(1)}, f32[16,128]{1,0:T(8,128)}, u32[]{:S(2)}) copy-start(f32[16,128]{1,0:T(8,128)} %get-tuple-element.25) | copy-start | bytes 24580
  33.4 11.2 %collective-permute-start.1 = (f32[3,8,512]{2,1,0:T(8,128)}, f32[3,8,512]{2,1,0:T(8,128)S(1)}, u32[]{:S(2)}, u32[]{:S(2)}) collective-permute-start(f32[3,8,512]{2,1,0:T(8,128)} %get-tuple-element.22), channel_id=1, source_target_pairs={{0,16},{16,32},{32,48},{48,64},{64,80},{80,96},{96,112},{112,0},{1... | collective-permute-start | bytes 147464 | tf_op jit(solution)/shard_map/ppermute | solution.py:22
  45.2 20.4 %collective-permute-start.3 = (f32[3,8,512]{2,1,0:T(8,128)S(1)}, f32[3,8,512]{2,1,0:T(8,128)S(1)}, u32[]{:S(2)}, u32[]{:S(2)}) collective-permute-start(f32[3,8,512]{2,1,0:T(8,128)S(1)} %get-tuple-element.28), channel_id=1, source_target_pairs={{0,1},{1,2},{2,3},{3,4},{4,5},{5,6},{6,7},{7,8},{8,9},{9,10},{10,1... | collective-permute-start | bytes 147464 | tf_op jit(solution)/shard_map/ppermute | solution.py:22
  45.7 19.9 %collective-permute-start.2 = (f32[3,8,512]{2,1,0:T(8,128)S(1)}, f32[3,8,512]{2,1,0:T(8,128)S(1)}, u32[]{:S(2)}, u32[]{:S(2)}) collective-permute-start(f32[3,8,512]{2,1,0:T(8,128)S(1)} %get-tuple-element.29), channel_id=1, source_target_pairs={{0,15},{1,0},{2,1},{3,2},{4,3},{5,4},{6,5},{7,6},{8,7},{9,8},{10,9... | collective-permute-start | bytes 147464 | tf_op jit(solution)/shard_map/ppermute | solution.py:22
  51.7 19.1 %copy-start = (bf16[48,32,128]{2,1,0:T(8,128)(2,1)}, bf16[48,32,128]{2,1,0:T(8,128)(2,1)S(1)}, u32[]{:S(2)}) copy-start(bf16[48,32,128]{2,1,0:T(8,128)(2,1)S(1)} %collective-permute-done.6.left) | copy-start | bytes 1179652
  51.7 19.1 %copy-start.1 = (bf16[48,32,128]{2,1,0:T(8,128)(2,1)}, bf16[48,32,128]{2,1,0:T(8,128)(2,1)S(1)}, u32[]{:S(2)}) copy-start(bf16[48,32,128]{2,1,0:T(8,128)(2,1)S(1)} %collective-permute-done.7.right) | copy-start | bytes 1179652
  53.1 17.7 %collective-permute-start.9 = (bf16[16,32,128]{2,1,0:T(8,128)(2,1)S(1)}, bf16[16,32,128]{2,1,0:T(8,128)(2,1)S(1)}, u32[]{:S(2)}, u32[]{:S(2)}) collective-permute-start(bf16[16,32,128]{2,1,0:T(8,128)(2,1)S(1)} %get-tuple-element.26), channel_id=1, source_target_pairs={{0,1},{1,2},{2,3},{3,4},{4,5},{5,6},{6,7},{7,8},{8,9},{9,10},{10,1... | collective-permute-start | bytes 393224 | tf_op jit(solution)/shard_map/ppermute | solution.py:22
  53.2 17.7 %collective-permute-start.8 = (bf16[16,32,128]{2,1,0:T(8,128)(2,1)S(1)}, bf16[16,32,128]{2,1,0:T(8,128)(2,1)S(1)}, u32[]{:S(2)}, u32[]{:S(2)}) collective-permute-start(bf16[16,32,128]{2,1,0:T(8,128)(2,1)S(1)} %get-tuple-element.27), channel_id=1, source_target_pairs={{0,15},{1,0},{2,1},{3,2},{4,3},{5,4},{6,5},{7,6},{8,7},{9,8},{10,9... | collective-permute-start | bytes 393224 | tf_op jit(solution)/shard_map/ppermute | solution.py:22
  58.5 7.1 %copy-start.9 = (f32[40,128]{1,0:T(8,128)}, f32[40,128]{1,0:T(8,128)S(1)}, u32[]{:S(2)}) copy-start(f32[40,128]{1,0:T(8,128)S(1)} %collective-permute-done.4.from_x) | copy-start | bytes 61444
  58.5 7.0 %collective-permute-start.5 = (f32[16,128]{1,0:T(8,128)S(1)}, f32[16,128]{1,0:T(8,128)S(1)}, u32[]{:S(2)}, u32[]{:S(2)}) collective-permute-start(f32[16,128]{1,0:T(8,128)S(1)} %scatter-add.4), channel_id=1, source_target_pairs={{0,1},{1,2},{2,3},{3,4},{4,5},{5,6},{6,7},{7,8},{8,9},{9,10},{10,1... | collective-permute-start | bytes 24584 | tf_op jit(solution)/shard_map/ppermute | solution.py:22
  65.6 0.6 copy-start.11
  65.6 0.6 copy-start.7
  65.6 0.6 copy-start.8
  70.8 0.7 copy-start.2
  71.5 0.7 copy-start.3
where the time goes:
time: 74.4 us; the launch traced here: 74.2 us
  Pallas kernels  43.7 us (59%)
  starting transfers between devices  16.3 us (22%)
  waiting for transfers between devices  6.98 us (9%)
  local copies, waits for them, and re-layouts  4.44 us (6%)
  other arithmetic  2.09 us (3%)
    pallas_call x3, Pallas kernels, fine_part(): pl.pallas_call(functools.partial(fine_kernel, PATCHES * part), grid_spec=...  31.9 us
    ppermute x10, starting transfers between devices, shift(): lax.ppermute(x, axis, [(i, (i + by) % devices) for i in range(devices)])  16.3 us
    ppermute x10, waiting for transfers between devices, shift(): lax.ppermute(x, axis, [(i, (i + by) % devices) for i in range(devices)])  6.98 us
    pallas_call x1, Pallas kernels, tile_part(): pl.pallas_call(tile_kernel, in_specs=[smem, smem, full, full, full, full]...  5.11 us
    pallas_call x1, Pallas kernels, base_part(): pl.pallas_call(base_kernel, in_specs=[full] * 6, out_specs=full, out_shap...  4.59 us
    unnamed x25, local copies, waits for them, and re-layouts  2.52 us
    pallas_call x1, Pallas kernels, sum_part(): pl.pallas_call(sum_kernel, grid=(1,), in_specs=[part, part, part, full, f...  2.09 us
  transfers between devices with their start and end apart: 10, of which 1 were waited for; matrix products, arithmetic and copies ran while one was open for 4% of the time, Pallas kernels for 42%

commit v1 on v0

v1 whole, which is shorter than its diff:
```python
import functools

import jax
import jax.numpy as jnp
from jax import lax
from jax.experimental import pallas as pl
from jax.experimental.pallas import tpu as pltpu
from jax.sharding import PartitionSpec as P

BF16 = jnp.bfloat16
F32 = jnp.float32
I32 = jnp.int32
NT = (((1,), (1,)), ((), ()))
LANES = 256
UNROLL = 16
PATCHES = 48
VMEM_LIMIT = 56 * 2**20


def shift(x, axis, by):
    devices = lax.axis_size(axis)
    return lax.ppermute(x, axis, [(i, (i + by) % devices) for i in range(devices)])


def sublane(rows, lanes):
    return lax.broadcasted_iota(I32, (rows, lanes), 0).astype(F32)


def dot_nt(a, b):
    return lax.dot_general(a, b, NT, preferred_element_type=F32)


def row8(ref, row):
    return ref[pl.ds(row, 8, stride=0), :]


def row16(ref, row):
    return jnp.concatenate([row8(ref, row)] * 2, 0).astype(BF16)


def high_low(x):
    high = x.astype(BF16)
    return high, (x - high.astype(F32)).astype(BF16)


def pack_virtual(offset, counts, data, cells, lines):
    lane = lax.broadcasted_iota(I32, (1, 512), 1)
    high = data[0, offset].astype(F32)
    cell = cells[0, offset : offset + 1, :]
    values = [
        jnp.where(lane < counts[0, offset], high[0:1], 0.0),
        high[1:2],
        high[2:3],
        high[3:4],
        (cell >> 8).astype(F32),
        (cell & 255).astype(F32),
    ]
    for field, value in enumerate(values):
        for quarter in range(4):
            at = 4 * field + quarter
            lines[at : at + 1, :] = value[:, 128 * quarter : 128 * quarter + 128]
    lines[24:32, :] = jnp.zeros((8, 128), F32)
    return lines[...].astype(BF16)


def fine_kernel(offsets, split, counts, vcounts, data_hbm, cells_hbm, vdata, vcells, face, wait, *rest):
    outs, rest = rest[:split], rest[split:]
    data, cells, total, fields, partial, lines, number, sems = rest
    patches = 16 * len(offsets)
    copies = []
    for at, offset in enumerate(offsets):
        copies.append(
            pltpu.make_async_copy(
                data_hbm.at[0, offset], data.at[pl.ds(16 * at, 16)], sems.at[2 * at]
            )
        )
        copies.append(
            pltpu.make_async_copy(
                cells_hbm.at[0, offset], cells.at[pl.ds(16 * at, 16)], sems.at[2 * at + 1]
            )
        )
    for copy in copies:
        copy.start()
    total[...] = jnp.zeros_like(total)
    partial[...] = jnp.zeros_like(partial)
    work = jnp.int32(0)
    for at, offset in enumerate(offsets):
        for patch in range(16):
            live = counts[0, offset, patch]
            number[16 * at + patch] = live
            work = work + jnp.maximum((live + (LANES - 1)) >> 8, 1)
    for extra in range(UNROLL + 4):
        number[patches + extra] = 0
    steps = lax.div(work + (UNROLL - 1), UNROLL)
    each = len(offsets) // split
    for index, offset in enumerate(offsets):
        slot = 17 * (index % each) + 16
        outs[index // each][slot] = pack_virtual(offset, vcounts, vdata, vcells, lines)
    if len(offsets) == 6:
        high, low = high_low(face[...])
        outs[1][51] = high[0:32]
        outs[1][52] = low[0:32]
        high, low = high_low(jnp.concatenate([face[32:40, :], jnp.zeros((8, 128), F32)], 0))
        outs[1][53] = jnp.concatenate([high, low], 0)
    lane = lax.broadcasted_iota(I32, (1, LANES), 1)
    here = sublane(16, LANES).astype(BF16)
    before = (sublane(16, LANES) - 1.0).astype(BF16)
    rows = sublane(8, LANES)
    zero = jnp.zeros((16, LANES), BF16)
    for copy in copies:
        copy.wait()

    def deposit(unit, group, start, live, next_one, next_two):
        patch = jnp.minimum(group, patches - 1)
        at = pl.multiple_of(start, LANES)
        high = data[patch, :, pl.ds(at, LANES)].astype(F32)
        cell = cells[pl.ds(patch, 1), pl.ds(at, LANES)]
        low = 1.0 - high
        mass = jnp.where(lane < live, high[0:1], 0.0)
        f = fields.at[unit]
        f[0:4, :] = high
        f[4:8, :] = low
        f[8:9, :] = high[3:4] * mass
        f[9:10, :] = low[3:4] * mass
        f[10:11, :] = (cell >> 8).astype(F32)
        f[11:12, :] = (cell & 15).astype(F32)
        f[12:13, :] = ((cell >> 4) & 3).astype(F32)
        f[13:14, :] = ((cell >> 6) & 3).astype(F32)
        inner = row8(f, 12)
        f[16:24, :] = jnp.where(
            rows == inner, row8(f, 6), jnp.where(rows - 1.0 == inner, row8(f, 2), 0.0)
        )
        x, outer, z = row16(f, 10), row16(f, 13), row16(f, 11)
        along_x = jnp.where(here == x, row16(f, 5), jnp.where(before == x, row16(f, 1), zero))
        along_z = jnp.where(here == z, row16(f, 9), jnp.where(before == z, row16(f, 8), zero))
        left = jnp.concatenate(
            [jnp.where(outer == BF16(k), along_x, zero) for k in range(4)], 0
        )
        right = jnp.concatenate([row16(f, 16 + k) * along_z for k in range(5)], 0)
        partial[unit, :, 0:80] = dot_nt(left, right)
        last = live <= LANES
        group = jnp.where(last, group + 1, group)
        return patch, (
            group,
            jnp.where(last, 0, start + LANES),
            jnp.where(last, next_one, live - LANES),
            jnp.where(last, next_two, next_one),
            number[group + 2],
        )

    def body(_, carry):
        state, old = carry[:5], carry[5:]
        new = []
        for unit in range(UNROLL):
            total[old[unit]] += partial[unit]
            patch, state = deposit(unit, *state)
            new.append(patch)
        return (*state, *new)

    none = jnp.int32(0)
    carry = lax.fori_loop(
        0, steps, body, (none, none, number[0], number[1], number[2]) + (none,) * UNROLL
    )
    for unit in range(UNROLL):
        total[carry[5 + unit]] += partial[unit]
    lane = lax.broadcasted_iota(I32, (16, 128), 1)

    for index in range(split):
        out = outs[index]

        def fold(k, _, index=index, out=out):
            group = 16 * each * index + k
            for half in range(2):
                at = 32 * half
                even = total[group, at : at + 16]
                odd = total[group, at + 16 : at + 32]
                prior = total[group, at - 16 : at] if half else jnp.zeros((16, 128), F32)
                swapped = pltpu.roll(jnp.where(lane < 64, odd, prior), 64, 1)
                out[k + (k >> 4), 16 * half : 16 * half + 16] = (even + swapped).astype(BF16)
            return 0

        lax.fori_loop(0, 16 * each, fold, 0, unroll=8)


def fine_part(offsets, sizes, counts, vcounts, data, cells, vdata, vcells, face, wait):
    slots = data.shape[4]
    patches = 16 * len(offsets)
    full = pl.BlockSpec(memory_space=pltpu.VMEM)
    smem = pl.BlockSpec(memory_space=pltpu.SMEM)
    anywhere = pl.BlockSpec(memory_space=pl.ANY)
    return pl.pallas_call(
        functools.partial(fine_kernel, offsets, len(sizes)),
        in_specs=[smem, smem, anywhere, anywhere, full, full, full, anywhere],
        out_specs=[full] * len(sizes),
        scratch_shapes=[
            pltpu.VMEM((patches, 4, slots), BF16),
            pltpu.VMEM((patches, slots), I32),
            pltpu.VMEM((patches, 64, 128), F32),
            pltpu.VMEM((UNROLL, 24, LANES), F32),
            pltpu.VMEM((UNROLL, 64, 128), F32),
            pltpu.VMEM((32, 128), F32),
            pltpu.SMEM((patches + UNROLL + 4,), I32),
            pltpu.SemaphoreType.DMA((2 * len(offsets),)),
        ],
        out_shape=[jax.ShapeDtypeStruct((size, 32, 128), BF16) for size in sizes],
        compiler_params=pltpu.CompilerParams(vmem_limit_bytes=VMEM_LIMIT),
        cost_estimate=pl.CostEstimate(
            flops=4 * patches * slots * 64 * 128, bytes_accessed=40000 * patches, transcendentals=0
        ),
        name="fine",
    )(counts, vcounts, data, cells, vdata, vcells, face, wait)


def tile_kernel(counts, data, cells, core, face_x, face_y, grid, fields):
    grid[...] = jnp.zeros_like(grid)
    lane = lax.broadcasted_iota(I32, (1, 128), 1)
    here = sublane(16, LANES).astype(BF16)
    before = (sublane(16, LANES) - 1.0).astype(BF16)
    fifteen = (sublane(16, LANES) + 15.0).astype(BF16)
    rows = sublane(16, LANES)
    zero = jnp.zeros((16, LANES), BF16)

    def column(col, _):
        tx = col >> 2
        ty = col & 3
        acc = jnp.zeros((144, 128), F32)
        for pair in range(8):
            tz = 2 * pair
            f = fields.at[pair]
            high = jnp.concatenate(
                [data[tx, ty, tz].astype(F32), data[tx, ty, tz + 1].astype(F32)], 1
            )
            low = 1.0 - high
            live = jnp.concatenate(
                [jnp.where(lane < counts[tx, ty, tz], 1.0, 0.0),
                 jnp.where(lane < counts[tx, ty, tz + 1], 1.0, 0.0)], 1
            )
            cell = jnp.concatenate(
                [cells[tx, ty, tz : tz + 1, :], cells[tx, ty, tz + 1 : tz + 2, :] + 1024], 1
            )
            mass = high[0:1] * live
            f[0:4, :] = high
            f[4:8, :] = low
            f[8:9, :] = high[3:4] * mass
            f[9:10, :] = low[3:4] * mass
            f[10:11, :] = ((cell >> 6) & 7).astype(F32)
            f[11:12, :] = ((cell >> 3) & 7).astype(F32)
            f[12:13, :] = ((cell & 7) + ((cell >> 10) << 3)).astype(F32)
            x = jnp.concatenate([row8(f, 10)] * 2, 0)
            low_x = jnp.concatenate([row8(f, 5)] * 2, 0)
            high_x = jnp.concatenate([row8(f, 1)] * 2, 0)
            f[16:32, :] = jnp.where(
                rows == x, low_x, jnp.where(rows - 1.0 == x, high_x, 0.0)
            )
            y, z = row16(f, 11), row16(f, 12)
            c0, c1 = row16(f, 9), row16(f, 8)
            along_y = jnp.where(
                here == y, row16(f, 6), jnp.where(before == y, row16(f, 2), zero)
            )
            along_z = jnp.concatenate(
                [jnp.where(here == z, c0, jnp.where(before == z, c1, zero)),
                 jnp.where(fifteen == z, c1, zero)], 0
            )
            left = jnp.concatenate([row16(f, 16 + k) * along_y for k in range(9)], 0)
            part = jnp.concatenate(
                [dot_nt(left, along_z), jnp.zeros((144, 96), F32)], 1
            )
            acc = acc + (pltpu.roll(part, 16 * pair, 1) if pair else part)
        for k in range(9):
            grid[8 * tx + k, pl.ds(pl.multiple_of(8 * ty, 8), 16), :] += acc[
                16 * k : 16 * k + 16
            ]
        return 0

    lax.fori_loop(0, 8, column, 0)
    core[...] = grid[0:16, 0:32, :]
    face_x[...] = grid[16]
    face_y[...] = grid[0:16, 32, :]


def tile_part(counts, data, cells):
    full = pl.BlockSpec(memory_space=pltpu.VMEM)
    smem = pl.BlockSpec(memory_space=pltpu.SMEM)
    return pl.pallas_call(
        tile_kernel,
        in_specs=[smem, full, full],
        out_specs=[full] * 3,
        out_shape=[
            jax.ShapeDtypeStruct((16, 32, 128), F32),
            jax.ShapeDtypeStruct((40, 128), F32),
            jax.ShapeDtypeStruct((16, 128), F32),
        ],
        scratch_shapes=[
            pltpu.VMEM((17, 40, 128), F32),
            pltpu.VMEM((8, 32, LANES), F32),
        ],
        compiler_params=pltpu.CompilerParams(vmem_limit_bytes=VMEM_LIMIT),
        name="tiles",
    )(counts, data, cells)


def virtual_deposit(packs, out, lines, fields):
    lanes = 512
    rows = sublane(16, lanes)
    zero = jnp.zeros((16, lanes), BF16)

    def place(at):
        return (rows + float(at)).astype(BF16)

    for which, (source, slot) in enumerate(packs):
        f = fields.at[which & 1]
        g = lines.at[which & 1]
        g[...] = source[slot].astype(F32)

        def value(field):
            return jnp.concatenate(
                [g[4 * field + quarter : 4 * field + quarter + 1, :] for quarter in range(4)], 1
            )

        cell = (value(4) * 256.0 + value(5)).astype(I32)
        mass, fx, fy, fz = value(0), value(1), value(2), value(3)
        f[0:1, :] = fx
        f[1:2, :] = 1.0 - fx
        f[2:3, :] = fy
        f[3:4, :] = 1.0 - fy
        f[4:5, :] = fz * mass
        f[5:6, :] = (1.0 - fz) * mass
        f[10:11, :] = (cell >> 12).astype(F32)
        f[11:12, :] = ((cell >> 7) & 31).astype(F32)
        f[12:13, :] = (cell & 127).astype(F32)
        f[13:14, :] = ((cell + 1) & 127).astype(F32)
        x = jnp.concatenate([row8(f, 10)] * 2, 0)
        low_x = jnp.concatenate([row8(f, 1)] * 2, 0)
        high_x = jnp.concatenate([row8(f, 0)] * 2, 0)
        f[16:32, :] = jnp.where(
            rows == x, low_x, jnp.where(rows - 1.0 == x, high_x, 0.0)
        )
        y, z, z_next = row16(f, 11), row16(f, 12), row16(f, 13)
        c0, c1 = row16(f, 5), row16(f, 4)
        y0, y1 = row16(f, 3), row16(f, 2)
        along_y = [
            jnp.where(place(16 * h) == y, y0, jnp.where(place(16 * h - 1) == y, y1, zero))
            for h in range(2)
        ]
        along_z = jnp.concatenate(
            [
                jnp.where(
                    place(16 * k) == z, c0, jnp.where(place(16 * k) == z_next, c1, zero)
                )
                for k in range(8)
            ],
            0,
        )
        left = []
        for k in range(16):
            w = row16(f, 16 + k)
            left += [w * along_y[0], w * along_y[1]]
        out[...] += dot_nt(jnp.concatenate(left, 0), along_z)


def base_kernel(own, right, left, core, out, lines, fields):
    out[...] = core[...].reshape(512, 128)
    out[0:32, :] += left[51].astype(F32) + left[52].astype(F32)
    virtual_deposit([(own, 16), (right, 33), (left, 33)], out, lines, fields)


def base_part(*args):
    full = pl.BlockSpec(memory_space=pltpu.VMEM)
    return pl.pallas_call(
        base_kernel,
        in_specs=[full] * 4,
        out_specs=full,
        out_shape=jax.ShapeDtypeStruct((512, 128), F32),
        scratch_shapes=[pltpu.VMEM((2, 32, 128), F32), pltpu.VMEM((2, 32, 512), F32)],
        compiler_params=pltpu.CompilerParams(vmem_limit_bytes=VMEM_LIMIT),
        cost_estimate=pl.CostEstimate(
            flops=6 * 3 * 512 * 512 * 128, bytes_accessed=1000000, transcendentals=0
        ),
        name="base",
    )(*args)


def join_kernel(own, right, left, face_y, up, down):
    for at, (out, slot) in enumerate(((up, 0), (down, 34))):
        for patch in range(16):
            out[patch] = (
                own[17 * at + patch].astype(F32)
                + right[slot + patch].astype(F32)
                + left[slot + patch].astype(F32)
            ).astype(BF16)
        out[16] = own[17 * at + 16]
        out[17] = right[slot + 16]
        out[18] = left[slot + 16]
    corner = left[53].astype(F32)
    row = lax.broadcasted_iota(I32, (16, 128), 0)
    face = face_y[...] + jnp.where(row == 0, corner[0:16] + corner[16:32], 0.0)
    high, low = high_low(face)
    down[19] = jnp.concatenate([high, low], 0)


def join_part(*args):
    full = pl.BlockSpec(memory_space=pltpu.VMEM)
    return pl.pallas_call(
        join_kernel,
        in_specs=[full] * 4,
        out_specs=[full] * 2,
        out_shape=[jax.ShapeDtypeStruct((size, 32, 128), BF16) for size in (19, 20)],
        compiler_params=pltpu.CompilerParams(vmem_limit_bytes=VMEM_LIMIT),
        name="join",
    )(*args)


def last_kernel(part, own, right, left, up, down, base, out, patches, fields, lines):
    for patch in range(16):
        mass = (
            (own[patch].astype(F32) + left[17 + patch].astype(F32))
            + (right[17 + patch].astype(F32) + up[patch].astype(F32))
        ) + down[patch].astype(F32)
        patches[32 * patch : 32 * patch + 32, :] = mass
    for group in range(2):
        for half in range(2):
            for x in range(16):
                block = patches[pl.ds(256 * group + 16 * half + x, 8, stride=32), :]
                at = 128 * (2 * x + half)
                out[8 * group : 8 * group + 8, at : at + 128] = block
    base[...] = part[...]
    both = down[19].astype(F32)
    face = both[0:16] + both[16:32]
    for x in range(16):
        base[32 * x : 32 * x + 1, :] += face[x : x + 1, :]
    virtual_deposit(
        [(source, slot) for source in (up, down) for slot in (16, 17, 18)], base, lines, fields
    )


def last_part(*args):
    full = pl.BlockSpec(memory_space=pltpu.VMEM)
    return pl.pallas_call(
        last_kernel,
        in_specs=[full] * 6,
        out_specs=[full] * 2,
        out_shape=[
            jax.ShapeDtypeStruct((512, 128), F32),
            jax.ShapeDtypeStruct((16, 4096), F32),
        ],
        scratch_shapes=[
            pltpu.VMEM((512, 128), F32),
            pltpu.VMEM((2, 32, 512), F32),
            pltpu.VMEM((2, 32, 128), F32),
        ],
        compiler_params=pltpu.CompilerParams(vmem_limit_bytes=VMEM_LIMIT),
        name="last",
    )(*args)


def on_device(
    part_data,
    tile_cells,
    tile_counts,
    ghost_data,
    halo_refined_cells,
    ghost_counts,
    virt_data,
    virt_cells,
    phantom_slot_counts,
):
    core, face_x, face_y = tile_part(tile_counts, part_data, tile_cells)
    ghosts = (ghost_counts, phantom_slot_counts, ghost_data, halo_refined_cells)
    ghosts += (virt_data, virt_cells, face_x)
    toward, away = fine_part((0, 1, 2, 6, 7, 8), (51, 54), *ghosts, core)
    right = shift(toward, "gx", -1)
    left = shift(away, "gx", 1)
    (sides,) = fine_part((3, 5), (34,), *ghosts, away)
    up, down = join_part(sides, right, left, face_y)
    from_up = shift(up, "gy", -1)
    from_down = shift(down, "gy", 1)
    (own,) = fine_part((4,), (17,), *ghosts, down)
    part = base_part(own, right, left, core)
    base, fine_mass = last_part(part, own, right, left, from_up, from_down)
    return base.reshape(16, 32, 128), fine_mass


def solution(mesh):
    return jax.shard_map(
        on_device,
        mesh=mesh,
        in_specs=(
            P("gx", "gy", None, None, None),
            P("gx", "gy", None, None),
            P("gx", "gy", None),
            P(("gx", "gy"), None, None, None, None),
            P(("gx", "gy"), None, None, None),
            P(("gx", "gy"), None, None),
            P(("gx", "gy"), None, None, None),
            P(("gx", "gy"), None, None),
            P(("gx", "gy"), None),
        ),
        out_specs=(P("gx", "gy", None), P(("gx", "gy"), None)),
        check_vma=False,
    )
```

time: 74.4 us -> 61.7 us (0.83)
  waiting for transfers between devices: 6.98 us -> 0.01 us
  starting transfers between devices: 16.3 us -> 12 us
  other arithmetic: 2.09 us -> 0 us
    ppermute x10 -> x4, waiting for transfers between devices: 6.98 us -> 0.01 us  [shift(): lax.ppermute(x, axis, [(i, (i + by) % devices) for i in range(devices)])]
    ppermute x10 -> x4, starting transfers between devices: 16.3 us -> 12 us  [shift(): lax.ppermute(x, axis, [(i, (i + by) % devices) for i in range(devices)])]
    unnamed x25 -> x10, local copies, waits for them, and re-layouts: 2.52 us -> 4.81 us
    convert_element_type x1 -> x0, other arithmetic: 1.36 us -> none  [joint(): return (fine_0[part].astype(F32) + fine_r[part].astype(F32) + fine_l[part...]
    reshape x2 -> x0, local copies, waits for them, and re-layouts: 1.26 us -> none  [the longest x1 0.66 us: on_device(): counts = ghost_counts.reshape(144)]
    pallas_call x6 -> x7, Pallas kernels: 43.7 us -> 43.7 us  [the longest x3 30.8 us: fine_part(): pl.pallas_call(functools.partial(fine_kernel, offsets, len(sizes)), in_sp...]
  transfers between devices with their start and end apart: 10 -> 4, of which waited for: 1 -> 0; matrix products, arithmetic and copies ran while one was open for 4% -> 0% of each run, Pallas kernels for 42% -> 26%
where the time goes in v1:
time: 61.7 us; the launch traced here: 61.2 us
  Pallas kernels  43.7 us (71%)
  starting transfers between devices  12 us (19%)
  local copies, waits for them, and re-layouts  4.81 us (8%)
  between operations  0.7 us (1%)
    pallas_call x3, Pallas kernels, fine_part(): pl.pallas_call(functools.partial(fine_kernel, offsets, len(sizes)), in_sp...  30.8 us
    ppermute x4, starting transfers between devices, shift(): lax.ppermute(x, axis, [(i, (i + by) % devices) for i in range(devices)])  12 us
    pallas_call x1, Pallas kernels, tile_part(): pl.pallas_call(tile_kernel, in_specs=[smem, full, full], out_specs=[full]...  5.05 us
    unnamed x10, local copies, waits for them, and re-layouts  4.81 us
    pallas_call x1, Pallas kernels, last_part(): pl.pallas_call(last_kernel, in_specs=[full] * 6, out_specs=[full] * 2, ou...  3.32 us
    pallas_call x1, Pallas kernels, base_part(): pl.pallas_call(base_kernel, in_specs=[full] * 4, out_specs=full, out_shap...  2.62 us
    pallas_call x1, Pallas kernels, join_part(): pl.pallas_call(join_kernel, in_specs=[full] * 4, out_specs=[full] * 2, ou...  1.99 us
  transfers between devices with their start and end apart: 4, of which 0 were waited for; matrix products, arithmetic and copies ran while one was open for 0% of the time, Pallas kernels for 26%

profile of v1, /device:TPU:0, one launch (start us, length us, event | category | flops | bytes accessed | tf_op | source)
XLA Modules:
  0.0 61.2 jit_solution(6873540560758307198)
XLA Ops:
  0.6 1.3 %copy.15.counts = s32[1,9,16]{2,1,0:T(8,128)} copy(s32[1,9,16]{2,0,1:T(1,128)} %param.14) | data formatting | bytes 1152 | tf_op args[5]
  1.9 1.3 %copy.16.vcells = s32[1,9,512]{2,1,0:T(8,128)} copy(s32[1,9,512]{2,0,1:T(1,128)} %param.16) | data formatting | bytes 36864 | tf_op args[7]
  3.2 5.1 %tiles.1 = (f32[16,32,128]{2,1,0:T(8,128)}, f32[40,128]{1,0:T(8,128)}, f32[16,128]{1,0:T(8,128)}) custom-call(s32[2,4,16]{2,1,0:T(4,128)} %counts.4, bf16[2,4,16,4,128]{4,3,2,1,0:T(4,128)(2,1)} %data.1, s32[2,4,16,128]{3,2,1,0:T(8,128)} %cells.1), custom_call_target="tpu_custom_call" | custom-call | tf_op jit(solution)/shard_map/tiles/pallas_call | solution.py:284
  8.3 17.2 %fine.3 = (bf16[51,32,128]{2,1,0:T(8,128)(2,1)}, bf16[54,32,128]{2,1,0:T(8,128)(2,1)}) custom-call(s32[1,9,16]{2,1,0:T(8,128)} %copy.15.counts, s32[1,9]{1,0:T(1,128)} %vcounts.5, bf16[1,9,16,4,2048]{4,3,2,1,0:T(4,128)(2,1)} %data_hbm.5, s32[1,9,16,2048]{3,2,1,0:T(8,128)} %cells_hbm.5, bf16[1,9,4,512]{3,2,1,0:T(4,128)(2,1)} %vdata.5, ...), custom_call_target="tpu_custom_call" | custom-call | flops 6442450944 | bytes 3840000 | tf_op jit(solution)/shard_map/fine/pallas_call | solution.py:191
  25.5 0.1 collective-permute-start.1
  25.5 3.7 %collective-permute-start = (bf16[51,32,128]{2,1,0:T(8,128)(2,1)}, bf16[51,32,128]{2,1,0:T(8,128)(2,1)S(1)}, u32[]{:S(2)}, u32[]{:S(2)}) collective-permute-start(bf16[51,32,128]{2,1,0:T(8,128)(2,1)} %get-tuple-element.14), channel_id=1, source_target_pairs={{0,112},{16,0},{32,16},{48,32},{64,48},{80,64},{96,80},{112,96},{1... | collective-permute-start | bytes 1253384 | tf_op jit(solution)/shard_map/ppermute | solution.py:22
  29.3 7.7 %fine.4.own = bf16[34,32,128]{2,1,0:T(8,128)(2,1)} custom-call(s32[1,9,16]{2,1,0:T(8,128)} %copy.15.counts, s32[1,9]{1,0:T(1,128)} %vcounts.5, bf16[1,9,16,4,2048]{4,3,2,1,0:T(4,128)(2,1)} %data_hbm.5, s32[1,9,16,2048]{3,2,1,0:T(8,128)} %cells_hbm.5, bf16[1,9,4,512]{3,2,1,0:T(4,128)(2,1)} %vdata.5, s32[1,9,512]{2,1,0:T(8,128)} %copy.16.vcells, ...), custom_call_target="tpu_custom_call" | custom-call | flops 2147483648 | bytes 1280000 | tf_op jit(solution)/shard_map/fine/pallas_call | solution.py:191
  37.0 0.0 collective-permute-done.right
  37.0 0.0 copy-start.1
  37.0 0.0 collective-permute-done.1.left
  37.0 0.0 copy-start
  37.0 0.7 %copy-done.1 = bf16[51,32,128]{2,1,0:T(8,128)(2,1)} copy-done((bf16[51,32,128]{2,1,0:T(8,128)(2,1)}, bf16[51,32,128]{2,1,0:T(8,128)(2,1)S(1)}, u32[]{:S(2)}) %copy-start.1) | copy-done | bytes 417816
  37.8 0.1 copy-done
  37.9 2.0 %join.1 = (bf16[19,32,128]{2,1,0:T(8,128)(2,1)}, bf16[20,32,128]{2,1,0:T(8,128)(2,1)}) custom-call(bf16[34,32,128]{2,1,0:T(8,128)(2,1)} %fine.4.own, bf16[51,32,128]{2,1,0:T(8,128)(2,1)} %copy-done.1, bf16[54,32,128]{2,1,0:T(8,128)(2,1)} %copy-done, f32[16,128]{1,0:T(8,128)} %get-tuple-element.15.face_y), custom_call_target="tpu_custom_call" | custom-call | tf_op jit(solution)/shard_map/join/pallas_call | solution.py:403
  39.9 2.6 %collective-permute-start.3 = (bf16[20,32,128]{2,1,0:T(8,128)(2,1)}, bf16[20,32,128]{2,1,0:T(8,128)(2,1)S(1)}, u32[]{:S(2)}, u32[]{:S(2)}) collective-permute-start(bf16[20,32,128]{2,1,0:T(8,128)(2,1)} %get-tuple-element.16.wait), channel_id=1, source_target_pairs={{0,1},{1,2},{2,3},{3,4},{4,5},{5,6},{6,7},{7,8},{8,9},{9,10},{10,1... | collective-permute-start | bytes 491528 | tf_op jit(solution)/shard_map/ppermute | solution.py:22
  42.5 5.5 %collective-permute-start.2 = (bf16[19,32,128]{2,1,0:T(8,128)(2,1)}, bf16[19,32,128]{2,1,0:T(8,128)(2,1)S(1)}, u32[]{:S(2)}, u32[]{:S(2)}) collective-permute-start(bf16[19,32,128]{2,1,0:T(8,128)(2,1)} %get-tuple-element.17), channel_id=1, source_target_pairs={{0,15},{1,0},{2,1},{3,2},{4,3},{5,4},{6,5},{7,6},{8,7},{9,8},{10,9... | collective-permute-start | bytes 466952 | tf_op jit(solution)/shard_map/ppermute | solution.py:22
  48.1 5.9 %fine.5.own = bf16[17,32,128]{2,1,0:T(8,128)(2,1)} custom-call(s32[1,9,16]{2,1,0:T(8,128)} %copy.15.counts, s32[1,9]{1,0:T(1,128)} %vcounts.5, bf16[1,9,16,4,2048]{4,3,2,1,0:T(4,128)(2,1)} %data_hbm.5, s32[1,9,16,2048]{3,2,1,0:T(8,128)} %cells_hbm.5, bf16[1,9,4,512]{3,2,1,0:T(4,128)(2,1)} %vdata.5, s32[1,9,512]{2,1,0:T(8,128)} %copy.16.vcells, ...), custom_call_target="tpu_custom_call" | custom-call | flops 1073741824 | bytes 640000 | tf_op jit(solution)/shard_map/fine/pallas_call | solution.py:191
  54.0 2.6 %base.1.part = f32[512,128]{1,0:T(8,128)} custom-call(bf16[17,32,128]{2,1,0:T(8,128)(2,1)} %fine.5.own, bf16[51,32,128]{2,1,0:T(8,128)(2,1)} %copy-done.1, bf16[54,32,128]{2,1,0:T(8,128)(2,1)} %copy-done, f32[16,32,128]{2,1,0:T(8,128)} %get-tuple-element.12.wait.core), custom_call_target="tpu_custom_call" | custom-call | flops 603979776 | bytes 1000000 | tf_op jit(solution)/shard_map/base/pallas_call | solution.py:369
  56.6 0.0 collective-permute-done.2.up
  56.6 0.0 copy-start.3
  56.6 0.0 collective-permute-done.3.down
  56.6 0.6 %copy-done.3 = bf16[19,32,128]{2,1,0:T(8,128)(2,1)} copy-done((bf16[19,32,128]{2,1,0:T(8,128)(2,1)}, bf16[19,32,128]{2,1,0:T(8,128)(2,1)S(1)}, u32[]{:S(2)}) %copy-start.3) | copy-done | bytes 155672
  57.2 0.0 copy-start.2
  57.2 0.7 %copy-done.2 = bf16[20,32,128]{2,1,0:T(8,128)(2,1)} copy-done((bf16[20,32,128]{2,1,0:T(8,128)(2,1)}, bf16[20,32,128]{2,1,0:T(8,128)(2,1)S(1)}, u32[]{:S(2)}) %copy-start.2) | copy-done | bytes 163864
  57.9 3.3 %last.1 = (f32[512,128]{1,0:T(8,128)}, f32[16,4096]{1,0:T(8,128)}) custom-call(f32[512,128]{1,0:T(8,128)} %base.1.part, bf16[17,32,128]{2,1,0:T(8,128)(2,1)} %fine.5.own, bf16[51,32,128]{2,1,0:T(8,128)(2,1)} %copy-done.1, bf16[54,32,128]{2,1,0:T(8,128)(2,1)} %copy-done, bf16[19,32,128]{2,1,0:T(8,128)(2,1)} %copy-done.3, bf16[20,32,128]{2,1,0:T(8,128)(2,1)} %copy-done.2), custom_call_target="tpu_custom_call" | custom-call | tf_op jit(solution)/shard_map/last/pallas_call | solution.py:438
Async XLA Ops:
  25.5 11.6 %collective-permute-start.1 = (bf16[54,32,128]{2,1,0:T(8,128)(2,1)}, bf16[54,32,128]{2,1,0:T(8,128)(2,1)S(1)}, u32[]{:S(2)}, u32[]{:S(2)}) collective-permute-start(bf16[54,32,128]{2,1,0:T(8,128)(2,1)} %get-tuple-element.13.wait), channel_id=1, source_target_pairs={{0,16},{16,32},{32,48},{48,64},{64,80},{80,96},{96,112},{112,0},{1... | collective-permute-start | bytes 1327112 | tf_op jit(solution)/shard_map/ppermute | solution.py:22
  25.5 11.5 %collective-permute-start = (bf16[51,32,128]{2,1,0:T(8,128)(2,1)}, bf16[51,32,128]{2,1,0:T(8,128)(2,1)S(1)}, u32[]{:S(2)}, u32[]{:S(2)}) collective-permute-start(bf16[51,32,128]{2,1,0:T(8,128)(2,1)} %get-tuple-element.14), channel_id=1, source_target_pairs={{0,112},{16,0},{32,16},{48,32},{64,48},{80,64},{96,80},{112,96},{1... | collective-permute-start | bytes 1253384 | tf_op jit(solution)/shard_map/ppermute | solution.py:22
  37.0 0.8 %copy-start.1 = (bf16[51,32,128]{2,1,0:T(8,128)(2,1)}, bf16[51,32,128]{2,1,0:T(8,128)(2,1)S(1)}, u32[]{:S(2)}) copy-start(bf16[51,32,128]{2,1,0:T(8,128)(2,1)S(1)} %collective-permute-done.right) | copy-start | bytes 1253380
  37.0 0.9 %copy-start = (bf16[54,32,128]{2,1,0:T(8,128)(2,1)}, bf16[54,32,128]{2,1,0:T(8,128)(2,1)S(1)}, u32[]{:S(2)}) copy-start(bf16[54,32,128]{2,1,0:T(8,128)(2,1)S(1)} %collective-permute-done.1.left) | copy-start | bytes 1327108
  39.9 16.7 %collective-permute-start.3 = (bf16[20,32,128]{2,1,0:T(8,128)(2,1)}, bf16[20,32,128]{2,1,0:T(8,128)(2,1)S(1)}, u32[]{:S(2)}, u32[]{:S(2)}) collective-permute-start(bf16[20,32,128]{2,1,0:T(8,128)(2,1)} %get-tuple-element.16.wait), channel_id=1, source_target_pairs={{0,1},{1,2},{2,3},{3,4},{4,5},{5,6},{6,7},{7,8},{8,9},{9,10},{10,1... | collective-permute-start | bytes 491528 | tf_op jit(solution)/shard_map/ppermute | solution.py:22
  42.5 14.0 %collective-permute-start.2 = (bf16[19,32,128]{2,1,0:T(8,128)(2,1)}, bf16[19,32,128]{2,1,0:T(8,128)(2,1)S(1)}, u32[]{:S(2)}, u32[]{:S(2)}) collective-permute-start(bf16[19,32,128]{2,1,0:T(8,128)(2,1)} %get-tuple-element.17), channel_id=1, source_target_pairs={{0,15},{1,0},{2,1},{3,2},{4,3},{5,4},{6,5},{7,6},{8,7},{9,8},{10,9... | collective-permute-start | bytes 466952 | tf_op jit(solution)/shard_map/ppermute | solution.py:22
  56.6 0.7 %copy-start.3 = (bf16[19,32,128]{2,1,0:T(8,128)(2,1)}, bf16[19,32,128]{2,1,0:T(8,128)(2,1)S(1)}, u32[]{:S(2)}) copy-start(bf16[19,32,128]{2,1,0:T(8,128)(2,1)S(1)} %collective-permute-done.2.up) | copy-start | bytes 466948
  57.2 0.7 %copy-start.2 = (bf16[20,32,128]{2,1,0:T(8,128)(2,1)}, bf16[20,32,128]{2,1,0:T(8,128)(2,1)S(1)}, u32[]{:S(2)}) copy-start(bf16[20,32,128]{2,1,0:T(8,128)(2,1)S(1)} %collective-permute-done.3.down) | copy-start | bytes 491524

commit v2 on v1

--- a/solution.py
+++ b/solution.py
@@ -12,9 +12,10 @@
 I32 = jnp.int32
 NT = (((1,), (1,)), ((), ()))
 LANES = 256
-UNROLL = 16
+UNROLL = 32
 PATCHES = 48
 VMEM_LIMIT = 56 * 2**20
+SMALL_LIMIT = 16 * 2**20
 
 
 def shift(x, axis, by):
@@ -46,7 +47,7 @@
 def pack_virtual(offset, counts, data, cells, lines):
     lane = lax.broadcasted_iota(I32, (1, 512), 1)
     high = data[0, offset].astype(F32)
-    cell = cells[0, offset : offset + 1, :]
+    cell = cells[offset]
     values = [
         jnp.where(lane < counts[0, offset], high[0:1], 0.0),
         high[1:2],
@@ -65,13 +66,13 @@
 
 def fine_kernel(offsets, split, counts, vcounts, data_hbm, cells_hbm, vdata, vcells, face, wait, *rest):
     outs, rest = rest[:split], rest[split:]
-    data, cells, total, fields, partial, lines, number, sems = rest
+    data, cells, total, fields, places, lines, number, sems = rest
     patches = 16 * len(offsets)
     copies = []
     for at, offset in enumerate(offsets):
         copies.append(
             pltpu.make_async_copy(
-                data_hbm.at[0, offset], data.at[pl.ds(16 * at, 16)], sems.at[2 * at]
+                data_hbm.at[offset], data.at[pl.ds(16 * at, 16)], sems.at[2 * at]
             )
         )
         copies.append(
@@ -82,11 +83,10 @@
     for copy in copies:
         copy.start()
     total[...] = jnp.zeros_like(total)
-    partial[...] = jnp.zeros_like(partial)
     work = jnp.int32(0)
     for at, offset in enumerate(offsets):
         for patch in range(16):
-            live = counts[0, offset, patch]
+            live = counts[offset, 0, patch]
             number[16 * at + patch] = live
             work = work + jnp.maximum((live + (LANES - 1)) >> 8, 1)
     for extra in range(UNROLL + 4):
@@ -102,45 +102,69 @@
         outs[1][52] = low[0:32]
         high, low = high_low(jnp.concatenate([face[32:40, :], jnp.zeros((8, 128), F32)], 0))
         outs[1][53] = jnp.concatenate([high, low], 0)
-    lane = lax.broadcasted_iota(I32, (1, LANES), 1)
-    here = sublane(16, LANES).astype(BF16)
-    before = (sublane(16, LANES) - 1.0).astype(BF16)
-    rows = sublane(8, LANES)
-    zero = jnp.zeros((16, LANES), BF16)
+    lane = lax.broadcasted_iota(I32, (8, 128), 1)
+    here = sublane(16, 128).astype(BF16)
+    before = (sublane(16, 128) - 1.0).astype(BF16)
+    rows = sublane(8, 128)
+    zero = jnp.zeros((16, 128), BF16)
     for copy in copies:
         copy.wait()
 
     def deposit(unit, group, start, live, next_one, next_two):
         patch = jnp.minimum(group, patches - 1)
         at = pl.multiple_of(start, LANES)
-        high = data[patch, :, pl.ds(at, LANES)].astype(F32)
+        high = data[patch, start >> 8].astype(F32)
         cell = cells[pl.ds(patch, 1), pl.ds(at, LANES)]
-        low = 1.0 - high
-        mass = jnp.where(lane < live, high[0:1], 0.0)
         f = fields.at[unit]
-        f[0:4, :] = high
-        f[4:8, :] = low
-        f[8:9, :] = high[3:4] * mass
-        f[9:10, :] = low[3:4] * mass
-        f[10:11, :] = (cell >> 8).astype(F32)
-        f[11:12, :] = (cell & 15).astype(F32)
-        f[12:13, :] = ((cell >> 4) & 3).astype(F32)
-        f[13:14, :] = ((cell >> 6) & 3).astype(F32)
-        inner = row8(f, 12)
-        f[16:24, :] = jnp.where(
-            rows == inner, row8(f, 6), jnp.where(rows - 1.0 == inner, row8(f, 2), 0.0)
+        g = places.at[unit]
+        f[0:8, :] = high
+        f[8:16, :] = 1.0 - high
+        g[0:1, :] = (cell >> 8).astype(F32)
+        g[1:2, :] = (cell & 15).astype(F32)
+        g[2:3, :] = ((cell >> 4) & 3).astype(F32)
+        g[3:4, :] = ((cell >> 6) & 3).astype(F32)
+        left, right = [], []
+        for half in range(2):
+            wide = slice(128 * half, 128 * half + 128)
+
+            def up(field, half=half):
+                return row8(f, 4 * half + field)
+
+            def down(field, half=half):
+                return row8(f, 8 + 4 * half + field)
+
+            def double(x):
+                return jnp.concatenate([x, x], 0).astype(BF16)
+
+            def where_at(field, wide=wide):
+                return g[pl.ds(field, 8, stride=0), :][:, wide]
+
+            mass = jnp.where(lane < live - 128 * half, up(0), 0.0)
+            c0, c1 = double(down(3) * mass), double(up(3) * mass)
+            x0, x1 = double(down(1)), double(up(1))
+            inner = where_at(2)
+            f[16 + 8 * half : 24 + 8 * half, :] = jnp.where(
+                rows == inner, down(2), jnp.where(rows - 1.0 == inner, up(2), 0.0)
+            )
+            x, z, outer = double(where_at(0)), double(where_at(1)), double(where_at(3))
+            along_x = jnp.where(here == x, x0, jnp.where(before == x, x1, zero))
+            along_z = jnp.where(here == z, c0, jnp.where(before == z, c1, zero))
+            left.append(
+                jnp.concatenate(
+                    [jnp.where(outer == BF16(k), along_x, zero) for k in range(4)], 0
+                )
+            )
+            right.append(
+                jnp.concatenate(
+                    [row16(f, 16 + 8 * half + k) * along_z for k in range(5)], 0
+                )
+            )
+        total[patch, :, 0:80] += dot_nt(
+            jnp.concatenate(left, 1), jnp.concatenate(right, 1)
         )
-        x, outer, z = row16(f, 10), row16(f, 13), row16(f, 11)
-        along_x = jnp.where(here == x, row16(f, 5), jnp.where(before == x, row16(f, 1), zero))
-        along_z = jnp.where(here == z, row16(f, 9), jnp.where(before == z, row16(f, 8), zero))
-        left = jnp.concatenate(
-            [jnp.where(outer == BF16(k), along_x, zero) for k in range(4)], 0
-        )
-        right = jnp.concatenate([row16(f, 16 + k) * along_z for k in range(5)], 0)
-        partial[unit, :, 0:80] = dot_nt(left, right)
         last = live <= LANES
         group = jnp.where(last, group + 1, group)
-        return patch, (
+        return (
             group,
             jnp.where(last, 0, start + LANES),
             jnp.where(last, next_one, live - LANES),
@@ -148,21 +172,13 @@
             number[group + 2],
         )
 
-    def body(_, carry):
-        state, old = carry[:5], carry[5:]
-        new = []
+    def body(_, state):
         for unit in range(UNROLL):
-            total[old[unit]] += partial[unit]
-            patch, state = deposit(unit, *state)
-            new.append(patch)
-        return (*state, *new)
+            state = deposit(unit, *state)
+        return state
 
     none = jnp.int32(0)
-    carry = lax.fori_loop(
-        0, steps, body, (none, none, number[0], number[1], number[2]) + (none,) * UNROLL
-    )
-    for unit in range(UNROLL):
-        total[carry[5 + unit]] += partial[unit]
+    lax.fori_loop(0, steps, body, (none, none, number[0], number[1], number[2]))
     lane = lax.broadcasted_iota(I32, (16, 128), 1)
 
     for index in range(split):
@@ -183,7 +199,7 @@
 
 
 def fine_part(offsets, sizes, counts, vcounts, data, cells, vdata, vcells, face, wait):
-    slots = data.shape[4]
+    slots = cells.shape[3]
     patches = 16 * len(offsets)
     full = pl.BlockSpec(memory_space=pltpu.VMEM)
     smem = pl.BlockSpec(memory_space=pltpu.SMEM)
@@ -193,11 +209,11 @@
         in_specs=[smem, smem, anywhere, anywhere, full, full, full, anywhere],
         out_specs=[full] * len(sizes),
         scratch_shapes=[
-            pltpu.VMEM((patches, 4, slots), BF16),
+            pltpu.VMEM((patches, slots // LANES, 8, 128), BF16),
             pltpu.VMEM((patches, slots), I32),
             pltpu.VMEM((patches, 64, 128), F32),
-            pltpu.VMEM((UNROLL, 24, LANES), F32),
-            pltpu.VMEM((UNROLL, 64, 128), F32),
+            pltpu.VMEM((UNROLL, 32, 128), F32),
+            pltpu.VMEM((UNROLL, 8, LANES), F32),
             pltpu.VMEM((32, 128), F32),
             pltpu.SMEM((patches + UNROLL + 4,), I32),
             pltpu.SemaphoreType.DMA((2 * len(offsets),)),
@@ -372,7 +388,7 @@
         out_specs=full,
         out_shape=jax.ShapeDtypeStruct((512, 128), F32),
         scratch_shapes=[pltpu.VMEM((2, 32, 128), F32), pltpu.VMEM((2, 32, 512), F32)],
-        compiler_params=pltpu.CompilerParams(vmem_limit_bytes=VMEM_LIMIT),
+        compiler_params=pltpu.CompilerParams(vmem_limit_bytes=SMALL_LIMIT),
         cost_estimate=pl.CostEstimate(
             flops=6 * 3 * 512 * 512 * 128, bytes_accessed=1000000, transcendentals=0
         ),
@@ -405,7 +421,7 @@
         in_specs=[full] * 4,
         out_specs=[full] * 2,
         out_shape=[jax.ShapeDtypeStruct((size, 32, 128), BF16) for size in (19, 20)],
-        compiler_params=pltpu.CompilerParams(vmem_limit_bytes=VMEM_LIMIT),
+        compiler_params=pltpu.CompilerParams(vmem_limit_bytes=SMALL_LIMIT),
         name="join",
     )(*args)
 
@@ -448,7 +464,7 @@
             pltpu.VMEM((2, 32, 512), F32),
             pltpu.VMEM((2, 32, 128), F32),
         ],
-        compiler_params=pltpu.CompilerParams(vmem_limit_bytes=VMEM_LIMIT),
+        compiler_params=pltpu.CompilerParams(vmem_limit_bytes=SMALL_LIMIT),
         name="last",
     )(*args)
 
@@ -465,8 +481,13 @@
     phantom_slot_counts,
 ):
     core, face_x, face_y = tile_part(tile_counts, part_data, tile_cells)
-    ghosts = (ghost_counts, phantom_slot_counts, ghost_data, halo_refined_cells)
-    ghosts += (virt_data, virt_cells, face_x)
+    sources, own_patches, fields, slots = ghost_data.shape[1:]
+    tiled = ghost_data.reshape(sources, own_patches, fields, slots // LANES, 2, 128)
+    tiled = tiled.transpose(0, 1, 3, 4, 2, 5)
+    tiled = tiled.reshape(sources, own_patches, slots // LANES, 8, 128)
+    counts = jnp.swapaxes(ghost_counts, 0, 1)
+    ghosts = (counts, phantom_slot_counts, tiled, halo_refined_cells)
+    ghosts += (virt_data, jnp.swapaxes(virt_cells, 0, 1), face_x)
     toward, away = fine_part((0, 1, 2, 6, 7, 8), (51, 54), *ghosts, core)
     right = shift(toward, "gx", -1)
     left = shift(away, "gx", 1)

time: 61.7 us -> 47.3 us (0.77)
  the two profiles are of different devices: /device:TPU:0 before, /device:TPU:1 now
where the time goes in v2:
time: 47.3 us; the launch traced here: 46.4 us
  Pallas kernels  34.9 us (74%)
  starting transfers between devices  8.22 us (17%)
  local copies, waits for them, and re-layouts  1.87 us (4%)
  waiting for transfers between devices  0.76 us (2%)
  between operations  0.71 us (2%)
    pallas_call x3, Pallas kernels, fine_part(): pl.pallas_call(functools.partial(fine_kernel, offsets, len(sizes)), in_sp...  27.1 us
    ppermute x4, starting transfers between devices, shift(): lax.ppermute(x, axis, [(i, (i + by) % devices) for i in range(devices)])  8.22 us
    pallas_call x1, Pallas kernels, tile_part(): pl.pallas_call(tile_kernel, in_specs=[smem, full, full], out_specs=[full]...  5.06 us
    pallas_call x1, Pallas kernels, last_part(): pl.pallas_call(last_kernel, in_specs=[full] * 6, out_specs=[full] * 2, ou...  1.97 us
    unnamed x10, local copies, waits for them, and re-layouts  1.87 us
  transfers between devices with their start and end apart: 4, of which 1 were waited for; matrix products, arithmetic and copies ran while one was open for 0% of the time, Pallas kernels for 25%

profile of v2, /device:TPU:1, one launch (start us, length us, event | category | flops | bytes accessed | tf_op | source)
XLA Modules:
  0.0 46.4 jit_solution(922496477530688099)
XLA Ops:
  0.6 5.1 %tiles.1 = (f32[16,32,128]{2,1,0:T(8,128)}, f32[40,128]{1,0:T(8,128)}, f32[16,128]{1,0:T(8,128)}) custom-call(s32[2,4,16]{2,1,0:T(4,128)} %counts.1, bf16[2,4,16,4,128]{4,3,2,1,0:T(4,128)(2,1)} %data.1, s32[2,4,16,128]{3,2,1,0:T(8,128)} %cells.1), custom_call_target="tpu_custom_call" | custom-call | tf_op jit(solution)/shard_map/tiles/pallas_call | solution.py:300
  5.7 15.9 %fine.3 = (bf16[51,32,128]{2,1,0:T(8,128)(2,1)}, bf16[54,32,128]{2,1,0:T(8,128)(2,1)}) custom-call(s32[9,1,16]{2,1,0:T(1,128)} %bitcast.15, s32[1,9]{1,0:T(1,128)} %vcounts.5, bf16[9,16,8,8,128]{4,3,2,1,0:T(8,128)(2,1)} %bitcast.8, s32[1,9,16,2048]{3,2,1,0:T(8,128)} %cells_hbm.5, bf16[1,9,4,512]{3,2,1,0:T(4,128)(2,1)} %vdata.5, s32[9,1,512]{2,1,0:T(1,128)} %bitcast.12, ...), custom_call_target="tpu_custom_call" | custom-call | flops 6442450944 | bytes 3840000 | tf_op jit(solution)/shard_map/fine/pallas_call | solution.py:207
  21.6 1.9 %collective-permute-start.1 = (bf16[54,32,128]{2,1,0:T(8,128)(2,1)}, bf16[54,32,128]{2,1,0:T(8,128)(2,1)S(1)}, u32[]{:S(2)}, u32[]{:S(2)}) collective-permute-start(bf16[54,32,128]{2,1,0:T(8,128)(2,1)} %get-tuple-element.13.wait), channel_id=1, source_target_pairs={{0,16},{16,32},{32,48},{48,64},{64,80},{80,96},{96,112},{112,0},{1... | collective-permute-start | bytes 1327112 | tf_op jit(solution)/shard_map/ppermute | solution.py:23
  23.5 0.0 copy-start.2
  23.5 0.0 collective-permute-start
  23.5 6.9 %fine.4.own = bf16[34,32,128]{2,1,0:T(8,128)(2,1)} custom-call(s32[9,1,16]{2,1,0:T(1,128)} %bitcast.16, s32[1,9]{1,0:T(1,128)} %vcounts.5, bf16[9,16,8,8,128]{4,3,2,1,0:T(8,128)(2,1)} %bitcast.9, s32[1,9,16,2048]{3,2,1,0:T(8,128)} %cells_hbm.5, bf16[1,9,4,512]{3,2,1,0:T(4,128)(2,1)} %vdata.5, s32[9,1,512]{2,1,0:T(1,128)} %bitcast.13, ...), custom_call_target="tpu_custom_call" | custom-call | flops 2147483648 | bytes 1280000 | tf_op jit(solution)/shard_map/fine/pallas_call | solution.py:207
  30.4 0.8 %collective-permute-done.right = bf16[51,32,128]{2,1,0:T(8,128)(2,1)S(1)} collective-permute-done((bf16[51,32,128]{2,1,0:T(8,128)(2,1)}, bf16[51,32,128]{2,1,0:T(8,128)(2,1)S(1)}, u32[]{:S(2)}, u32[]{:S(2)}) %collective-permute-start) | collective-permute-done | bytes 417824 | tf_op jit(solution)/shard_map/ppermute | solution.py:23
  31.2 0.0 collective-permute-done.1.left
  31.2 0.0 copy-done.2
  31.2 0.0 copy-start
  31.2 1.0 %copy-done = bf16[34,32,128]{2,1,0:T(8,128)(2,1)S(1)} copy-done((bf16[34,32,128]{2,1,0:T(8,128)(2,1)S(1)}, bf16[34,32,128]{2,1,0:T(8,128)(2,1)}, u32[]{:S(2)}) %copy-start) | copy-done | bytes 278552
  32.1 0.0 copy-start.3
  32.1 0.1 join.1
  32.3 0.0 copy-start.4
  32.3 2.0 %collective-permute-start.3 = (bf16[20,32,128]{2,1,0:T(8,128)(2,1)S(1)}, bf16[20,32,128]{2,1,0:T(8,128)(2,1)S(1)}, u32[]{:S(2)}, u32[]{:S(2)}) collective-permute-start(bf16[20,32,128]{2,1,0:T(8,128)(2,1)S(1)} %get-tuple-element.16.wait), channel_id=1, source_target_pairs={{0,1},{1,2},{2,3},{3,4},{4,5},{5,6},{6,7},{7,8},{8,9},{9,10},{10,1... | collective-permute-start | bytes 491528 | tf_op jit(solution)/shard_map/ppermute | solution.py:23
  34.3 4.4 %collective-permute-start.2 = (bf16[19,32,128]{2,1,0:T(8,128)(2,1)S(1)}, bf16[19,32,128]{2,1,0:T(8,128)(2,1)S(1)}, u32[]{:S(2)}, u32[]{:S(2)}) collective-permute-start(bf16[19,32,128]{2,1,0:T(8,128)(2,1)S(1)} %get-tuple-element.17), channel_id=1, source_target_pairs={{0,15},{1,0},{2,1},{3,2},{4,3},{5,4},{6,5},{7,6},{8,7},{9,8},{10,9... | collective-permute-start | bytes 466952 | tf_op jit(solution)/shard_map/ppermute | solution.py:23
  38.6 0.0 copy-done.4
  38.6 4.2 %fine.5.own = bf16[17,32,128]{2,1,0:T(8,128)(2,1)} custom-call(s32[9,1,16]{2,1,0:T(1,128)} %bitcast.17, s32[1,9]{1,0:T(1,128)} %vcounts.5, bf16[9,16,8,8,128]{4,3,2,1,0:T(8,128)(2,1)} %bitcast.10, s32[1,9,16,2048]{3,2,1,0:T(8,128)} %cells_hbm.5, bf16[1,9,4,512]{3,2,1,0:T(4,128)(2,1)} %vdata.5, s32[9,1,512]{2,1,0:T(1,128)} %bitcast.14, ...), custom_call_target="tpu_custom_call" | custom-call | flops 1073741824 | bytes 640000 | tf_op jit(solution)/shard_map/fine/pallas_call | solution.py:207
  42.9 0.0 copy-done.3
  42.9 0.0 copy-start.1
  42.9 0.9 %copy-done.1 = bf16[17,32,128]{2,1,0:T(8,128)(2,1)S(1)} copy-done((bf16[17,32,128]{2,1,0:T(8,128)(2,1)S(1)}, bf16[17,32,128]{2,1,0:T(8,128)(2,1)}, u32[]{:S(2)}) %copy-start.1) | copy-done | bytes 139288
  43.8 0.6 %base.1.part = f32[512,128]{1,0:T(8,128)S(1)} custom-call(bf16[17,32,128]{2,1,0:T(8,128)(2,1)S(1)} %copy-done.1, bf16[51,32,128]{2,1,0:T(8,128)(2,1)S(1)} %collective-permute-done.right, bf16[54,32,128]{2,1,0:T(8,128)(2,1)S(1)} %collective-permute-done.1.left, f32[16,32,128]{2,1,0:T(8,128)S(1)} %copy-done.3), custom_call_target="tpu_custom_call" | custom-call | flops 603979776 | bytes 1000000 | tf_op jit(solution)/shard_map/base/pallas_call | solution.py:385
  44.4 0.0 collective-permute-done.2.up
  44.4 0.0 collective-permute-done.3.down
  44.5 2.0 %last.1 = (f32[512,128]{1,0:T(8,128)}, f32[16,4096]{1,0:T(8,128)}) custom-call(f32[512,128]{1,0:T(8,128)S(1)} %base.1.part, bf16[17,32,128]{2,1,0:T(8,128)(2,1)S(1)} %copy-done.1, bf16[51,32,128]{2,1,0:T(8,128)(2,1)S(1)} %collective-permute-done.right, bf16[54,32,128]{2,1,0:T(8,128)(2,1)S(1)} %collective-permute-done.1.left, ...), custom_call_target="tpu_custom_call" | custom-call | tf_op jit(solution)/shard_map/last/pallas_call | solution.py:454
Async XLA Ops:
  21.6 9.5 %collective-permute-start.1 = (bf16[54,32,128]{2,1,0:T(8,128)(2,1)}, bf16[54,32,128]{2,1,0:T(8,128)(2,1)S(1)}, u32[]{:S(2)}, u32[]{:S(2)}) collective-permute-start(bf16[54,32,128]{2,1,0:T(8,128)(2,1)} %get-tuple-element.13.wait), channel_id=1, source_target_pairs={{0,16},{16,32},{32,48},{48,64},{64,80},{80,96},{96,112},{112,0},{1... | collective-permute-start | bytes 1327112 | tf_op jit(solution)/shard_map/ppermute | solution.py:23
  23.5 7.7 %copy-start.2 = (f32[16,128]{1,0:T(8,128)S(1)}, f32[16,128]{1,0:T(8,128)}, u32[]{:S(2)}) copy-start(f32[16,128]{1,0:T(8,128)} %get-tuple-element.15.face_y) | copy-start | bytes 24580
  23.5 7.7 %collective-permute-start = (bf16[51,32,128]{2,1,0:T(8,128)(2,1)}, bf16[51,32,128]{2,1,0:T(8,128)(2,1)S(1)}, u32[]{:S(2)}, u32[]{:S(2)}) collective-permute-start(bf16[51,32,128]{2,1,0:T(8,128)(2,1)} %get-tuple-element.14), channel_id=1, source_target_pairs={{0,112},{16,0},{32,16},{48,32},{64,48},{80,64},{96,80},{112,96},{1... | collective-permute-start | bytes 1253384 | tf_op jit(solution)/shard_map/ppermute | solution.py:23
  31.2 1.0 %copy-start = (bf16[34,32,128]{2,1,0:T(8,128)(2,1)S(1)}, bf16[34,32,128]{2,1,0:T(8,128)(2,1)}, u32[]{:S(2)}) copy-start(bf16[34,32,128]{2,1,0:T(8,128)(2,1)} %fine.4.own) | copy-start | bytes 835588
  32.1 10.7 %copy-start.3 = (f32[16,32,128]{2,1,0:T(8,128)S(1)}, f32[16,32,128]{2,1,0:T(8,128)}, u32[]{:S(2)}) copy-start(f32[16,32,128]{2,1,0:T(8,128)} %get-tuple-element.12.wait.core) | copy-start | bytes 786436
  32.3 6.4 %copy-start.4 = (bf16[20,32,128]{2,1,0:T(8,128)(2,1)}, bf16[20,32,128]{2,1,0:T(8,128)(2,1)S(1)}, u32[]{:S(2)}) copy-start(bf16[20,32,128]{2,1,0:T(8,128)(2,1)S(1)} %get-tuple-element.16.wait) | copy-start | bytes 491524
  32.3 12.2 %collective-permute-start.3 = (bf16[20,32,128]{2,1,0:T(8,128)(2,1)S(1)}, bf16[20,32,128]{2,1,0:T(8,128)(2,1)S(1)}, u32[]{:S(2)}, u32[]{:S(2)}) collective-permute-start(bf16[20,32,128]{2,1,0:T(8,128)(2,1)S(1)} %get-tuple-element.16.wait), channel_id=1, source_target_pairs={{0,1},{1,2},{2,3},{3,4},{4,5},{5,6},{6,7},{7,8},{8,9},{9,10},{10,1... | collective-permute-start | bytes 491528 | tf_op jit(solution)/shard_map/ppermute | solution.py:23
  34.3 10.2 %collective-permute-start.2 = (bf16[19,32,128]{2,1,0:T(8,128)(2,1)S(1)}, bf16[19,32,128]{2,1,0:T(8,128)(2,1)S(1)}, u32[]{:S(2)}, u32[]{:S(2)}) collective-permute-start(bf16[19,32,128]{2,1,0:T(8,128)(2,1)S(1)} %get-tuple-element.17), channel_id=1, source_target_pairs={{0,15},{1,0},{2,1},{3,2},{4,3},{5,4},{6,5},{7,6},{8,7},{9,8},{10,9... | collective-permute-start | bytes 466952 | tf_op jit(solution)/shard_map/ppermute | solution.py:23
  42.9 0.9 %copy-start.1 = (bf16[17,32,128]{2,1,0:T(8,128)(2,1)S(1)}, bf16[17,32,128]{2,1,0:T(8,128)(2,1)}, u32[]{:S(2)}) copy-start(bf16[17,32,128]{2,1,0:T(8,128)(2,1)} %fine.5.own) | copy-start | bytes 417796

commit v3 on v2

--- a/solution.py
+++ b/solution.py
@@ -12,10 +12,9 @@
 I32 = jnp.int32
 NT = (((1,), (1,)), ((), ()))
 LANES = 256
-UNROLL = 32
-PATCHES = 48
-VMEM_LIMIT = 56 * 2**20
-SMALL_LIMIT = 16 * 2**20
+OUTER = (0, 1, 2, 6, 7, 8)
+VMEM_LIMIT = 16 * 2**20
+FIRST_LIMIT = 56 * 2**20
 
 
 def shift(x, axis, by):
@@ -64,24 +63,10 @@
     return lines[...].astype(BF16)
 
 
-def fine_kernel(offsets, split, counts, vcounts, data_hbm, cells_hbm, vdata, vcells, face, wait, *rest):
-    outs, rest = rest[:split], rest[split:]
-    data, cells, total, fields, places, lines, number, sems = rest
+def deposit_ghosts(offsets, unroll, counts, get_data, get_cells, outs, total, fields, places, number, ready):
+    split = len(outs)
     patches = 16 * len(offsets)
-    copies = []
-    for at, offset in enumerate(offsets):
-        copies.append(
-            pltpu.make_async_copy(
-                data_hbm.at[offset], data.at[pl.ds(16 * at, 16)], sems.at[2 * at]
-            )
-        )
-        copies.append(
-            pltpu.make_async_copy(
-                cells_hbm.at[0, offset], cells.at[pl.ds(16 * at, 16)], sems.at[2 * at + 1]
-            )
-        )
-    for copy in copies:
-        copy.start()
+    each = len(offsets) // split
     total[...] = jnp.zeros_like(total)
     work = jnp.int32(0)
     for at, offset in enumerate(offsets):
@@ -89,32 +74,22 @@
             live = counts[offset, 0, patch]
             number[16 * at + patch] = live
             work = work + jnp.maximum((live + (LANES - 1)) >> 8, 1)
-    for extra in range(UNROLL + 4):
+    for extra in range(unroll + 4):
         number[patches + extra] = 0
-    steps = lax.div(work + (UNROLL - 1), UNROLL)
-    each = len(offsets) // split
-    for index, offset in enumerate(offsets):
-        slot = 17 * (index % each) + 16
-        outs[index // each][slot] = pack_virtual(offset, vcounts, vdata, vcells, lines)
-    if len(offsets) == 6:
-        high, low = high_low(face[...])
-        outs[1][51] = high[0:32]
-        outs[1][52] = low[0:32]
-        high, low = high_low(jnp.concatenate([face[32:40, :], jnp.zeros((8, 128), F32)], 0))
-        outs[1][53] = jnp.concatenate([high, low], 0)
+    steps = lax.div(work + (unroll - 1), unroll)
     lane = lax.broadcasted_iota(I32, (8, 128), 1)
     here = sublane(16, 128).astype(BF16)
     before = (sublane(16, 128) - 1.0).astype(BF16)
     rows = sublane(8, 128)
     zero = jnp.zeros((16, 128), BF16)
-    for copy in copies:
+    for copy in ready:
         copy.wait()
 
     def deposit(unit, group, start, live, next_one, next_two):
         patch = jnp.minimum(group, patches - 1)
         at = pl.multiple_of(start, LANES)
-        high = data[patch, start >> 8].astype(F32)
-        cell = cells[pl.ds(patch, 1), pl.ds(at, LANES)]
+        high = get_data(patch, start >> 8).astype(F32)
+        cell = get_cells(patch, at)
         f = fields.at[unit]
         g = places.at[unit]
         f[0:8, :] = high
@@ -173,7 +148,7 @@
         )
 
     def body(_, state):
-        for unit in range(UNROLL):
+        for unit in range(unroll):
             state = deposit(unit, *state)
         return state
 
@@ -192,43 +167,13 @@
                 odd = total[group, at + 16 : at + 32]
                 prior = total[group, at - 16 : at] if half else jnp.zeros((16, 128), F32)
                 swapped = pltpu.roll(jnp.where(lane < 64, odd, prior), 64, 1)
-                out[k + (k >> 4), 16 * half : 16 * half + 16] = (even + swapped).astype(BF16)
+                out[k + (k >> 4) if split > 1 else k, 16 * half : 16 * half + 16] = (even + swapped).astype(BF16)
             return 0
 
         lax.fori_loop(0, 16 * each, fold, 0, unroll=8)
 
 
-def fine_part(offsets, sizes, counts, vcounts, data, cells, vdata, vcells, face, wait):
-    slots = cells.shape[3]
-    patches = 16 * len(offsets)
-    full = pl.BlockSpec(memory_space=pltpu.VMEM)
-    smem = pl.BlockSpec(memory_space=pltpu.SMEM)
-    anywhere = pl.BlockSpec(memory_space=pl.ANY)
-    return pl.pallas_call(
-        functools.partial(fine_kernel, offsets, len(sizes)),
-        in_specs=[smem, smem, anywhere, anywhere, full, full, full, anywhere],
-        out_specs=[full] * len(sizes),
-        scratch_shapes=[
-            pltpu.VMEM((patches, slots // LANES, 8, 128), BF16),
-            pltpu.VMEM((patches, slots), I32),
-            pltpu.VMEM((patches, 64, 128), F32),
-            pltpu.VMEM((UNROLL, 32, 128), F32),
-            pltpu.VMEM((UNROLL, 8, LANES), F32),
-            pltpu.VMEM((32, 128), F32),
-            pltpu.SMEM((patches + UNROLL + 4,), I32),
-            pltpu.SemaphoreType.DMA((2 * len(offsets),)),
-        ],
-        out_shape=[jax.ShapeDtypeStruct((size, 32, 128), BF16) for size in sizes],
-        compiler_params=pltpu.CompilerParams(vmem_limit_bytes=VMEM_LIMIT),
-        cost_estimate=pl.CostEstimate(
-            flops=4 * patches * slots * 64 * 128, bytes_accessed=40000 * patches, transcendentals=0
-        ),
-        name="fine",
-    )(counts, vcounts, data, cells, vdata, vcells, face, wait)
-
-
-def tile_kernel(counts, data, cells, core, face_x, face_y, grid, fields):
-    grid[...] = jnp.zeros_like(grid)
+def deposit_tiles(counts, data, cells, core, face_y, grid, fields):
     lane = lax.broadcasted_iota(I32, (1, 128), 1)
     here = sublane(16, LANES).astype(BF16)
     before = (sublane(16, LANES) - 1.0).astype(BF16)
@@ -290,29 +235,140 @@
 
     lax.fori_loop(0, 8, column, 0)
     core[...] = grid[0:16, 0:32, :]
-    face_x[...] = grid[16]
     face_y[...] = grid[0:16, 32, :]
 
 
-def tile_part(counts, data, cells):
+def first_kernel(
+    counts, vcounts, tcounts, data_hbm, cells_hbm, vdata_hbm, vcells_hbm, tdata_hbm, tcells_hbm,
+    toward, away, packs, core, face_y,
+    data, cells, vdata, vcells, tdata, tcells, grid, tile_fields, total, fields, places, lines, number, sems,
+):
+    sources = [(tdata_hbm, tdata), (tcells_hbm, tcells), (vdata_hbm, vdata), (vcells_hbm, vcells)]
+    for at, offset in enumerate(OUTER):
+        here = pl.ds(16 * at, 16)
+        sources.append((data_hbm.at[offset], data.at[here]))
+        sources.append((cells_hbm.at[0, offset], cells.at[here]))
+    copies = [
+        pltpu.make_async_copy(source, target, sems.at[index])
+        for index, (source, target) in enumerate(sources)
+    ]
+    for copy in copies:
+        copy.start()
+    grid[...] = jnp.zeros_like(grid)
+    for copy in copies[:2]:
+        copy.wait()
+    deposit_tiles(tcounts, tdata, tcells, core, face_y, grid, tile_fields)
+    for copy in copies[2:4]:
+        copy.wait()
+    for offset in range(9):
+        out = (toward, packs, away)[offset // 3]
+        slot = offset % 3 if out is packs else 17 * (offset % 3) + 16
+        out[slot] = pack_virtual(offset, vcounts, vdata, vcells, lines)
+    high, low = high_low(grid[16, 0:32, :])
+    away[51] = high
+    away[52] = low
+    high, low = high_low(
+        jnp.concatenate([grid[16, 32:40, :], jnp.zeros((8, 128), F32)], 0)
+    )
+    away[53] = jnp.concatenate([high, low], 0)
+    deposit_ghosts(
+        OUTER,
+        32,
+        counts,
+        lambda group, chunk: data[group, chunk],
+        lambda group, at: cells[pl.ds(group, 1), pl.ds(at, LANES)],
+        (toward, away),
+        total,
+        fields,
+        places,
+        number,
+        copies[4:],
+    )
+
+
+def first_part(counts, vcounts, tcounts, data, cells, vdata, vcells, tdata, tcells):
+    slots = cells.shape[3]
+    patches = 16 * len(OUTER)
     full = pl.BlockSpec(memory_space=pltpu.VMEM)
     smem = pl.BlockSpec(memory_space=pltpu.SMEM)
+    hbm = pl.BlockSpec(memory_space=pltpu.HBM)
     return pl.pallas_call(
-        tile_kernel,
-        in_specs=[smem, full, full],
-        out_specs=[full] * 3,
+        first_kernel,
+        in_specs=[smem] * 3 + [hbm] * 6,
+        out_specs=[full] * 5,
+        scratch_shapes=[
+            pltpu.VMEM((patches, slots // LANES, 8, 128), BF16),
+            pltpu.VMEM((patches, slots), I32),
+            pltpu.VMEM(vdata.shape, BF16),
+            pltpu.VMEM(vcells.shape, I32),
+            pltpu.VMEM(tdata.shape, BF16),
+            pltpu.VMEM(tcells.shape, I32),
+            pltpu.VMEM((17, 40, 128), F32),
+            pltpu.VMEM((8, 32, LANES), F32),
+            pltpu.VMEM((patches, 64, 128), F32),
+            pltpu.VMEM((32, 32, 128), F32),
+            pltpu.VMEM((32, 8, LANES), F32),
+            pltpu.VMEM((32, 128), F32),
+            pltpu.SMEM((patches + 36,), I32),
+            pltpu.SemaphoreType.DMA((16,)),
+        ],
         out_shape=[
+            jax.ShapeDtypeStruct((51, 32, 128), BF16),
+            jax.ShapeDtypeStruct((54, 32, 128), BF16),
+            jax.ShapeDtypeStruct((3, 32, 128), BF16),
             jax.ShapeDtypeStruct((16, 32, 128), F32),
-            jax.ShapeDtypeStruct((40, 128), F32),
             jax.ShapeDtypeStruct((16, 128), F32),
         ],
+        compiler_params=pltpu.CompilerParams(vmem_limit_bytes=FIRST_LIMIT),
+        cost_estimate=pl.CostEstimate(
+            flops=4 * patches * slots * 64 * 128, bytes_accessed=4000000, transcendentals=0
+        ),
+        name="first",
+    )(counts, vcounts, tcounts, data, cells, vdata, vcells, tdata, tcells)
+
+
+def own_kernel(
+    offsets, counts, data, cells, wait, out, total, fields, places, number
+):
+    def split(group):
+        return offsets[0] + 2 * (group >> 4), group & 15
+
+    def get_data(group, chunk):
+        offset, patch = split(group)
+        return data[offset, patch, chunk]
+
+    def get_cells(group, at):
+        offset, patch = split(group)
+        return cells[0, offset, pl.ds(patch, 1), pl.ds(at, LANES)]
+
+    deposit_ghosts(
+        offsets, 24, counts, get_data, get_cells, (out,), total, fields, places, number, ()
+    )
+
+
+def own_part(offsets, counts, data, cells, wait):
+    slots = cells.shape[3]
+    patches = 16 * len(offsets)
+    full = pl.BlockSpec(memory_space=pltpu.VMEM)
+    smem = pl.BlockSpec(memory_space=pltpu.SMEM)
+    anywhere = pl.BlockSpec(memory_space=pl.ANY)
+    return pl.pallas_call(
+        functools.partial(own_kernel, offsets),
+        in_specs=[smem, full, full, anywhere],
+        out_specs=full,
         scratch_shapes=[
-            pltpu.VMEM((17, 40, 128), F32),
-            pltpu.VMEM((8, 32, LANES), F32),
+            pltpu.VMEM((patches, 64, 128), F32),
+            pltpu.VMEM((24, 32, 128), F32),
+            pltpu.VMEM((24, 8, LANES), F32),
+            pltpu.SMEM((patches + 28,), I32),
         ],
+        out_shape=jax.ShapeDtypeStruct((patches, 32, 128), BF16),
         compiler_params=pltpu.CompilerParams(vmem_limit_bytes=VMEM_LIMIT),
-        name="tiles",
-    )(counts, data, cells)
+        cost_estimate=pl.CostEstimate(
+            flops=4 * patches * slots * 64 * 128, bytes_accessed=4000000, transcendentals=0
+        ),
+        name="own",
+    )(counts, data, cells, wait)
 
 
 def virtual_deposit(packs, out, lines, fields):
@@ -374,10 +430,10 @@
         out[...] += dot_nt(jnp.concatenate(left, 0), along_z)
 
 
-def base_kernel(own, right, left, core, out, lines, fields):
+def base_kernel(packs, right, left, core, out, lines, fields):
     out[...] = core[...].reshape(512, 128)
     out[0:32, :] += left[51].astype(F32) + left[52].astype(F32)
-    virtual_deposit([(own, 16), (right, 33), (left, 33)], out, lines, fields)
+    virtual_deposit([(packs, 1), (right, 33), (left, 33)], out, lines, fields)
 
 
 def base_part(*args):
@@ -388,7 +444,7 @@
         out_specs=full,
         out_shape=jax.ShapeDtypeStruct((512, 128), F32),
         scratch_shapes=[pltpu.VMEM((2, 32, 128), F32), pltpu.VMEM((2, 32, 512), F32)],
-        compiler_params=pltpu.CompilerParams(vmem_limit_bytes=SMALL_LIMIT),
+        compiler_params=pltpu.CompilerParams(vmem_limit_bytes=VMEM_LIMIT),
         cost_estimate=pl.CostEstimate(
             flops=6 * 3 * 512 * 512 * 128, bytes_accessed=1000000, transcendentals=0
         ),
@@ -396,15 +452,15 @@
     )(*args)
 
 
-def join_kernel(own, right, left, face_y, up, down):
+def join_kernel(own, packs, right, left, face_y, up, down):
     for at, (out, slot) in enumerate(((up, 0), (down, 34))):
         for patch in range(16):
             out[patch] = (
-                own[17 * at + patch].astype(F32)
+                own[16 * at + patch].astype(F32)
                 + right[slot + patch].astype(F32)
                 + left[slot + patch].astype(F32)
             ).astype(BF16)
-        out[16] = own[17 * at + 16]
+        out[16] = packs[2 * at]
         out[17] = right[slot + 16]
         out[18] = left[slot + 16]
     corner = left[53].astype(F32)
@@ -418,10 +474,10 @@
     full = pl.BlockSpec(memory_space=pltpu.VMEM)
     return pl.pallas_call(
         join_kernel,
-        in_specs=[full] * 4,
+        in_specs=[full] * 5,
         out_specs=[full] * 2,
         out_shape=[jax.ShapeDtypeStruct((size, 32, 128), BF16) for size in (19, 20)],
-        compiler_params=pltpu.CompilerParams(vmem_limit_bytes=SMALL_LIMIT),
+        compiler_params=pltpu.CompilerParams(vmem_limit_bytes=VMEM_LIMIT),
         name="join",
     )(*args)
 
@@ -464,7 +520,7 @@
             pltpu.VMEM((2, 32, 512), F32),
             pltpu.VMEM((2, 32, 128), F32),
         ],
-        compiler_params=pltpu.CompilerParams(vmem_limit_bytes=SMALL_LIMIT),
+        compiler_params=pltpu.CompilerParams(vmem_limit_bytes=VMEM_LIMIT),
         name="last",
     )(*args)
 
@@ -480,23 +536,30 @@
     virt_cells,
     phantom_slot_counts,
 ):
-    core, face_x, face_y = tile_part(tile_counts, part_data, tile_cells)
     sources, own_patches, fields, slots = ghost_data.shape[1:]
     tiled = ghost_data.reshape(sources, own_patches, fields, slots // LANES, 2, 128)
     tiled = tiled.transpose(0, 1, 3, 4, 2, 5)
     tiled = tiled.reshape(sources, own_patches, slots // LANES, 8, 128)
     counts = jnp.swapaxes(ghost_counts, 0, 1)
-    ghosts = (counts, phantom_slot_counts, tiled, halo_refined_cells)
-    ghosts += (virt_data, jnp.swapaxes(virt_cells, 0, 1), face_x)
-    toward, away = fine_part((0, 1, 2, 6, 7, 8), (51, 54), *ghosts, core)
+    toward, away, packs, core, face_y = first_part(
+        counts,
+        phantom_slot_counts,
+        tile_counts,
+        tiled,
+        halo_refined_cells,
+        virt_data,
+        jnp.swapaxes(virt_cells, 0, 1),
+        part_data,
+        tile_cells,
+    )
     right = shift(toward, "gx", -1)
     left = shift(away, "gx", 1)
-    (sides,) = fine_part((3, 5), (34,), *ghosts, away)
-    up, down = join_part(sides, right, left, face_y)
+    sides = own_part((3, 5), counts, tiled, halo_refined_cells, away)
+    up, down = join_part(sides, packs, right, left, face_y)
     from_up = shift(up, "gy", -1)
     from_down = shift(down, "gy", 1)
-    (own,) = fine_part((4,), (17,), *ghosts, down)
-    part = base_part(own, right, left, core)
+    own = own_part((4,), counts, tiled, halo_refined_cells, down)
+    part = base_part(packs, right, left, core)
     base, fine_mass = last_part(part, own, right, left, from_up, from_down)
     return base.reshape(16, 32, 128), fine_mass
 

time: 47.3 us -> 43 us (0.909)
  Pallas kernels: 34.9 us -> 30 us
  waiting for transfers between devices: 0.76 us -> 1.98 us
  local copies, waits for them, and re-layouts: 1.87 us -> 1.03 us
    pallas_call x5 -> x4, Pallas kernels: 32.3 us -> 27.4 us  [the longest x1 19.4 us: first_part(): pl.pallas_call(first_kernel, in_specs=[smem] * 3 + [hbm] * 6, out_specs=[...]
    ppermute x4, waiting for transfers between devices: 0.76 us -> 1.98 us  [shift(): lax.ppermute(x, axis, [(i, (i + by) % devices) for i in range(devices)])]
    unnamed x10 -> x14, local copies, waits for them, and re-layouts: 1.87 us -> 1.03 us
  transfers between devices with their start and end apart: 4 -> 4, of which waited for: 1 -> 1; matrix products, arithmetic and copies ran while one was open for 0% -> 0% of each run, Pallas kernels for 25% -> 20%
where the time goes in v3:
time: 43 us; the launch traced here: 42.3 us
  Pallas kernels  30 us (70%)
  starting transfers between devices  8.51 us (20%)
  waiting for transfers between devices  1.98 us (5%)
  local copies, waits for them, and re-layouts  1.03 us (2%)
  between operations  0.74 us (2%)
    pallas_call x1, Pallas kernels, first_part(): pl.pallas_call(first_kernel, in_specs=[smem] * 3 + [hbm] * 6, out_specs=[...  19.4 us
    ppermute x4, starting transfers between devices, shift(): lax.ppermute(x, axis, [(i, (i + by) % devices) for i in range(devices)])  8.51 us
    pallas_call x2, Pallas kernels, own_part(): pl.pallas_call(functools.partial(own_kernel, offsets), in_specs=[smem, fu...  7.89 us
    ppermute x4, waiting for transfers between devices, shift(): lax.ppermute(x, axis, [(i, (i + by) % devices) for i in range(devices)])  1.98 us
    pallas_call x1, Pallas kernels, last_part(): pl.pallas_call(last_kernel, in_specs=[full] * 6, out_specs=[full] * 2, ou...  1.97 us
    unnamed x14, local copies, waits for them, and re-layouts  1.03 us
  transfers between devices with their start and end apart: 4, of which 1 were waited for; matrix products, arithmetic and copies ran while one was open for 0% of the time, Pallas kernels for 20%

profile of v3, /device:TPU:1, one launch (start us, length us, event | category | flops | bytes accessed | tf_op | source)
XLA Modules:
  0.0 42.3 jit_solution(11419940150467183839)
XLA Ops:
  0.6 0.0 copy-start.2
  0.6 0.0 copy-start.3
  0.7 0.0 copy-start.5
  0.7 19.4 %first.1 = (bf16[51,32,128]{2,1,0:T(8,128)(2,1)}, bf16[54,32,128]{2,1,0:T(8,128)(2,1)}, bf16[3,32,128]{2,1,0:T(8,128)(2,1)}, f32[16,32,128]{2,1,0:T(8,128)}, f32[16,128]{1,0:T(8,128)}) custom-call(s32[9,1,16]{2,1,0:T(1,128)} %bitcast.11, s32[1,9]{1,0:T(1,128)} %vcounts.1, s32[2,4,16]{2,1,0:T(4,128)} %tcounts.1, bf16[9,16,8,8,128]{4,3,2,1,0:T(8,128)(2,1)} %bitcast.8, ...), custom_call_target="tpu_custom_call" | custom-call | flops 6442450944 | bytes 4000000 | tf_op jit(solution)/shard_map/first/pallas_call | solution.py:295
  20.1 2.6 %collective-permute-start.1 = (bf16[54,32,128]{2,1,0:T(8,128)(2,1)}, bf16[54,32,128]{2,1,0:T(8,128)(2,1)S(1)}, u32[]{:S(2)}, u32[]{:S(2)}) collective-permute-start(bf16[54,32,128]{2,1,0:T(8,128)(2,1)} %get-tuple-element.13.wait), channel_id=1, source_target_pairs={{0,16},{16,32},{32,48},{48,64},{64,80},{80,96},{96,112},{112,0},{1... | collective-permute-start | bytes 1327112 | tf_op jit(solution)/shard_map/ppermute | solution.py:22
  22.7 0.0 copy-start
  22.7 0.0 copy-start.1
  22.7 0.0 collective-permute-start
  22.7 0.0 copy-done.2
  22.7 0.0 copy-done.3
  22.7 0.0 copy-done.5
  22.7 0.0 copy-start.4
  22.8 1.0 %copy-done.4 = bf16[54,32,128]{2,1,0:T(8,128)(2,1)S(1)} copy-done((bf16[54,32,128]{2,1,0:T(8,128)(2,1)S(1)}, bf16[54,32,128]{2,1,0:T(8,128)(2,1)}, u32[]{:S(2)}) %copy-start.4) | copy-done | bytes 442392
  23.8 0.0 copy-start.6
  23.8 4.7 %own.2 = bf16[32,32,128]{2,1,0:T(8,128)(2,1)S(1)} custom-call(s32[9,1,16]{2,1,0:T(1,128)S(1)} %bitcast.12, bf16[9,16,8,8,128]{4,3,2,1,0:T(8,128)(2,1)S(1)} %bitcast.9, s32[1,9,16,2048]{3,2,1,0:T(8,128)S(1)} %copy-done.3, bf16[54,32,128]{2,1,0:T(8,128)(2,1)S(1)} %copy-done.4), custom_call_target="tpu_custom_call" | custom-call | flops 2147483648 | bytes 4000000 | tf_op jit(solution)/shard_map/own/pallas_call | solution.py:355
  28.4 2.0 %collective-permute-done.right = bf16[51,32,128]{2,1,0:T(8,128)(2,1)S(1)} collective-permute-done((bf16[51,32,128]{2,1,0:T(8,128)(2,1)}, bf16[51,32,128]{2,1,0:T(8,128)(2,1)S(1)}, u32[]{:S(2)}, u32[]{:S(2)}) %collective-permute-start) | collective-permute-done | bytes 417824 | tf_op jit(solution)/shard_map/ppermute | solution.py:22
  30.4 0.0 collective-permute-done.1.left
  30.4 0.0 copy-done
  30.4 0.0 copy-done.1
  30.4 0.1 join.1
  30.5 0.5 %collective-permute-start.3 = (bf16[20,32,128]{2,1,0:T(8,128)(2,1)S(1)}, bf16[20,32,128]{2,1,0:T(8,128)(2,1)S(1)}, u32[]{:S(2)}, u32[]{:S(2)}) collective-permute-start(bf16[20,32,128]{2,1,0:T(8,128)(2,1)S(1)} %get-tuple-element.16.wait), channel_id=1, source_target_pairs={{0,1},{1,2},{2,3},{3,4},{4,5},{5,6},{6,7},{7,8},{8,9},{9,10},{10,1... | collective-permute-start | bytes 491528 | tf_op jit(solution)/shard_map/ppermute | solution.py:22
  31.0 5.4 %collective-permute-start.2 = (bf16[19,32,128]{2,1,0:T(8,128)(2,1)S(1)}, bf16[19,32,128]{2,1,0:T(8,128)(2,1)S(1)}, u32[]{:S(2)}, u32[]{:S(2)}) collective-permute-start(bf16[19,32,128]{2,1,0:T(8,128)(2,1)S(1)} %get-tuple-element.17), channel_id=1, source_target_pairs={{0,15},{1,0},{2,1},{3,2},{4,3},{5,4},{6,5},{7,6},{8,7},{9,8},{10,9... | collective-permute-start | bytes 466952 | tf_op jit(solution)/shard_map/ppermute | solution.py:22
  36.4 0.0 copy-done.6
  36.4 0.6 %base.1.part = f32[512,128]{1,0:T(8,128)S(1)} custom-call(bf16[3,32,128]{2,1,0:T(8,128)(2,1)S(1)} %copy-done, bf16[51,32,128]{2,1,0:T(8,128)(2,1)S(1)} %collective-permute-done.right, bf16[54,32,128]{2,1,0:T(8,128)(2,1)S(1)} %collective-permute-done.1.left, f32[16,32,128]{2,1,0:T(8,128)S(1)} %copy-done.6), custom_call_target="tpu_custom_call" | custom-call | flops 603979776 | bytes 1000000 | tf_op jit(solution)/shard_map/base/pallas_call | solution.py:441
  37.0 3.2 %own.3 = bf16[16,32,128]{2,1,0:T(8,128)(2,1)S(1)} custom-call(s32[9,1,16]{2,1,0:T(1,128)S(1)} %bitcast.13, bf16[9,16,8,8,128]{4,3,2,1,0:T(8,128)(2,1)S(1)} %bitcast.10, s32[1,9,16,2048]{3,2,1,0:T(8,128)S(1)} %copy-done.3, bf16[20,32,128]{2,1,0:T(8,128)(2,1)S(1)} %get-tuple-element.16.wait), custom_call_target="tpu_custom_call" | custom-call | flops 1073741824 | bytes 4000000 | tf_op jit(solution)/shard_map/own/pallas_call | solution.py:355
  40.3 0.0 collective-permute-done.2.up
  40.3 0.0 collective-permute-done.3.down
  40.3 2.0 %last.1 = (f32[512,128]{1,0:T(8,128)}, f32[16,4096]{1,0:T(8,128)}) custom-call(f32[512,128]{1,0:T(8,128)S(1)} %base.1.part, bf16[16,32,128]{2,1,0:T(8,128)(2,1)S(1)} %own.3, bf16[51,32,128]{2,1,0:T(8,128)(2,1)S(1)} %collective-permute-done.right, bf16[54,32,128]{2,1,0:T(8,128)(2,1)S(1)} %collective-permute-done.1.left, ...), custom_call_target="tpu_custom_call" | custom-call | tf_op jit(solution)/shard_map/last/pallas_call | solution.py:510
Async XLA Ops:
  0.6 22.1 %copy-start.2 = (bf16[1,9,16,4,2048]{4,3,2,1,0:T(4,128)(2,1)S(1)}, bf16[1,9,16,4,2048]{4,3,2,1,0:T(4,128)(2,1)}, u32[]{:S(2)}) copy-start(bf16[1,9,16,4,2048]{4,3,2,1,0:T(4,128)(2,1)} %param.12) | copy-start | bytes 7077892
  0.6 22.1 %copy-start.3 = (s32[1,9,16,2048]{3,2,1,0:T(8,128)S(1)}, s32[1,9,16,2048]{3,2,1,0:T(8,128)}, u32[]{:S(2)}) copy-start(s32[1,9,16,2048]{3,2,1,0:T(8,128)} %cells.3) | copy-start | bytes 3538948
  0.7 22.1 %copy-start.5 = (s32[1,9,16]{2,0,1:T(1,128)S(1)}, s32[1,9,16]{2,0,1:T(1,128)}, u32[]{:S(2)}) copy-start(s32[1,9,16]{2,0,1:T(1,128)} %param.14) | copy-start | bytes 1732
  20.1 10.3 %collective-permute-start.1 = (bf16[54,32,128]{2,1,0:T(8,128)(2,1)}, bf16[54,32,128]{2,1,0:T(8,128)(2,1)S(1)}, u32[]{:S(2)}, u32[]{:S(2)}) collective-permute-start(bf16[54,32,128]{2,1,0:T(8,128)(2,1)} %get-tuple-element.13.wait), channel_id=1, source_target_pairs={{0,16},{16,32},{32,48},{48,64},{64,80},{80,96},{96,112},{112,0},{1... | collective-permute-start | bytes 1327112 | tf_op jit(solution)/shard_map/ppermute | solution.py:22
  22.7 7.7 %copy-start = (bf16[3,32,128]{2,1,0:T(8,128)(2,1)S(1)}, bf16[3,32,128]{2,1,0:T(8,128)(2,1)}, u32[]{:S(2)}) copy-start(bf16[3,32,128]{2,1,0:T(8,128)(2,1)} %get-tuple-element.11.packs) | copy-start | bytes 73732
  22.7 7.7 %copy-start.1 = (f32[16,128]{1,0:T(8,128)S(1)}, f32[16,128]{1,0:T(8,128)}, u32[]{:S(2)}) copy-start(f32[16,128]{1,0:T(8,128)} %get-tuple-element.15.face_y) | copy-start | bytes 24580
  22.7 7.7 %collective-permute-start = (bf16[51,32,128]{2,1,0:T(8,128)(2,1)}, bf16[51,32,128]{2,1,0:T(8,128)(2,1)S(1)}, u32[]{:S(2)}, u32[]{:S(2)}) collective-permute-start(bf16[51,32,128]{2,1,0:T(8,128)(2,1)} %get-tuple-element.12), channel_id=1, source_target_pairs={{0,112},{16,0},{32,16},{48,32},{64,48},{80,64},{96,80},{112,96},{1... | collective-permute-start | bytes 1253384 | tf_op jit(solution)/shard_map/ppermute | solution.py:22
  22.7 1.0 %copy-start.4 = (bf16[54,32,128]{2,1,0:T(8,128)(2,1)S(1)}, bf16[54,32,128]{2,1,0:T(8,128)(2,1)}, u32[]{:S(2)}) copy-start(bf16[54,32,128]{2,1,0:T(8,128)(2,1)} %get-tuple-element.13.wait) | copy-start | bytes 1327108
  23.8 12.7 %copy-start.6 = (f32[16,32,128]{2,1,0:T(8,128)S(1)}, f32[16,32,128]{2,1,0:T(8,128)}, u32[]{:S(2)}) copy-start(f32[16,32,128]{2,1,0:T(8,128)} %get-tuple-element.14.core) | copy-start | bytes 786436
  30.5 9.8 %collective-permute-start.3 = (bf16[20,32,128]{2,1,0:T(8,128)(2,1)S(1)}, bf16[20,32,128]{2,1,0:T(8,128)(2,1)S(1)}, u32[]{:S(2)}, u32[]{:S(2)}) collective-permute-start(bf16[20,32,128]{2,1,0:T(8,128)(2,1)S(1)} %get-tuple-element.16.wait), channel_id=1, source_target_pairs={{0,1},{1,2},{2,3},{3,4},{4,5},{5,6},{6,7},{7,8},{8,9},{9,10},{10,1... | collective-permute-start | bytes 491528 | tf_op jit(solution)/shard_map/ppermute | solution.py:22
  31.0 9.3 %collective-permute-start.2 = (bf16[19,32,128]{2,1,0:T(8,128)(2,1)S(1)}, bf16[19,32,128]{2,1,0:T(8,128)(2,1)S(1)}, u32[]{:S(2)}, u32[]{:S(2)}) collective-permute-start(bf16[19,32,128]{2,1,0:T(8,128)(2,1)S(1)} %get-tuple-element.17), channel_id=1, source_target_pairs={{0,15},{1,0},{2,1},{3,2},{4,3},{5,4},{6,5},{7,6},{8,7},{9,8},{10,9... | collective-permute-start | bytes 466952 | tf_op jit(solution)/shard_map/ppermute | solution.py:22

commit v4 on v3

--- a/solution.py
+++ b/solution.py
@@ -173,75 +173,83 @@
         lax.fori_loop(0, 16 * each, fold, 0, unroll=8)
 
 
-def deposit_tiles(counts, data, cells, core, face_y, grid, fields):
-    lane = lax.broadcasted_iota(I32, (1, 128), 1)
-    here = sublane(16, LANES).astype(BF16)
-    before = (sublane(16, LANES) - 1.0).astype(BF16)
-    fifteen = (sublane(16, LANES) + 15.0).astype(BF16)
-    rows = sublane(16, LANES)
-    zero = jnp.zeros((16, LANES), BF16)
+def deposit_tiles(columns, counts, data, cells, grid, fields, places, depth):
+    lane = lax.broadcasted_iota(I32, (8, 128), 1)
+    here = sublane(16, 128).astype(BF16)
+    before = (sublane(16, 128) - 1.0).astype(BF16)
+    fifteen = (sublane(16, 128) + 15.0).astype(BF16)
+    rows = sublane(16, 128)
+    odd = lax.broadcasted_iota(I32, (2, 128), 0) * 8
+    zero = jnp.zeros((16, 128), BF16)
+
+    def double(x):
+        return jnp.concatenate([x, x], 0).astype(BF16)
 
     def column(col, _):
         tx = col >> 2
         ty = col & 3
-        acc = jnp.zeros((144, 128), F32)
+        depth[...] = jnp.zeros_like(depth)
         for pair in range(8):
-            tz = 2 * pair
             f = fields.at[pair]
-            high = jnp.concatenate(
-                [data[tx, ty, tz].astype(F32), data[tx, ty, tz + 1].astype(F32)], 1
+            g = places.at[pair]
+            high = data[tx, ty, pair].astype(F32)
+            cell = cells[tx, ty, 2 * pair : 2 * pair + 2, :]
+            f[0:8, :] = high
+            f[8:16, :] = 1.0 - high
+            g[0:2, :] = (cell >> 6).astype(F32)
+            g[2:4, :] = ((cell >> 3) & 7).astype(F32)
+            g[4:6, :] = ((cell & 7) + odd).astype(F32)
+            left, right = [], []
+            for half in range(2):
+                def up(field, half=half):
+                    return row8(f, 4 * half + field)
+
+                def down(field, half=half):
+                    return row8(f, 8 + 4 * half + field)
+
+                def wide(x):
+                    return jnp.concatenate([x, x], 0)
+
+                mass = jnp.where(lane < counts[tx, ty, 2 * pair + half], up(0), 0.0)
+                c0, c1 = double(down(3) * mass), double(up(3) * mass)
+                x = wide(row8(g, half))
+                f[16 + 16 * half : 32 + 16 * half, :] = jnp.where(
+                    rows == x, wide(down(1)), jnp.where(rows - 1.0 == x, wide(up(1)), 0.0)
+                )
+                y, z = double(row8(g, 2 + half)), double(row8(g, 4 + half))
+                along_y = jnp.where(
+                    here == y, double(down(2)), jnp.where(before == y, double(up(2)), zero)
+                )
+                left.append(
+                    jnp.concatenate(
+                        [jnp.where(here == z, c0, jnp.where(before == z, c1, zero)),
+                         jnp.where(fifteen == z, c1, zero)], 0
+                    )
+                )
+                right.append(
+                    jnp.concatenate(
+                        [row16(f, 16 + 16 * half + k) * along_y for k in range(9)], 0
+                    )
+                )
+            depth[16 * pair : 16 * pair + 32, 0:144] += dot_nt(
+                jnp.concatenate(left, 1), jnp.concatenate(right, 1)
             )
-            low = 1.0 - high
-            live = jnp.concatenate(
-                [jnp.where(lane < counts[tx, ty, tz], 1.0, 0.0),
-                 jnp.where(lane < counts[tx, ty, tz + 1], 1.0, 0.0)], 1
-            )
-            cell = jnp.concatenate(
-                [cells[tx, ty, tz : tz + 1, :], cells[tx, ty, tz + 1 : tz + 2, :] + 1024], 1
-            )
-            mass = high[0:1] * live
-            f[0:4, :] = high
-            f[4:8, :] = low
-            f[8:9, :] = high[3:4] * mass
-            f[9:10, :] = low[3:4] * mass
-            f[10:11, :] = ((cell >> 6) & 7).astype(F32)
-            f[11:12, :] = ((cell >> 3) & 7).astype(F32)
-            f[12:13, :] = ((cell & 7) + ((cell >> 10) << 3)).astype(F32)
-            x = jnp.concatenate([row8(f, 10)] * 2, 0)
-            low_x = jnp.concatenate([row8(f, 5)] * 2, 0)
-            high_x = jnp.concatenate([row8(f, 1)] * 2, 0)
-            f[16:32, :] = jnp.where(
-                rows == x, low_x, jnp.where(rows - 1.0 == x, high_x, 0.0)
-            )
-            y, z = row16(f, 11), row16(f, 12)
-            c0, c1 = row16(f, 9), row16(f, 8)
-            along_y = jnp.where(
-                here == y, row16(f, 6), jnp.where(before == y, row16(f, 2), zero)
-            )
-            along_z = jnp.concatenate(
-                [jnp.where(here == z, c0, jnp.where(before == z, c1, zero)),
-                 jnp.where(fifteen == z, c1, zero)], 0
-            )
-            left = jnp.concatenate([row16(f, 16 + k) * along_y for k in range(9)], 0)
-            part = jnp.concatenate(
-                [dot_nt(left, along_z), jnp.zeros((144, 96), F32)], 1
-            )
-            acc = acc + (pltpu.roll(part, 16 * pair, 1) if pair else part)
-        for k in range(9):
-            grid[8 * tx + k, pl.ds(pl.multiple_of(8 * ty, 8), 16), :] += acc[
-                16 * k : 16 * k + 16
-            ]
+        depth[0:16, :] += depth[128:144, :]
+        first = jnp.transpose(depth[0:128, 0:128])
+        final = jnp.transpose(depth[0:128, 128:256])
+        at = pl.ds(pl.multiple_of(8 * ty, 8), 16)
+        for k in range(8):
+            grid[8 * tx + k, at, :] += first[16 * k : 16 * k + 16]
+        grid[8 * tx + 8, at, :] += final[0:16]
         return 0
 
-    lax.fori_loop(0, 8, column, 0)
-    core[...] = grid[0:16, 0:32, :]
-    face_y[...] = grid[0:16, 32, :]
+    lax.fori_loop(*columns, column, 0)
 
 
 def first_kernel(
     counts, vcounts, tcounts, data_hbm, cells_hbm, vdata_hbm, vcells_hbm, tdata_hbm, tcells_hbm,
     toward, away, packs, core, face_y,
-    data, cells, vdata, vcells, tdata, tcells, grid, tile_fields, total, fields, places, lines, number, sems,
+    data, cells, vdata, vcells, tdata, tcells, grid, tile_fields, tile_places, depth, total, fields, places, lines, number, sems,
 ):
     sources = [(tdata_hbm, tdata), (tcells_hbm, tcells), (vdata_hbm, vdata), (vcells_hbm, vcells)]
     for at, offset in enumerate(OUTER):
@@ -257,7 +265,9 @@
     grid[...] = jnp.zeros_like(grid)
     for copy in copies[:2]:
         copy.wait()
-    deposit_tiles(tcounts, tdata, tcells, core, face_y, grid, tile_fields)
+    deposit_tiles((3, 8), tcounts, tdata, tcells, grid, tile_fields, tile_places, depth)
+    core[...] = grid[0:16, 0:32, :]
+    face_y[...] = grid[0:16, 32, :]
     for copy in copies[2:4]:
         copy.wait()
     for offset in range(9):
@@ -304,7 +314,9 @@
             pltpu.VMEM(tdata.shape, BF16),
             pltpu.VMEM(tcells.shape, I32),
             pltpu.VMEM((17, 40, 128), F32),
-            pltpu.VMEM((8, 32, LANES), F32),
+            pltpu.VMEM((8, 48, 128), F32),
+            pltpu.VMEM((8, 8, 128), F32),
+            pltpu.VMEM((144, 256), F32),
             pltpu.VMEM((patches, 64, 128), F32),
             pltpu.VMEM((32, 32, 128), F32),
             pltpu.VMEM((32, 8, LANES), F32),
@@ -430,20 +442,34 @@
         out[...] += dot_nt(jnp.concatenate(left, 0), along_z)
 
 
-def base_kernel(packs, right, left, core, out, lines, fields):
-    out[...] = core[...].reshape(512, 128)
+def base_kernel(
+    tcounts, tdata, tcells, packs, right, left, core, out, lines, fields, grid, tile_fields,
+    tile_places, depth
+):
+    grid[...] = jnp.zeros_like(grid)
+    grid[0:16, 0:32, :] = core[...]
+    deposit_tiles((0, 3), tcounts, tdata, tcells, grid, tile_fields, tile_places, depth)
+    out[...] = grid[0:16, 0:32, :].reshape(512, 128)
     out[0:32, :] += left[51].astype(F32) + left[52].astype(F32)
     virtual_deposit([(packs, 1), (right, 33), (left, 33)], out, lines, fields)
 
 
 def base_part(*args):
     full = pl.BlockSpec(memory_space=pltpu.VMEM)
+    smem = pl.BlockSpec(memory_space=pltpu.SMEM)
     return pl.pallas_call(
         base_kernel,
-        in_specs=[full] * 4,
+        in_specs=[smem] + [full] * 6,
         out_specs=full,
         out_shape=jax.ShapeDtypeStruct((512, 128), F32),
-        scratch_shapes=[pltpu.VMEM((2, 32, 128), F32), pltpu.VMEM((2, 32, 512), F32)],
+        scratch_shapes=[
+            pltpu.VMEM((2, 32, 128), F32),
+            pltpu.VMEM((2, 32, 512), F32),
+            pltpu.VMEM((17, 40, 128), F32),
+            pltpu.VMEM((8, 48, 128), F32),
+            pltpu.VMEM((8, 8, 128), F32),
+            pltpu.VMEM((144, 256), F32),
+        ],
         compiler_params=pltpu.CompilerParams(vmem_limit_bytes=VMEM_LIMIT),
         cost_estimate=pl.CostEstimate(
             flops=6 * 3 * 512 * 512 * 128, bytes_accessed=1000000, transcendentals=0
@@ -541,6 +567,8 @@
     tiled = tiled.transpose(0, 1, 3, 4, 2, 5)
     tiled = tiled.reshape(sources, own_patches, slots // LANES, 8, 128)
     counts = jnp.swapaxes(ghost_counts, 0, 1)
+    tiles = part_data.shape
+    pairs = part_data.reshape(tiles[0], tiles[1], tiles[2] // 2, 8, tiles[4])
     toward, away, packs, core, face_y = first_part(
         counts,
         phantom_slot_counts,
@@ -549,17 +577,17 @@
         halo_refined_cells,
         virt_data,
         jnp.swapaxes(virt_cells, 0, 1),
-        part_data,
+        pairs,
         tile_cells,
     )
     right = shift(toward, "gx", -1)
     left = shift(away, "gx", 1)
-    sides = own_part((3, 5), counts, tiled, halo_refined_cells, away)
+    sides = own_part((3, 5), counts, tiled, halo_refined_cells, face_y)
     up, down = join_part(sides, packs, right, left, face_y)
     from_up = shift(up, "gy", -1)
     from_down = shift(down, "gy", 1)
     own = own_part((4,), counts, tiled, halo_refined_cells, down)
-    part = base_part(packs, right, left, core)
+    part = base_part(tile_counts, pairs, tile_cells, packs, right, left, core)
     base, fine_mass = last_part(part, own, right, left, from_up, from_down)
     return base.reshape(16, 32, 128), fine_mass
 

time: 43 us -> 42.9 us (level); the launches traced: 42.3 us -> 42.7 us
  Pallas kernels: 30 us -> 30.6 us
    pallas_call x1, Pallas kernels: 0.63 us -> 2.54 us  [base_part(): pl.pallas_call(base_kernel, in_specs=[smem] + [full] * 6, out_specs=full,...]
    pallas_call x1, Pallas kernels: 19.4 us -> 17.5 us  [first_part(): pl.pallas_call(first_kernel, in_specs=[smem] * 3 + [hbm] * 6, out_specs=[...]
    pallas_call x2, Pallas kernels: 7.89 us -> 8.49 us  [own_part(): pl.pallas_call(functools.partial(own_kernel, offsets), in_specs=[smem, fu...]
    unnamed x14 -> x18, local copies, waits for them, and re-layouts: 1.03 us -> 0.72 us
  transfers between devices with their start and end apart: 4 -> 4, of which waited for: 1 -> 1; matrix products, arithmetic and copies ran while one was open for 0% -> 0% of each run, Pallas kernels for 20% -> 26%
where the time goes in v4:
time: 42.9 us; the launch traced here: 42.7 us
  Pallas kernels  30.6 us (71%)
  starting transfers between devices  8.67 us (20%)
  waiting for transfers between devices  1.98 us (5%)
  between operations  0.75 us (2%)
  local copies, waits for them, and re-layouts  0.72 us (2%)
    pallas_call x1, Pallas kernels, first_part(): pl.pallas_call(first_kernel, in_specs=[smem] * 3 + [hbm] * 6, out_specs=[...  17.5 us
    ppermute x4, starting transfers between devices, shift(): lax.ppermute(x, axis, [(i, (i + by) % devices) for i in range(devices)])  8.67 us
    pallas_call x2, Pallas kernels, own_part(): pl.pallas_call(functools.partial(own_kernel, offsets), in_specs=[smem, fu...  8.49 us
    pallas_call x1, Pallas kernels, base_part(): pl.pallas_call(base_kernel, in_specs=[smem] + [full] * 6, out_specs=full,...  2.54 us
    ppermute x4, waiting for transfers between devices, shift(): lax.ppermute(x, axis, [(i, (i + by) % devices) for i in range(devices)])  1.98 us
    pallas_call x1, Pallas kernels, last_part(): pl.pallas_call(last_kernel, in_specs=[full] * 6, out_specs=[full] * 2, ou...  1.96 us
  transfers between devices with their start and end apart: 4, of which 1 were waited for; matrix products, arithmetic and copies ran while one was open for 0% of the time, Pallas kernels for 26%

profile of v4, /device:TPU:1, one launch (start us, length us, event | category | flops | bytes accessed | tf_op | source)
XLA Modules:
  0.0 42.7 jit_solution(690361640342128064)
XLA Ops:
  0.6 0.0 copy-start.2
  0.6 0.0 copy-start.3
  0.7 0.0 copy-start.6
  0.7 17.5 %first.1 = (bf16[51,32,128]{2,1,0:T(8,128)(2,1)}, bf16[54,32,128]{2,1,0:T(8,128)(2,1)}, bf16[3,32,128]{2,1,0:T(8,128)(2,1)}, f32[16,32,128]{2,1,0:T(8,128)}, f32[16,128]{1,0:T(8,128)}) custom-call(s32[9,1,16]{2,1,0:T(1,128)} %bitcast.14, s32[1,9]{1,0:T(1,128)} %vcounts.1, s32[2,4,16]{2,1,0:T(4,128)} %tcounts.3, bf16[9,16,8,8,128]{4,3,2,1,0:T(8,128)(2,1)} %bitcast.9, ...), custom_call_target="tpu_custom_call" | custom-call | flops 6442450944 | bytes 4000000 | tf_op jit(solution)/shard_map/first/pallas_call | solution.py:305
  18.2 1.9 %collective-permute-start.1 = (bf16[54,32,128]{2,1,0:T(8,128)(2,1)}, bf16[54,32,128]{2,1,0:T(8,128)(2,1)S(1)}, u32[]{:S(2)}, u32[]{:S(2)}) collective-permute-start(bf16[54,32,128]{2,1,0:T(8,128)(2,1)} %get-tuple-element.13), channel_id=1, source_target_pairs={{0,16},{16,32},{32,48},{48,64},{64,80},{80,96},{96,112},{112,0},{1... | collective-permute-start | bytes 1327112 | tf_op jit(solution)/shard_map/ppermute | solution.py:22
  20.1 0.0 collective-permute-start
  20.1 0.0 copy-done.2
  20.1 0.0 copy-done.3
  20.1 0.0 copy-done.6
  20.1 0.0 copy-start.1
  20.1 0.7 %copy-done.1 = f32[16,128]{1,0:T(8,128)S(1)} copy-done((f32[16,128]{1,0:T(8,128)S(1)}, f32[16,128]{1,0:T(8,128)}, u32[]{:S(2)}) %copy-start.1) | copy-done | bytes 8216
  20.8 0.0 copy-start
  20.8 0.0 copy-start.4
  20.8 0.0 copy-start.5
  20.8 0.0 copy-start.7
  20.8 0.0 copy-start.8
  20.8 5.3 %own.2 = bf16[32,32,128]{2,1,0:T(8,128)(2,1)S(1)} custom-call(s32[9,1,16]{2,1,0:T(1,128)S(1)} %bitcast.15, bf16[9,16,8,8,128]{4,3,2,1,0:T(8,128)(2,1)S(1)} %bitcast.10, s32[1,9,16,2048]{3,2,1,0:T(8,128)S(1)} %copy-done.3, f32[16,128]{1,0:T(8,128)S(1)} %copy-done.1), custom_call_target="tpu_custom_call" | custom-call | flops 2147483648 | bytes 4000000 | tf_op jit(solution)/shard_map/own/pallas_call | solution.py:367
  26.1 2.0 %collective-permute-done.right = bf16[51,32,128]{2,1,0:T(8,128)(2,1)S(1)} collective-permute-done((bf16[51,32,128]{2,1,0:T(8,128)(2,1)}, bf16[51,32,128]{2,1,0:T(8,128)(2,1)S(1)}, u32[]{:S(2)}, u32[]{:S(2)}) %collective-permute-start) | collective-permute-done | bytes 417824 | tf_op jit(solution)/shard_map/ppermute | solution.py:22
  28.0 0.0 collective-permute-done.1.left
  28.0 0.0 copy-done
  28.0 0.1 join.1
  28.1 2.9 %collective-permute-start.3 = (bf16[20,32,128]{2,1,0:T(8,128)(2,1)S(1)}, bf16[20,32,128]{2,1,0:T(8,128)(2,1)S(1)}, u32[]{:S(2)}, u32[]{:S(2)}) collective-permute-start(bf16[20,32,128]{2,1,0:T(8,128)(2,1)S(1)} %get-tuple-element.16.wait), channel_id=1, source_target_pairs={{0,1},{1,2},{2,3},{3,4},{4,5},{5,6},{6,7},{7,8},{8,9},{9,10},{10,1... | collective-permute-start | bytes 491528 | tf_op jit(solution)/shard_map/ppermute | solution.py:22
  31.1 3.9 %collective-permute-start.2 = (bf16[19,32,128]{2,1,0:T(8,128)(2,1)S(1)}, bf16[19,32,128]{2,1,0:T(8,128)(2,1)S(1)}, u32[]{:S(2)}, u32[]{:S(2)}) collective-permute-start(bf16[19,32,128]{2,1,0:T(8,128)(2,1)S(1)} %get-tuple-element.17), channel_id=1, source_target_pairs={{0,15},{1,0},{2,1},{3,2},{4,3},{5,4},{6,5},{7,6},{8,7},{9,8},{10,9... | collective-permute-start | bytes 466952 | tf_op jit(solution)/shard_map/ppermute | solution.py:22
  35.0 0.0 copy-done.4
  35.0 0.0 copy-done.5
  35.0 0.0 copy-done.7
  35.0 0.0 copy-done.8
  35.0 2.5 %base.1.part = f32[512,128]{1,0:T(8,128)S(1)} custom-call(s32[2,4,16]{2,1,0:T(4,128)S(1)} %copy-done.7, bf16[2,4,8,8,128]{4,3,2,1,0:T(8,128)(2,1)S(1)} %bitcast.13, s32[2,4,16,128]{3,2,1,0:T(8,128)S(1)} %copy-done.5, bf16[3,32,128]{2,1,0:T(8,128)(2,1)S(1)} %copy-done, bf16[51,32,128]{2,1,0:T(8,128)(2,1)S(1)} %collective-permute-done.right, ...), custom_call_target="tpu_custom_call" | custom-call | flops 603979776 | bytes 1000000 | tf_op jit(solution)/shard_map/base/pallas_call | solution.py:460
  37.5 3.2 %own.3 = bf16[16,32,128]{2,1,0:T(8,128)(2,1)S(1)} custom-call(s32[9,1,16]{2,1,0:T(1,128)S(1)} %bitcast.16, bf16[9,16,8,8,128]{4,3,2,1,0:T(8,128)(2,1)S(1)} %bitcast.11, s32[1,9,16,2048]{3,2,1,0:T(8,128)S(1)} %copy-done.3, bf16[20,32,128]{2,1,0:T(8,128)(2,1)S(1)} %get-tuple-element.16.wait), custom_call_target="tpu_custom_call" | custom-call | flops 1073741824 | bytes 4000000 | tf_op jit(solution)/shard_map/own/pallas_call | solution.py:367
  40.8 0.0 collective-permute-done.2.up
  40.8 0.0 collective-permute-done.3.down
  40.8 2.0 %last.1 = (f32[512,128]{1,0:T(8,128)}, f32[16,4096]{1,0:T(8,128)}) custom-call(f32[512,128]{1,0:T(8,128)S(1)} %base.1.part, bf16[16,32,128]{2,1,0:T(8,128)(2,1)S(1)} %own.3, bf16[51,32,128]{2,1,0:T(8,128)(2,1)S(1)} %collective-permute-done.right, bf16[54,32,128]{2,1,0:T(8,128)(2,1)S(1)} %collective-permute-done.1.left, ...), custom_call_target="tpu_custom_call" | custom-call | tf_op jit(solution)/shard_map/last/pallas_call | solution.py:536
Async XLA Ops:
  0.6 19.4 %copy-start.2 = (bf16[1,9,16,4,2048]{4,3,2,1,0:T(4,128)(2,1)S(1)}, bf16[1,9,16,4,2048]{4,3,2,1,0:T(4,128)(2,1)}, u32[]{:S(2)}) copy-start(bf16[1,9,16,4,2048]{4,3,2,1,0:T(4,128)(2,1)} %param.12) | copy-start | bytes 7077892
  0.6 19.4 %copy-start.3 = (s32[1,9,16,2048]{3,2,1,0:T(8,128)S(1)}, s32[1,9,16,2048]{3,2,1,0:T(8,128)}, u32[]{:S(2)}) copy-start(s32[1,9,16,2048]{3,2,1,0:T(8,128)} %cells.3) | copy-start | bytes 3538948
  0.7 19.4 %copy-start.6 = (s32[1,9,16]{2,0,1:T(1,128)S(1)}, s32[1,9,16]{2,0,1:T(1,128)}, u32[]{:S(2)}) copy-start(s32[1,9,16]{2,0,1:T(1,128)} %param.14) | copy-start | bytes 1732
  18.2 9.8 %collective-permute-start.1 = (bf16[54,32,128]{2,1,0:T(8,128)(2,1)}, bf16[54,32,128]{2,1,0:T(8,128)(2,1)S(1)}, u32[]{:S(2)}, u32[]{:S(2)}) collective-permute-start(bf16[54,32,128]{2,1,0:T(8,128)(2,1)} %get-tuple-element.13), channel_id=1, source_target_pairs={{0,16},{16,32},{32,48},{48,64},{64,80},{80,96},{96,112},{112,0},{1... | collective-permute-start | bytes 1327112 | tf_op jit(solution)/shard_map/ppermute | solution.py:22
  20.1 8.0 %collective-permute-start = (bf16[51,32,128]{2,1,0:T(8,128)(2,1)}, bf16[51,32,128]{2,1,0:T(8,128)(2,1)S(1)}, u32[]{:S(2)}, u32[]{:S(2)}) collective-permute-start(bf16[51,32,128]{2,1,0:T(8,128)(2,1)} %get-tuple-element.12), channel_id=1, source_target_pairs={{0,112},{16,0},{32,16},{48,32},{64,48},{80,64},{96,80},{112,96},{1... | collective-permute-start | bytes 1253384 | tf_op jit(solution)/shard_map/ppermute | solution.py:22
  20.1 0.7 %copy-start.1 = (f32[16,128]{1,0:T(8,128)S(1)}, f32[16,128]{1,0:T(8,128)}, u32[]{:S(2)}) copy-start(f32[16,128]{1,0:T(8,128)} %get-tuple-element.15.wait.face_y) | copy-start | bytes 24580
  20.8 7.3 %copy-start = (bf16[3,32,128]{2,1,0:T(8,128)(2,1)S(1)}, bf16[3,32,128]{2,1,0:T(8,128)(2,1)}, u32[]{:S(2)}) copy-start(bf16[3,32,128]{2,1,0:T(8,128)(2,1)} %get-tuple-element.11.packs) | copy-start | bytes 73732
  20.8 14.2 %copy-start.4 = (bf16[2,4,16,4,128]{4,3,2,1,0:T(4,128)(2,1)S(1)}, bf16[2,4,16,4,128]{4,3,2,1,0:T(4,128)(2,1)}, u32[]{:S(2)}) copy-start(bf16[2,4,16,4,128]{4,3,2,1,0:T(4,128)(2,1)} %param.9) | copy-start | bytes 393220
  20.8 14.2 %copy-start.5 = (s32[2,4,16,128]{3,2,1,0:T(8,128)S(1)}, s32[2,4,16,128]{3,2,1,0:T(8,128)}, u32[]{:S(2)}) copy-start(s32[2,4,16,128]{3,2,1,0:T(8,128)} %tcells.1) | copy-start | bytes 196612
  20.8 14.2 %copy-start.7 = (s32[2,4,16]{2,1,0:T(4,128)S(1)}, s32[2,4,16]{2,1,0:T(4,128)}, u32[]{:S(2)}) copy-start(s32[2,4,16]{2,1,0:T(4,128)} %tcounts.3) | copy-start | bytes 1540
  20.8 14.2 %copy-start.8 = (f32[16,32,128]{2,1,0:T(8,128)S(1)}, f32[16,32,128]{2,1,0:T(8,128)}, u32[]{:S(2)}) copy-start(f32[16,32,128]{2,1,0:T(8,128)} %get-tuple-element.14.core) | copy-start | bytes 786436
  28.1 12.6 %collective-permute-start.3 = (bf16[20,32,128]{2,1,0:T(8,128)(2,1)S(1)}, bf16[20,32,128]{2,1,0:T(8,128)(2,1)S(1)}, u32[]{:S(2)}, u32[]{:S(2)}) collective-permute-start(bf16[20,32,128]{2,1,0:T(8,128)(2,1)S(1)} %get-tuple-element.16.wait), channel_id=1, source_target_pairs={{0,1},{1,2},{2,3},{3,4},{4,5},{5,6},{6,7},{7,8},{8,9},{9,10},{10,1... | collective-permute-start | bytes 491528 | tf_op jit(solution)/shard_map/ppermute | solution.py:22
  31.1 9.7 %collective-permute-start.2 = (bf16[19,32,128]{2,1,0:T(8,128)(2,1)S(1)}, bf16[19,32,128]{2,1,0:T(8,128)(2,1)S(1)}, u32[]{:S(2)}, u32[]{:S(2)}) collective-permute-start(bf16[19,32,128]{2,1,0:T(8,128)(2,1)S(1)} %get-tuple-element.17), channel_id=1, source_target_pairs={{0,15},{1,0},{2,1},{3,2},{4,3},{5,4},{6,5},{7,6},{8,7},{9,8},{10,9... | collective-permute-start | bytes 466952 | tf_op jit(solution)/shard_map/ppermute | solution.py:22

commit v5 on v4

--- a/solution.py
+++ b/solution.py
@@ -12,6 +12,9 @@
 I32 = jnp.int32
 NT = (((1,), (1,)), ((), ()))
 LANES = 256
+FIRST_UNROLLS = (48, 16)
+OWN_UNROLLS = (48, 16)
+EXTRA = 64
 OUTER = (0, 1, 2, 6, 7, 8)
 VMEM_LIMIT = 16 * 2**20
 FIRST_LIMIT = 56 * 2**20
@@ -63,7 +66,7 @@
     return lines[...].astype(BF16)
 
 
-def deposit_ghosts(offsets, unroll, counts, get_data, get_cells, outs, total, fields, places, number, ready):
+def deposit_ghosts(offsets, unrolls, counts, get_data, get_cells, outs, total, fields, places, number, ready):
     split = len(outs)
     patches = 16 * len(offsets)
     each = len(offsets) // split
@@ -74,9 +77,8 @@
             live = counts[offset, 0, patch]
             number[16 * at + patch] = live
             work = work + jnp.maximum((live + (LANES - 1)) >> 8, 1)
-    for extra in range(unroll + 4):
+    for extra in range(EXTRA):
         number[patches + extra] = 0
-    steps = lax.div(work + (unroll - 1), unroll)
     lane = lax.broadcasted_iota(I32, (8, 128), 1)
     here = sublane(16, 128).astype(BF16)
     before = (sublane(16, 128) - 1.0).astype(BF16)
@@ -147,13 +149,21 @@
             number[group + 2],
         )
 
-    def body(_, state):
-        for unit in range(unroll):
-            state = deposit(unit, *state)
-        return state
-
     none = jnp.int32(0)
-    lax.fori_loop(0, steps, body, (none, none, number[0], number[1], number[2]))
+    state = (none, none, number[0], number[1], number[2])
+    for unroll in unrolls:
+        if unroll == unrolls[-1]:
+            steps = lax.div(work + (unroll - 1), unroll)
+        else:
+            steps = lax.div(work, unroll)
+            work = work - steps * unroll
+
+        def body(_, state, unroll=unroll):
+            for unit in range(unroll):
+                state = deposit(unit, *state)
+            return state
+
+        state = lax.fori_loop(0, steps, body, state)
     lane = lax.broadcasted_iota(I32, (16, 128), 1)
 
     for index in range(split):
@@ -283,7 +293,7 @@
     away[53] = jnp.concatenate([high, low], 0)
     deposit_ghosts(
         OUTER,
-        32,
+        FIRST_UNROLLS,
         counts,
         lambda group, chunk: data[group, chunk],
         lambda group, at: cells[pl.ds(group, 1), pl.ds(at, LANES)],
@@ -318,10 +328,10 @@
             pltpu.VMEM((8, 8, 128), F32),
             pltpu.VMEM((144, 256), F32),
             pltpu.VMEM((patches, 64, 128), F32),
-            pltpu.VMEM((32, 32, 128), F32),
-            pltpu.VMEM((32, 8, LANES), F32),
+            pltpu.VMEM((max(FIRST_UNROLLS), 32, 128), F32),
+            pltpu.VMEM((max(FIRST_UNROLLS), 8, LANES), F32),
             pltpu.VMEM((32, 128), F32),
-            pltpu.SMEM((patches + 36,), I32),
+            pltpu.SMEM((patches + EXTRA,), I32),
             pltpu.SemaphoreType.DMA((16,)),
         ],
         out_shape=[
@@ -354,7 +364,7 @@
         return cells[0, offset, pl.ds(patch, 1), pl.ds(at, LANES)]
 
     deposit_ghosts(
-        offsets, 24, counts, get_data, get_cells, (out,), total, fields, places, number, ()
+        offsets, OWN_UNROLLS, counts, get_data, get_cells, (out,), total, fields, places, number, ()
     )
 
 
@@ -370,9 +380,9 @@
         out_specs=full,
         scratch_shapes=[
             pltpu.VMEM((patches, 64, 128), F32),
-            pltpu.VMEM((24, 32, 128), F32),
-            pltpu.VMEM((24, 8, LANES), F32),
-            pltpu.SMEM((patches + 28,), I32),
+            pltpu.VMEM((max(OWN_UNROLLS), 32, 128), F32),
+            pltpu.VMEM((max(OWN_UNROLLS), 8, LANES), F32),
+            pltpu.SMEM((patches + EXTRA,), I32),
         ],
         out_shape=jax.ShapeDtypeStruct((patches, 32, 128), BF16),
         compiler_params=pltpu.CompilerParams(vmem_limit_bytes=VMEM_LIMIT),
@@ -508,7 +518,9 @@
     )(*args)
 
 
-def last_kernel(part, own, right, left, up, down, base, out, patches, fields, lines):
+def last_kernel(
+    part, own, right, left, up, down, base_hbm, out_hbm, patches, fields, lines, base, out, sems
+):
     for patch in range(16):
         mass = (
             (own[patch].astype(F32) + left[17 + patch].astype(F32))
@@ -521,6 +533,8 @@
                 block = patches[pl.ds(256 * group + 16 * half + x, 8, stride=32), :]
                 at = 128 * (2 * x + half)
                 out[8 * group : 8 * group + 8, at : at + 128] = block
+    fine_copy = pltpu.make_async_copy(out, out_hbm, sems.at[0])
+    fine_copy.start()
     base[...] = part[...]
     both = down[19].astype(F32)
     face = both[0:16] + both[16:32]
@@ -529,6 +543,10 @@
     virtual_deposit(
         [(source, slot) for source in (up, down) for slot in (16, 17, 18)], base, lines, fields
     )
+    base_copy = pltpu.make_async_copy(base, base_hbm, sems.at[1])
+    base_copy.start()
+    fine_copy.wait()
+    base_copy.wait()
 
 
 def last_part(*args):
@@ -536,7 +554,7 @@
     return pl.pallas_call(
         last_kernel,
         in_specs=[full] * 6,
-        out_specs=[full] * 2,
+        out_specs=[pl.BlockSpec(memory_space=pl.ANY)] * 2,
         out_shape=[
             jax.ShapeDtypeStruct((512, 128), F32),
             jax.ShapeDtypeStruct((16, 4096), F32),
@@ -545,6 +563,9 @@
             pltpu.VMEM((512, 128), F32),
             pltpu.VMEM((2, 32, 512), F32),
             pltpu.VMEM((2, 32, 128), F32),
+            pltpu.VMEM((512, 128), F32),
+            pltpu.VMEM((16, 4096), F32),
+            pltpu.SemaphoreType.DMA((2,)),
         ],
         compiler_params=pltpu.CompilerParams(vmem_limit_bytes=VMEM_LIMIT),
         name="last",

time: 42.9 us -> 42.1 us (0.981)
  Pallas kernels: 30.6 us -> 28 us
  starting transfers between devices: 8.67 us -> 9.86 us
  waiting for transfers between devices: 1.98 us -> 2.66 us
    pallas_call x1, Pallas kernels: 17.5 us -> 15.9 us  [first_part(): pl.pallas_call(first_kernel, in_specs=[smem] * 3 + [hbm] * 6, out_specs=[...]
    ppermute x4, starting transfers between devices: 8.67 us -> 9.86 us  [shift(): lax.ppermute(x, axis, [(i, (i + by) % devices) for i in range(devices)])]
    pallas_call x2, Pallas kernels: 8.49 us -> 7.4 us  [own_part(): pl.pallas_call(functools.partial(own_kernel, offsets), in_specs=[smem, fu...]
    ppermute x4, waiting for transfers between devices: 1.98 us -> 2.66 us  [shift(): lax.ppermute(x, axis, [(i, (i + by) % devices) for i in range(devices)])]
  transfers between devices with their start and end apart: 4 -> 4, of which waited for: 1 -> 1; matrix products, arithmetic and copies ran while one was open for 0% -> 0% of each run, Pallas kernels for 26% -> 24%
where the time goes in v5:
time: 42.1 us; the launch traced here: 42 us
  Pallas kernels  28 us (67%)
  starting transfers between devices  9.86 us (23%)
  waiting for transfers between devices  2.66 us (6%)
  between operations  0.75 us (2%)
  local copies, waits for them, and re-layouts  0.72 us (2%)
    pallas_call x1, Pallas kernels, first_part(): pl.pallas_call(first_kernel, in_specs=[smem] * 3 + [hbm] * 6, out_specs=[...  15.9 us
    ppermute x4, starting transfers between devices, shift(): lax.ppermute(x, axis, [(i, (i + by) % devices) for i in range(devices)])  9.86 us
    pallas_call x2, Pallas kernels, own_part(): pl.pallas_call(functools.partial(own_kernel, offsets), in_specs=[smem, fu...  7.4 us
    ppermute x4, waiting for transfers between devices, shift(): lax.ppermute(x, axis, [(i, (i + by) % devices) for i in range(devices)])  2.66 us
    pallas_call x1, Pallas kernels, base_part(): pl.pallas_call(base_kernel, in_specs=[smem] + [full] * 6, out_specs=full,...  2.54 us
    pallas_call x1, Pallas kernels, last_part(): pl.pallas_call(last_kernel, in_specs=[full] * 6, out_specs=[pl.BlockSpec(...  2.07 us
  transfers between devices with their start and end apart: 4, of which 1 were waited for; matrix products, arithmetic and copies ran while one was open for 0% of the time, Pallas kernels for 24%

profile of v5, /device:TPU:1, one launch (start us, length us, event | category | flops | bytes accessed | tf_op | source)
XLA Modules:
  0.0 42.0 jit_solution(1663471885724394656)
XLA Ops:
  0.6 0.0 copy-start.2
  0.6 0.0 copy-start.3
  0.7 0.0 copy-start.6
  0.7 15.9 %first.1 = (bf16[51,32,128]{2,1,0:T(8,128)(2,1)}, bf16[54,32,128]{2,1,0:T(8,128)(2,1)}, bf16[3,32,128]{2,1,0:T(8,128)(2,1)}, f32[16,32,128]{2,1,0:T(8,128)}, f32[16,128]{1,0:T(8,128)}) custom-call(s32[9,1,16]{2,1,0:T(1,128)} %bitcast.14, s32[1,9]{1,0:T(1,128)} %vcounts.1, s32[2,4,16]{2,1,0:T(4,128)} %tcounts.3, bf16[9,16,8,8,128]{4,3,2,1,0:T(8,128)(2,1)} %bitcast.9, ...), custom_call_target="tpu_custom_call" | custom-call | flops 6442450944 | bytes 4000000 | tf_op jit(solution)/shard_map/first/pallas_call | solution.py:315
  16.6 3.1 %collective-permute-start.1 = (bf16[54,32,128]{2,1,0:T(8,128)(2,1)}, bf16[54,32,128]{2,1,0:T(8,128)(2,1)S(1)}, u32[]{:S(2)}, u32[]{:S(2)}) collective-permute-start(bf16[54,32,128]{2,1,0:T(8,128)(2,1)} %get-tuple-element.13), channel_id=1, source_target_pairs={{0,16},{16,32},{32,48},{48,64},{64,80},{80,96},{96,112},{112,0},{1... | collective-permute-start | bytes 1327112 | tf_op jit(solution)/shard_map/ppermute | solution.py:25
  19.6 0.0 collective-permute-start
  19.7 0.0 copy-done.2
  19.7 0.0 copy-done.3
  19.7 0.0 copy-done.6
  19.7 0.0 copy-start.1
  19.7 0.7 %copy-done.1 = f32[16,128]{1,0:T(8,128)S(1)} copy-done((f32[16,128]{1,0:T(8,128)S(1)}, f32[16,128]{1,0:T(8,128)}, u32[]{:S(2)}) %copy-start.1) | copy-done | bytes 8216
  20.4 0.0 copy-start
  20.4 0.0 copy-start.4
  20.4 0.0 copy-start.5
  20.4 0.0 copy-start.7
  20.4 0.0 copy-start.8
  20.4 4.6 %own.2 = bf16[32,32,128]{2,1,0:T(8,128)(2,1)S(1)} custom-call(s32[9,1,16]{2,1,0:T(1,128)S(1)} %bitcast.15, bf16[9,16,8,8,128]{4,3,2,1,0:T(8,128)(2,1)S(1)} %bitcast.10, s32[1,9,16,2048]{3,2,1,0:T(8,128)S(1)} %copy-done.3, f32[16,128]{1,0:T(8,128)S(1)} %copy-done.1), custom_call_target="tpu_custom_call" | custom-call | flops 2147483648 | bytes 4000000 | tf_op jit(solution)/shard_map/own/pallas_call | solution.py:377
  25.0 2.6 %collective-permute-done.right = bf16[51,32,128]{2,1,0:T(8,128)(2,1)S(1)} collective-permute-done((bf16[51,32,128]{2,1,0:T(8,128)(2,1)}, bf16[51,32,128]{2,1,0:T(8,128)(2,1)S(1)}, u32[]{:S(2)}, u32[]{:S(2)}) %collective-permute-start) | collective-permute-done | bytes 417824 | tf_op jit(solution)/shard_map/ppermute | solution.py:25
  27.6 0.0 collective-permute-done.1.left
  27.6 0.0 copy-done
  27.6 0.1 join.1
  27.7 2.5 %collective-permute-start.3 = (bf16[20,32,128]{2,1,0:T(8,128)(2,1)S(1)}, bf16[20,32,128]{2,1,0:T(8,128)(2,1)S(1)}, u32[]{:S(2)}, u32[]{:S(2)}) collective-permute-start(bf16[20,32,128]{2,1,0:T(8,128)(2,1)S(1)} %get-tuple-element.16.wait), channel_id=1, source_target_pairs={{0,1},{1,2},{2,3},{3,4},{4,5},{5,6},{6,7},{7,8},{8,9},{9,10},{10,1... | collective-permute-start | bytes 491528 | tf_op jit(solution)/shard_map/ppermute | solution.py:25
  30.2 4.3 %collective-permute-start.2 = (bf16[19,32,128]{2,1,0:T(8,128)(2,1)S(1)}, bf16[19,32,128]{2,1,0:T(8,128)(2,1)S(1)}, u32[]{:S(2)}, u32[]{:S(2)}) collective-permute-start(bf16[19,32,128]{2,1,0:T(8,128)(2,1)S(1)} %get-tuple-element.17), channel_id=1, source_target_pairs={{0,15},{1,0},{2,1},{3,2},{4,3},{5,4},{6,5},{7,6},{8,7},{9,8},{10,9... | collective-permute-start | bytes 466952 | tf_op jit(solution)/shard_map/ppermute | solution.py:25
  34.5 0.0 copy-done.4
  34.5 0.0 copy-done.5
  34.5 0.0 copy-done.7
  34.5 0.0 copy-done.8
  34.5 2.5 %base.1.part = f32[512,128]{1,0:T(8,128)S(1)} custom-call(s32[2,4,16]{2,1,0:T(4,128)S(1)} %copy-done.7, bf16[2,4,8,8,128]{4,3,2,1,0:T(8,128)(2,1)S(1)} %bitcast.13, s32[2,4,16,128]{3,2,1,0:T(8,128)S(1)} %copy-done.5, bf16[3,32,128]{2,1,0:T(8,128)(2,1)S(1)} %copy-done, bf16[51,32,128]{2,1,0:T(8,128)(2,1)S(1)} %collective-permute-done.right, ...), custom_call_target="tpu_custom_call" | custom-call | flops 603979776 | bytes 1000000 | tf_op jit(solution)/shard_map/base/pallas_call | solution.py:470
  37.1 2.8 %own.3 = bf16[16,32,128]{2,1,0:T(8,128)(2,1)S(1)} custom-call(s32[9,1,16]{2,1,0:T(1,128)S(1)} %bitcast.16, bf16[9,16,8,8,128]{4,3,2,1,0:T(8,128)(2,1)S(1)} %bitcast.11, s32[1,9,16,2048]{3,2,1,0:T(8,128)S(1)} %copy-done.3, bf16[20,32,128]{2,1,0:T(8,128)(2,1)S(1)} %get-tuple-element.16.wait), custom_call_target="tpu_custom_call" | custom-call | flops 1073741824 | bytes 4000000 | tf_op jit(solution)/shard_map/own/pallas_call | solution.py:377
  39.9 0.0 collective-permute-done.2.up
  39.9 0.0 collective-permute-done.3.down
  39.9 2.1 %last.1 = (f32[512,128]{1,0:T(8,128)}, f32[16,4096]{1,0:T(8,128)}) custom-call(f32[512,128]{1,0:T(8,128)S(1)} %base.1.part, bf16[16,32,128]{2,1,0:T(8,128)(2,1)S(1)} %own.3, bf16[51,32,128]{2,1,0:T(8,128)(2,1)S(1)} %collective-permute-done.right, bf16[54,32,128]{2,1,0:T(8,128)(2,1)S(1)} %collective-permute-done.1.left, ...), custom_call_target="tpu_custom_call" | custom-call | tf_op jit(solution)/shard_map/last/pallas_call | solution.py:554
Async XLA Ops:
  0.6 19.0 %copy-start.2 = (bf16[1,9,16,4,2048]{4,3,2,1,0:T(4,128)(2,1)S(1)}, bf16[1,9,16,4,2048]{4,3,2,1,0:T(4,128)(2,1)}, u32[]{:S(2)}) copy-start(bf16[1,9,16,4,2048]{4,3,2,1,0:T(4,128)(2,1)} %param.12) | copy-start | bytes 7077892
  0.6 19.0 %copy-start.3 = (s32[1,9,16,2048]{3,2,1,0:T(8,128)S(1)}, s32[1,9,16,2048]{3,2,1,0:T(8,128)}, u32[]{:S(2)}) copy-start(s32[1,9,16,2048]{3,2,1,0:T(8,128)} %cells.3) | copy-start | bytes 3538948
  0.7 19.0 %copy-start.6 = (s32[1,9,16]{2,0,1:T(1,128)S(1)}, s32[1,9,16]{2,0,1:T(1,128)}, u32[]{:S(2)}) copy-start(s32[1,9,16]{2,0,1:T(1,128)} %param.14) | copy-start | bytes 1732
  16.6 11.0 %collective-permute-start.1 = (bf16[54,32,128]{2,1,0:T(8,128)(2,1)}, bf16[54,32,128]{2,1,0:T(8,128)(2,1)S(1)}, u32[]{:S(2)}, u32[]{:S(2)}) collective-permute-start(bf16[54,32,128]{2,1,0:T(8,128)(2,1)} %get-tuple-element.13), channel_id=1, source_target_pairs={{0,16},{16,32},{32,48},{48,64},{64,80},{80,96},{96,112},{112,0},{1... | collective-permute-start | bytes 1327112 | tf_op jit(solution)/shard_map/ppermute | solution.py:25
  19.6 8.0 %collective-permute-start = (bf16[51,32,128]{2,1,0:T(8,128)(2,1)}, bf16[51,32,128]{2,1,0:T(8,128)(2,1)S(1)}, u32[]{:S(2)}, u32[]{:S(2)}) collective-permute-start(bf16[51,32,128]{2,1,0:T(8,128)(2,1)} %get-tuple-element.12), channel_id=1, source_target_pairs={{0,112},{16,0},{32,16},{48,32},{64,48},{80,64},{96,80},{112,96},{1... | collective-permute-start | bytes 1253384 | tf_op jit(solution)/shard_map/ppermute | solution.py:25
  19.7 0.7 %copy-start.1 = (f32[16,128]{1,0:T(8,128)S(1)}, f32[16,128]{1,0:T(8,128)}, u32[]{:S(2)}) copy-start(f32[16,128]{1,0:T(8,128)} %get-tuple-element.15.wait.face_y) | copy-start | bytes 24580
  20.4 7.3 %copy-start = (bf16[3,32,128]{2,1,0:T(8,128)(2,1)S(1)}, bf16[3,32,128]{2,1,0:T(8,128)(2,1)}, u32[]{:S(2)}) copy-start(bf16[3,32,128]{2,1,0:T(8,128)(2,1)} %get-tuple-element.11.packs) | copy-start | bytes 73732
  20.4 14.2 %copy-start.4 = (bf16[2,4,16,4,128]{4,3,2,1,0:T(4,128)(2,1)S(1)}, bf16[2,4,16,4,128]{4,3,2,1,0:T(4,128)(2,1)}, u32[]{:S(2)}) copy-start(bf16[2,4,16,4,128]{4,3,2,1,0:T(4,128)(2,1)} %param.9) | copy-start | bytes 393220
  20.4 14.2 %copy-start.5 = (s32[2,4,16,128]{3,2,1,0:T(8,128)S(1)}, s32[2,4,16,128]{3,2,1,0:T(8,128)}, u32[]{:S(2)}) copy-start(s32[2,4,16,128]{3,2,1,0:T(8,128)} %tcells.1) | copy-start | bytes 196612
  20.4 14.2 %copy-start.7 = (s32[2,4,16]{2,1,0:T(4,128)S(1)}, s32[2,4,16]{2,1,0:T(4,128)}, u32[]{:S(2)}) copy-start(s32[2,4,16]{2,1,0:T(4,128)} %tcounts.3) | copy-start | bytes 1540
  20.4 14.2 %copy-start.8 = (f32[16,32,128]{2,1,0:T(8,128)S(1)}, f32[16,32,128]{2,1,0:T(8,128)}, u32[]{:S(2)}) copy-start(f32[16,32,128]{2,1,0:T(8,128)} %get-tuple-element.14.core) | copy-start | bytes 786436
  27.7 12.2 %collective-permute-start.3 = (bf16[20,32,128]{2,1,0:T(8,128)(2,1)S(1)}, bf16[20,32,128]{2,1,0:T(8,128)(2,1)S(1)}, u32[]{:S(2)}, u32[]{:S(2)}) collective-permute-start(bf16[20,32,128]{2,1,0:T(8,128)(2,1)S(1)} %get-tuple-element.16.wait), channel_id=1, source_target_pairs={{0,1},{1,2},{2,3},{3,4},{4,5},{5,6},{6,7},{7,8},{8,9},{9,10},{10,1... | collective-permute-start | bytes 491528 | tf_op jit(solution)/shard_map/ppermute | solution.py:25
  30.2 9.7 %collective-permute-start.2 = (bf16[19,32,128]{2,1,0:T(8,128)(2,1)S(1)}, bf16[19,32,128]{2,1,0:T(8,128)(2,1)S(1)}, u32[]{:S(2)}, u32[]{:S(2)}) collective-permute-start(bf16[19,32,128]{2,1,0:T(8,128)(2,1)S(1)} %get-tuple-element.17), channel_id=1, source_target_pairs={{0,15},{1,0},{2,1},{3,2},{4,3},{5,4},{6,5},{7,6},{8,7},{9,8},{10,9... | collective-permute-start | bytes 466952 | tf_op jit(solution)/shard_map/ppermute | solution.py:25

commit v6 on v5

--- a/solution.py
+++ b/solution.py
@@ -70,7 +70,6 @@
     split = len(outs)
     patches = 16 * len(offsets)
     each = len(offsets) // split
-    total[...] = jnp.zeros_like(total)
     work = jnp.int32(0)
     for at, offset in enumerate(offsets):
         for patch in range(16):
@@ -180,10 +179,10 @@
                 out[k + (k >> 4) if split > 1 else k, 16 * half : 16 * half + 16] = (even + swapped).astype(BF16)
             return 0
 
-        lax.fori_loop(0, 16 * each, fold, 0, unroll=8)
-
-
-def deposit_tiles(columns, counts, data, cells, grid, fields, places, depth):
+        lax.fori_loop(0, 16 * each, fold, 0, unroll=16)
+
+
+def deposit_tiles(columns, counts, data, cells, grid, fields, places, depth, total=None):
     lane = lax.broadcasted_iota(I32, (8, 128), 1)
     here = sublane(16, 128).astype(BF16)
     before = (sublane(16, 128) - 1.0).astype(BF16)
@@ -199,6 +198,11 @@
         tx = col >> 2
         ty = col & 3
         depth[...] = jnp.zeros_like(depth)
+        if total is not None:
+            patches = total.shape[0]
+            share = -(-patches // (columns[1] - columns[0]))
+            begin = jnp.minimum((col - columns[0]) * share, patches - share)
+            total[pl.ds(begin, share)] = jnp.zeros((share,) + total.shape[1:], F32)
         for pair in range(8):
             f = fields.at[pair]
             g = places.at[pair]
@@ -275,7 +279,7 @@
     grid[...] = jnp.zeros_like(grid)
     for copy in copies[:2]:
         copy.wait()
-    deposit_tiles((3, 8), tcounts, tdata, tcells, grid, tile_fields, tile_places, depth)
+    deposit_tiles((3, 8), tcounts, tdata, tcells, grid, tile_fields, tile_places, depth, total)
     core[...] = grid[0:16, 0:32, :]
     face_y[...] = grid[0:16, 32, :]
     for copy in copies[2:4]:
@@ -350,8 +354,10 @@
 
 
 def own_kernel(
-    offsets, counts, data, cells, wait, out, total, fields, places, number
+    offsets, counts, data, cells, *rest
 ):
+    out, total, fields, places, number = rest[-5:]
+
     def split(group):
         return offsets[0] + 2 * (group >> 4), group & 15
 
@@ -363,6 +369,7 @@
         offset, patch = split(group)
         return cells[0, offset, pl.ds(patch, 1), pl.ds(at, LANES)]
 
+    total[...] = jnp.zeros_like(total)
     deposit_ghosts(
         offsets, OWN_UNROLLS, counts, get_data, get_cells, (out,), total, fields, places, number, ()
     )
@@ -370,13 +377,14 @@
 
 def own_part(offsets, counts, data, cells, wait):
     slots = cells.shape[3]
+    waits = () if wait is None else (wait,)
     patches = 16 * len(offsets)
     full = pl.BlockSpec(memory_space=pltpu.VMEM)
     smem = pl.BlockSpec(memory_space=pltpu.SMEM)
     anywhere = pl.BlockSpec(memory_space=pl.ANY)
     return pl.pallas_call(
         functools.partial(own_kernel, offsets),
-        in_specs=[smem, full, full, anywhere],
+        in_specs=[smem, full, full] + [anywhere] * len(waits),
         out_specs=full,
         scratch_shapes=[
             pltpu.VMEM((patches, 64, 128), F32),
@@ -390,7 +398,7 @@
             flops=4 * patches * slots * 64 * 128, bytes_accessed=4000000, transcendentals=0
         ),
         name="own",
-    )(counts, data, cells, wait)
+    )(counts, data, cells, *waits)
 
 
 def virtual_deposit(packs, out, lines, fields):
@@ -603,7 +611,7 @@
     )
     right = shift(toward, "gx", -1)
     left = shift(away, "gx", 1)
-    sides = own_part((3, 5), counts, tiled, halo_refined_cells, face_y)
+    sides = own_part((3, 5), counts, tiled, halo_refined_cells, None)
     up, down = join_part(sides, packs, right, left, face_y)
     from_up = shift(up, "gy", -1)
     from_down = shift(down, "gy", 1)

time: 42.1 us -> 41.8 us (level)
  the two profiles are of different devices: /device:TPU:1 before, /device:TPU:7 now
where the time goes in v6:
time: 41.8 us
  Pallas kernels  28 us (67%)
  starting transfers between devices  8.65 us (21%)
  waiting for transfers between devices  4.41 us (11%)
  between operations  0.77 us (2%)
    pallas_call x1, Pallas kernels, first_part(): pl.pallas_call(first_kernel, in_specs=[smem] * 3 + [hbm] * 6, out_specs=[...  16.1 us
    ppermute x4, starting transfers between devices, shift(): lax.ppermute(x, axis, [(i, (i + by) % devices) for i in range(devices)])  8.65 us
    pallas_call x2, Pallas kernels, own_part(): pl.pallas_call(functools.partial(own_kernel, offsets), in_specs=[smem, fu...  7.19 us
    ppermute x4, waiting for transfers between devices, shift(): lax.ppermute(x, axis, [(i, (i + by) % devices) for i in range(devices)])  4.41 us
    pallas_call x1, Pallas kernels, base_part(): pl.pallas_call(base_kernel, in_specs=[smem] + [full] * 6, out_specs=full,...  2.54 us
    pallas_call x1, Pallas kernels, last_part(): pl.pallas_call(last_kernel, in_specs=[full] * 6, out_specs=[pl.BlockSpec(...  2.07 us
  transfers between devices with their start and end apart: 4, of which 1 were waited for; matrix products, arithmetic and copies ran while one was open for 0% of the time, Pallas kernels for 23%

profile of v6, /device:TPU:7, one launch (start us, length us, event | category | flops | bytes accessed | tf_op | source)
XLA Modules:
  0.0 41.8 jit_solution(1257140770262367615)
XLA Ops:
  0.6 0.0 copy-start.2
  0.6 0.0 copy-start.3
  0.7 0.0 copy-start.6
  0.7 16.1 %first.1 = (bf16[51,32,128]{2,1,0:T(8,128)(2,1)}, bf16[54,32,128]{2,1,0:T(8,128)(2,1)}, bf16[3,32,128]{2,1,0:T(8,128)(2,1)}, f32[16,32,128]{2,1,0:T(8,128)}, f32[16,128]{1,0:T(8,128)}) custom-call(s32[9,1,16]{2,1,0:T(1,128)} %bitcast.14, s32[1,9]{1,0:T(1,128)} %vcounts.1, s32[2,4,16]{2,1,0:T(4,128)} %tcounts.3, bf16[9,16,8,8,128]{4,3,2,1,0:T(8,128)(2,1)} %bitcast.9, ...), custom_call_target="tpu_custom_call" | custom-call | flops 6442450944 | bytes 4000000 | tf_op jit(solution)/shard_map/first/pallas_call | solution.py:319
  16.7 1.7 %collective-permute-start.1 = (bf16[54,32,128]{2,1,0:T(8,128)(2,1)}, bf16[54,32,128]{2,1,0:T(8,128)(2,1)S(1)}, u32[]{:S(2)}, u32[]{:S(2)}) collective-permute-start(bf16[54,32,128]{2,1,0:T(8,128)(2,1)} %get-tuple-element.13), channel_id=1, source_target_pairs={{0,16},{16,32},{32,48},{48,64},{64,80},{80,96},{96,112},{112,0},{1... | collective-permute-start | bytes 1327112 | tf_op jit(solution)/shard_map/ppermute | solution.py:25
  18.5 0.0 copy-start
  18.5 0.0 copy-start.1
  18.5 0.0 copy-start.4
  18.5 0.0 copy-start.5
  18.5 0.0 copy-start.7
  18.5 0.0 copy-start.8
  18.5 0.0 collective-permute-start
  18.5 0.0 copy-done.2
  18.5 0.0 copy-done.3
  18.6 0.0 copy-done.6
  18.6 4.4 %own.2 = bf16[32,32,128]{2,1,0:T(8,128)(2,1)S(1)} custom-call(s32[9,1,16]{2,1,0:T(1,128)S(1)} %bitcast.15, bf16[9,16,8,8,128]{4,3,2,1,0:T(8,128)(2,1)S(1)} %bitcast.10, s32[1,9,16,2048]{3,2,1,0:T(8,128)S(1)} %copy-done.3), custom_call_target="tpu_custom_call" | custom-call | flops 2147483648 | bytes 4000000 | tf_op jit(solution)/shard_map/own/pallas_call | solution.py:385
  23.0 4.4 %collective-permute-done.right = bf16[51,32,128]{2,1,0:T(8,128)(2,1)S(1)} collective-permute-done((bf16[51,32,128]{2,1,0:T(8,128)(2,1)}, bf16[51,32,128]{2,1,0:T(8,128)(2,1)S(1)}, u32[]{:S(2)}, u32[]{:S(2)}) %collective-permute-start) | collective-permute-done | bytes 417824 | tf_op jit(solution)/shard_map/ppermute | solution.py:25
  27.4 0.0 collective-permute-done.1.left
  27.4 0.0 copy-done
  27.4 0.0 copy-done.1
  27.4 0.1 join.1
  27.5 0.7 %collective-permute-start.3 = (bf16[20,32,128]{2,1,0:T(8,128)(2,1)S(1)}, bf16[20,32,128]{2,1,0:T(8,128)(2,1)S(1)}, u32[]{:S(2)}, u32[]{:S(2)}) collective-permute-start(bf16[20,32,128]{2,1,0:T(8,128)(2,1)S(1)} %get-tuple-element.16.rest_0_), channel_id=1, source_target_pairs={{0,1},{1,2},{2,3},{3,4},{4,5},{5,6},{6,7},{7,8},{8,9},{9,10},{10,1... | collective-permute-start | bytes 491528 | tf_op jit(solution)/shard_map/ppermute | solution.py:25
  28.3 6.2 %collective-permute-start.2 = (bf16[19,32,128]{2,1,0:T(8,128)(2,1)S(1)}, bf16[19,32,128]{2,1,0:T(8,128)(2,1)S(1)}, u32[]{:S(2)}, u32[]{:S(2)}) collective-permute-start(bf16[19,32,128]{2,1,0:T(8,128)(2,1)S(1)} %get-tuple-element.17), channel_id=1, source_target_pairs={{0,15},{1,0},{2,1},{3,2},{4,3},{5,4},{6,5},{7,6},{8,7},{9,8},{10,9... | collective-permute-start | bytes 466952 | tf_op jit(solution)/shard_map/ppermute | solution.py:25
  34.4 0.0 copy-done.4
  34.4 0.0 copy-done.5
  34.4 0.0 copy-done.7
  34.4 0.0 copy-done.8
  34.4 2.5 %base.1.part = f32[512,128]{1,0:T(8,128)S(1)} custom-call(s32[2,4,16]{2,1,0:T(4,128)S(1)} %copy-done.7, bf16[2,4,8,8,128]{4,3,2,1,0:T(8,128)(2,1)S(1)} %bitcast.13, s32[2,4,16,128]{3,2,1,0:T(8,128)S(1)} %copy-done.5, bf16[3,32,128]{2,1,0:T(8,128)(2,1)S(1)} %copy-done, bf16[51,32,128]{2,1,0:T(8,128)(2,1)S(1)} %collective-permute-done.right, ...), custom_call_target="tpu_custom_call" | custom-call | flops 603979776 | bytes 1000000 | tf_op jit(solution)/shard_map/base/pallas_call | solution.py:478
  37.0 2.8 %own.3 = bf16[16,32,128]{2,1,0:T(8,128)(2,1)S(1)} custom-call(s32[9,1,16]{2,1,0:T(1,128)S(1)} %bitcast.16, bf16[9,16,8,8,128]{4,3,2,1,0:T(8,128)(2,1)S(1)} %bitcast.11, s32[1,9,16,2048]{3,2,1,0:T(8,128)S(1)} %copy-done.3, bf16[20,32,128]{2,1,0:T(8,128)(2,1)S(1)} %get-tuple-element.16.rest_0_), custom_call_target="tpu_custom_call" | custom-call | flops 1073741824 | bytes 4000000 | tf_op jit(solution)/shard_map/own/pallas_call | solution.py:385
  39.7 0.0 collective-permute-done.2.up
  39.7 0.0 collective-permute-done.3.down
  39.8 2.1 %last.1 = (f32[512,128]{1,0:T(8,128)}, f32[16,4096]{1,0:T(8,128)}) custom-call(f32[512,128]{1,0:T(8,128)S(1)} %base.1.part, bf16[16,32,128]{2,1,0:T(8,128)(2,1)S(1)} %own.3, bf16[51,32,128]{2,1,0:T(8,128)(2,1)S(1)} %collective-permute-done.right, bf16[54,32,128]{2,1,0:T(8,128)(2,1)S(1)} %collective-permute-done.1.left, ...), custom_call_target="tpu_custom_call" | custom-call | tf_op jit(solution)/shard_map/last/pallas_call | solution.py:562
Async XLA Ops:
  0.6 17.9 %copy-start.2 = (bf16[1,9,16,4,2048]{4,3,2,1,0:T(4,128)(2,1)S(1)}, bf16[1,9,16,4,2048]{4,3,2,1,0:T(4,128)(2,1)}, u32[]{:S(2)}) copy-start(bf16[1,9,16,4,2048]{4,3,2,1,0:T(4,128)(2,1)} %param.12) | copy-start | bytes 7077892
  0.6 17.9 %copy-start.3 = (s32[1,9,16,2048]{3,2,1,0:T(8,128)S(1)}, s32[1,9,16,2048]{3,2,1,0:T(8,128)}, u32[]{:S(2)}) copy-start(s32[1,9,16,2048]{3,2,1,0:T(8,128)} %cells.3) | copy-start | bytes 3538948
  0.7 17.9 %copy-start.6 = (s32[1,9,16]{2,0,1:T(1,128)S(1)}, s32[1,9,16]{2,0,1:T(1,128)}, u32[]{:S(2)}) copy-start(s32[1,9,16]{2,0,1:T(1,128)} %param.14) | copy-start | bytes 1732
  16.7 10.7 %collective-permute-start.1 = (bf16[54,32,128]{2,1,0:T(8,128)(2,1)}, bf16[54,32,128]{2,1,0:T(8,128)(2,1)S(1)}, u32[]{:S(2)}, u32[]{:S(2)}) collective-permute-start(bf16[54,32,128]{2,1,0:T(8,128)(2,1)} %get-tuple-element.13), channel_id=1, source_target_pairs={{0,16},{16,32},{32,48},{48,64},{64,80},{80,96},{96,112},{112,0},{1... | collective-permute-start | bytes 1327112 | tf_op jit(solution)/shard_map/ppermute | solution.py:25
  18.5 8.9 %copy-start = (bf16[3,32,128]{2,1,0:T(8,128)(2,1)S(1)}, bf16[3,32,128]{2,1,0:T(8,128)(2,1)}, u32[]{:S(2)}) copy-start(bf16[3,32,128]{2,1,0:T(8,128)(2,1)} %get-tuple-element.11.packs) | copy-start | bytes 73732
  18.5 8.9 %copy-start.1 = (f32[16,128]{1,0:T(8,128)S(1)}, f32[16,128]{1,0:T(8,128)}, u32[]{:S(2)}) copy-start(f32[16,128]{1,0:T(8,128)} %get-tuple-element.15.face_y) | copy-start | bytes 24580
  18.5 15.9 %copy-start.4 = (bf16[2,4,16,4,128]{4,3,2,1,0:T(4,128)(2,1)S(1)}, bf16[2,4,16,4,128]{4,3,2,1,0:T(4,128)(2,1)}, u32[]{:S(2)}) copy-start(bf16[2,4,16,4,128]{4,3,2,1,0:T(4,128)(2,1)} %param.9) | copy-start | bytes 393220
  18.5 15.9 %copy-start.5 = (s32[2,4,16,128]{3,2,1,0:T(8,128)S(1)}, s32[2,4,16,128]{3,2,1,0:T(8,128)}, u32[]{:S(2)}) copy-start(s32[2,4,16,128]{3,2,1,0:T(8,128)} %tcells.1) | copy-start | bytes 196612
  18.5 15.9 %copy-start.7 = (s32[2,4,16]{2,1,0:T(4,128)S(1)}, s32[2,4,16]{2,1,0:T(4,128)}, u32[]{:S(2)}) copy-start(s32[2,4,16]{2,1,0:T(4,128)} %tcounts.3) | copy-start | bytes 1540
  18.5 15.9 %copy-start.8 = (f32[16,32,128]{2,1,0:T(8,128)S(1)}, f32[16,32,128]{2,1,0:T(8,128)}, u32[]{:S(2)}) copy-start(f32[16,32,128]{2,1,0:T(8,128)} %get-tuple-element.14.core) | copy-start | bytes 786436
  18.5 8.9 %collective-permute-start = (bf16[51,32,128]{2,1,0:T(8,128)(2,1)}, bf16[51,32,128]{2,1,0:T(8,128)(2,1)S(1)}, u32[]{:S(2)}, u32[]{:S(2)}) collective-permute-start(bf16[51,32,128]{2,1,0:T(8,128)(2,1)} %get-tuple-element.12), channel_id=1, source_target_pairs={{0,112},{16,0},{32,16},{48,32},{64,48},{80,64},{96,80},{112,96},{1... | collective-permute-start | bytes 1253384 | tf_op jit(solution)/shard_map/ppermute | solution.py:25
  27.5 12.2 %collective-permute-start.3 = (bf16[20,32,128]{2,1,0:T(8,128)(2,1)S(1)}, bf16[20,32,128]{2,1,0:T(8,128)(2,1)S(1)}, u32[]{:S(2)}, u32[]{:S(2)}) collective-permute-start(bf16[20,32,128]{2,1,0:T(8,128)(2,1)S(1)} %get-tuple-element.16.rest_0_), channel_id=1, source_target_pairs={{0,1},{1,2},{2,3},{3,4},{4,5},{5,6},{6,7},{7,8},{8,9},{9,10},{10,1... | collective-permute-start | bytes 491528 | tf_op jit(solution)/shard_map/ppermute | solution.py:25
  28.3 11.5 %collective-permute-start.2 = (bf16[19,32,128]{2,1,0:T(8,128)(2,1)S(1)}, bf16[19,32,128]{2,1,0:T(8,128)(2,1)S(1)}, u32[]{:S(2)}, u32[]{:S(2)}) collective-permute-start(bf16[19,32,128]{2,1,0:T(8,128)(2,1)S(1)} %get-tuple-element.17), channel_id=1, source_target_pairs={{0,15},{1,0},{2,1},{3,2},{4,3},{5,4},{6,5},{7,6},{8,7},{9,8},{10,9... | collective-permute-start | bytes 466952 | tf_op jit(solution)/shard_map/ppermute | solution.py:25

commit v7 on v6

--- a/solution.py
+++ b/solution.py
@@ -14,7 +14,7 @@
 LANES = 256
 FIRST_UNROLLS = (48, 16)
 OWN_UNROLLS = (48, 16)
-EXTRA = 64
+EXTRA = 24
 OUTER = (0, 1, 2, 6, 7, 8)
 VMEM_LIMIT = 16 * 2**20
 FIRST_LIMIT = 56 * 2**20
@@ -328,12 +328,12 @@
             pltpu.VMEM(tdata.shape, BF16),
             pltpu.VMEM(tcells.shape, I32),
             pltpu.VMEM((17, 40, 128), F32),
-            pltpu.VMEM((8, 48, 128), F32),
-            pltpu.VMEM((8, 8, 128), F32),
+            pltpu.VMEM((8, 56, 128), F32),
+            pltpu.VMEM((8, 16, 128), F32),
             pltpu.VMEM((144, 256), F32),
             pltpu.VMEM((patches, 64, 128), F32),
-            pltpu.VMEM((max(FIRST_UNROLLS), 32, 128), F32),
-            pltpu.VMEM((max(FIRST_UNROLLS), 8, LANES), F32),
+            pltpu.VMEM((max(FIRST_UNROLLS), 40, 128), F32),
+            pltpu.VMEM((max(FIRST_UNROLLS), 16, LANES), F32),
             pltpu.VMEM((32, 128), F32),
             pltpu.SMEM((patches + EXTRA,), I32),
             pltpu.SemaphoreType.DMA((16,)),
@@ -388,8 +388,8 @@
         out_specs=full,
         scratch_shapes=[
             pltpu.VMEM((patches, 64, 128), F32),
-            pltpu.VMEM((max(OWN_UNROLLS), 32, 128), F32),
-            pltpu.VMEM((max(OWN_UNROLLS), 8, LANES), F32),
+            pltpu.VMEM((max(OWN_UNROLLS), 40, 128), F32),
+            pltpu.VMEM((max(OWN_UNROLLS), 16, LANES), F32),
             pltpu.SMEM((patches + EXTRA,), I32),
         ],
         out_shape=jax.ShapeDtypeStruct((patches, 32, 128), BF16),
@@ -482,10 +482,10 @@
         out_shape=jax.ShapeDtypeStruct((512, 128), F32),
         scratch_shapes=[
             pltpu.VMEM((2, 32, 128), F32),
-            pltpu.VMEM((2, 32, 512), F32),
+            pltpu.VMEM((2, 40, 512), F32),
             pltpu.VMEM((17, 40, 128), F32),
-            pltpu.VMEM((8, 48, 128), F32),
-            pltpu.VMEM((8, 8, 128), F32),
+            pltpu.VMEM((8, 56, 128), F32),
+            pltpu.VMEM((8, 16, 128), F32),
             pltpu.VMEM((144, 256), F32),
         ],
         compiler_params=pltpu.CompilerParams(vmem_limit_bytes=VMEM_LIMIT),
@@ -569,7 +569,7 @@
         ],
         scratch_shapes=[
             pltpu.VMEM((512, 128), F32),
-            pltpu.VMEM((2, 32, 512), F32),
+            pltpu.VMEM((2, 40, 512), F32),
             pltpu.VMEM((2, 32, 128), F32),
             pltpu.VMEM((512, 128), F32),
             pltpu.VMEM((16, 4096), F32),

time: 41.8 us -> 42 us (level)
  the two profiles are of different devices: /device:TPU:7 before, /device:TPU:1 now
where the time goes in v7:
time: 42 us; the launch traced here: 42.4 us
  Pallas kernels  29 us (69%)
  starting transfers between devices  9.61 us (23%)
  waiting for transfers between devices  3.05 us (7%)
  between operations  0.77 us (2%)
    pallas_call x1, Pallas kernels, first_part(): pl.pallas_call(first_kernel, in_specs=[smem] * 3 + [hbm] * 6, out_specs=[...  16.5 us
    ppermute x4, starting transfers between devices, shift(): lax.ppermute(x, axis, [(i, (i + by) % devices) for i in range(devices)])  9.61 us
    pallas_call x2, Pallas kernels, own_part(): pl.pallas_call(functools.partial(own_kernel, offsets), in_specs=[smem, fu...  7.77 us
    ppermute x4, waiting for transfers between devices, shift(): lax.ppermute(x, axis, [(i, (i + by) % devices) for i in range(devices)])  3.05 us
    pallas_call x1, Pallas kernels, base_part(): pl.pallas_call(base_kernel, in_specs=[smem] + [full] * 6, out_specs=full,...  2.54 us
    pallas_call x1, Pallas kernels, last_part(): pl.pallas_call(last_kernel, in_specs=[full] * 6, out_specs=[pl.BlockSpec(...  2.07 us
  transfers between devices with their start and end apart: 4, of which 1 were waited for; matrix products, arithmetic and copies ran while one was open for 0% of the time, Pallas kernels for 24%

profile of v7, /device:TPU:1, one launch (start us, length us, event | category | flops | bytes accessed | tf_op | source)
XLA Modules:
  0.0 42.4 jit_solution(12870833015018857168)
XLA Ops:
  0.6 0.0 copy-start.2
  0.6 0.0 copy-start.3
  0.7 0.0 copy-start.6
  0.7 16.5 %first.1 = (bf16[51,32,128]{2,1,0:T(8,128)(2,1)}, bf16[54,32,128]{2,1,0:T(8,128)(2,1)}, bf16[3,32,128]{2,1,0:T(8,128)(2,1)}, f32[16,32,128]{2,1,0:T(8,128)}, f32[16,128]{1,0:T(8,128)}) custom-call(s32[9,1,16]{2,1,0:T(1,128)} %bitcast.14, s32[1,9]{1,0:T(1,128)} %vcounts.1, s32[2,4,16]{2,1,0:T(4,128)} %tcounts.3, bf16[9,16,8,8,128]{4,3,2,1,0:T(8,128)(2,1)} %bitcast.9, ...), custom_call_target="tpu_custom_call" | custom-call | flops 6442450944 | bytes 4000000 | tf_op jit(solution)/shard_map/first/pallas_call | solution.py:319
  17.1 2.8 %collective-permute-start.1 = (bf16[54,32,128]{2,1,0:T(8,128)(2,1)}, bf16[54,32,128]{2,1,0:T(8,128)(2,1)S(1)}, u32[]{:S(2)}, u32[]{:S(2)}) collective-permute-start(bf16[54,32,128]{2,1,0:T(8,128)(2,1)} %get-tuple-element.13), channel_id=1, source_target_pairs={{0,16},{16,32},{32,48},{48,64},{64,80},{80,96},{96,112},{112,0},{1... | collective-permute-start | bytes 1327112 | tf_op jit(solution)/shard_map/ppermute | solution.py:25
  19.9 0.0 copy-start
  19.9 0.0 copy-start.1
  19.9 0.0 copy-start.4
  19.9 0.0 copy-start.5
  19.9 0.0 copy-start.7
  20.0 0.0 copy-start.8
  20.0 0.0 collective-permute-start
  20.0 0.0 copy-done.2
  20.0 0.0 copy-done.3
  20.0 0.0 copy-done.6
  20.0 4.6 %own.2 = bf16[32,32,128]{2,1,0:T(8,128)(2,1)S(1)} custom-call(s32[9,1,16]{2,1,0:T(1,128)S(1)} %bitcast.15, bf16[9,16,8,8,128]{4,3,2,1,0:T(8,128)(2,1)S(1)} %bitcast.10, s32[1,9,16,2048]{3,2,1,0:T(8,128)S(1)} %copy-done.3), custom_call_target="tpu_custom_call" | custom-call | flops 2147483648 | bytes 4000000 | tf_op jit(solution)/shard_map/own/pallas_call | solution.py:385
  24.6 3.0 %collective-permute-done.right = bf16[51,32,128]{2,1,0:T(8,128)(2,1)S(1)} collective-permute-done((bf16[51,32,128]{2,1,0:T(8,128)(2,1)}, bf16[51,32,128]{2,1,0:T(8,128)(2,1)S(1)}, u32[]{:S(2)}, u32[]{:S(2)}) %collective-permute-start) | collective-permute-done | bytes 417824 | tf_op jit(solution)/shard_map/ppermute | solution.py:25
  27.7 0.0 collective-permute-done.1.left
  27.7 0.0 copy-done
  27.7 0.0 copy-done.1
  27.7 0.1 join.1
  27.8 0.9 %collective-permute-start.3 = (bf16[20,32,128]{2,1,0:T(8,128)(2,1)S(1)}, bf16[20,32,128]{2,1,0:T(8,128)(2,1)S(1)}, u32[]{:S(2)}, u32[]{:S(2)}) collective-permute-start(bf16[20,32,128]{2,1,0:T(8,128)(2,1)S(1)} %get-tuple-element.16.rest_0_), channel_id=1, source_target_pairs={{0,1},{1,2},{2,3},{3,4},{4,5},{5,6},{6,7},{7,8},{8,9},{9,10},{10,1... | collective-permute-start | bytes 491528 | tf_op jit(solution)/shard_map/ppermute | solution.py:25
  28.7 5.9 %collective-permute-start.2 = (bf16[19,32,128]{2,1,0:T(8,128)(2,1)S(1)}, bf16[19,32,128]{2,1,0:T(8,128)(2,1)S(1)}, u32[]{:S(2)}, u32[]{:S(2)}) collective-permute-start(bf16[19,32,128]{2,1,0:T(8,128)(2,1)S(1)} %get-tuple-element.17), channel_id=1, source_target_pairs={{0,15},{1,0},{2,1},{3,2},{4,3},{5,4},{6,5},{7,6},{8,7},{9,8},{10,9... | collective-permute-start | bytes 466952 | tf_op jit(solution)/shard_map/ppermute | solution.py:25
  34.6 0.0 copy-done.4
  34.6 0.0 copy-done.5
  34.6 0.0 copy-done.7
  34.6 0.0 copy-done.8
  34.6 2.5 %base.1.part = f32[512,128]{1,0:T(8,128)S(1)} custom-call(s32[2,4,16]{2,1,0:T(4,128)S(1)} %copy-done.7, bf16[2,4,8,8,128]{4,3,2,1,0:T(8,128)(2,1)S(1)} %bitcast.13, s32[2,4,16,128]{3,2,1,0:T(8,128)S(1)} %copy-done.5, bf16[3,32,128]{2,1,0:T(8,128)(2,1)S(1)} %copy-done, bf16[51,32,128]{2,1,0:T(8,128)(2,1)S(1)} %collective-permute-done.right, ...), custom_call_target="tpu_custom_call" | custom-call | flops 603979776 | bytes 1000000 | tf_op jit(solution)/shard_map/base/pallas_call | solution.py:478
  37.1 3.2 %own.3 = bf16[16,32,128]{2,1,0:T(8,128)(2,1)S(1)} custom-call(s32[9,1,16]{2,1,0:T(1,128)S(1)} %bitcast.16, bf16[9,16,8,8,128]{4,3,2,1,0:T(8,128)(2,1)S(1)} %bitcast.11, s32[1,9,16,2048]{3,2,1,0:T(8,128)S(1)} %copy-done.3, bf16[20,32,128]{2,1,0:T(8,128)(2,1)S(1)} %get-tuple-element.16.rest_0_), custom_call_target="tpu_custom_call" | custom-call | flops 1073741824 | bytes 4000000 | tf_op jit(solution)/shard_map/own/pallas_call | solution.py:385
  40.3 0.0 collective-permute-done.2.up
  40.3 0.0 collective-permute-done.3.down
  40.3 2.1 %last.1 = (f32[512,128]{1,0:T(8,128)}, f32[16,4096]{1,0:T(8,128)}) custom-call(f32[512,128]{1,0:T(8,128)S(1)} %base.1.part, bf16[16,32,128]{2,1,0:T(8,128)(2,1)S(1)} %own.3, bf16[51,32,128]{2,1,0:T(8,128)(2,1)S(1)} %collective-permute-done.right, bf16[54,32,128]{2,1,0:T(8,128)(2,1)S(1)} %collective-permute-done.1.left, ...), custom_call_target="tpu_custom_call" | custom-call | tf_op jit(solution)/shard_map/last/pallas_call | solution.py:562
Async XLA Ops:
  0.6 19.4 %copy-start.2 = (bf16[1,9,16,4,2048]{4,3,2,1,0:T(4,128)(2,1)S(1)}, bf16[1,9,16,4,2048]{4,3,2,1,0:T(4,128)(2,1)}, u32[]{:S(2)}) copy-start(bf16[1,9,16,4,2048]{4,3,2,1,0:T(4,128)(2,1)} %param.12) | copy-start | bytes 7077892
  0.6 19.4 %copy-start.3 = (s32[1,9,16,2048]{3,2,1,0:T(8,128)S(1)}, s32[1,9,16,2048]{3,2,1,0:T(8,128)}, u32[]{:S(2)}) copy-start(s32[1,9,16,2048]{3,2,1,0:T(8,128)} %cells.3) | copy-start | bytes 3538948
  0.7 19.4 %copy-start.6 = (s32[1,9,16]{2,0,1:T(1,128)S(1)}, s32[1,9,16]{2,0,1:T(1,128)}, u32[]{:S(2)}) copy-start(s32[1,9,16]{2,0,1:T(1,128)} %param.14) | copy-start | bytes 1732
  17.1 10.5 %collective-permute-start.1 = (bf16[54,32,128]{2,1,0:T(8,128)(2,1)}, bf16[54,32,128]{2,1,0:T(8,128)(2,1)S(1)}, u32[]{:S(2)}, u32[]{:S(2)}) collective-permute-start(bf16[54,32,128]{2,1,0:T(8,128)(2,1)} %get-tuple-element.13), channel_id=1, source_target_pairs={{0,16},{16,32},{32,48},{48,64},{64,80},{80,96},{96,112},{112,0},{1... | collective-permute-start | bytes 1327112 | tf_op jit(solution)/shard_map/ppermute | solution.py:25
  19.9 7.7 %copy-start = (bf16[3,32,128]{2,1,0:T(8,128)(2,1)S(1)}, bf16[3,32,128]{2,1,0:T(8,128)(2,1)}, u32[]{:S(2)}) copy-start(bf16[3,32,128]{2,1,0:T(8,128)(2,1)} %get-tuple-element.11.packs) | copy-start | bytes 73732
  19.9 7.7 %copy-start.1 = (f32[16,128]{1,0:T(8,128)S(1)}, f32[16,128]{1,0:T(8,128)}, u32[]{:S(2)}) copy-start(f32[16,128]{1,0:T(8,128)} %get-tuple-element.15.face_y) | copy-start | bytes 24580
  19.9 14.6 %copy-start.4 = (bf16[2,4,16,4,128]{4,3,2,1,0:T(4,128)(2,1)S(1)}, bf16[2,4,16,4,128]{4,3,2,1,0:T(4,128)(2,1)}, u32[]{:S(2)}) copy-start(bf16[2,4,16,4,128]{4,3,2,1,0:T(4,128)(2,1)} %param.9) | copy-start | bytes 393220
  19.9 14.6 %copy-start.5 = (s32[2,4,16,128]{3,2,1,0:T(8,128)S(1)}, s32[2,4,16,128]{3,2,1,0:T(8,128)}, u32[]{:S(2)}) copy-start(s32[2,4,16,128]{3,2,1,0:T(8,128)} %tcells.1) | copy-start | bytes 196612
  19.9 14.6 %copy-start.7 = (s32[2,4,16]{2,1,0:T(4,128)S(1)}, s32[2,4,16]{2,1,0:T(4,128)}, u32[]{:S(2)}) copy-start(s32[2,4,16]{2,1,0:T(4,128)} %tcounts.3) | copy-start | bytes 1540
  20.0 14.6 %copy-start.8 = (f32[16,32,128]{2,1,0:T(8,128)S(1)}, f32[16,32,128]{2,1,0:T(8,128)}, u32[]{:S(2)}) copy-start(f32[16,32,128]{2,1,0:T(8,128)} %get-tuple-element.14.core) | copy-start | bytes 786436
  20.0 7.7 %collective-permute-start = (bf16[51,32,128]{2,1,0:T(8,128)(2,1)}, bf16[51,32,128]{2,1,0:T(8,128)(2,1)S(1)}, u32[]{:S(2)}, u32[]{:S(2)}) collective-permute-start(bf16[51,32,128]{2,1,0:T(8,128)(2,1)} %get-tuple-element.12), channel_id=1, source_target_pairs={{0,112},{16,0},{32,16},{48,32},{64,48},{80,64},{96,80},{112,96},{1... | collective-permute-start | bytes 1253384 | tf_op jit(solution)/shard_map/ppermute | solution.py:25
  27.8 12.6 %collective-permute-start.3 = (bf16[20,32,128]{2,1,0:T(8,128)(2,1)S(1)}, bf16[20,32,128]{2,1,0:T(8,128)(2,1)S(1)}, u32[]{:S(2)}, u32[]{:S(2)}) collective-permute-start(bf16[20,32,128]{2,1,0:T(8,128)(2,1)S(1)} %get-tuple-element.16.rest_0_), channel_id=1, source_target_pairs={{0,1},{1,2},{2,3},{3,4},{4,5},{5,6},{6,7},{7,8},{8,9},{9,10},{10,1... | collective-permute-start | bytes 491528 | tf_op jit(solution)/shard_map/ppermute | solution.py:25
  28.7 11.6 %collective-permute-start.2 = (bf16[19,32,128]{2,1,0:T(8,128)(2,1)S(1)}, bf16[19,32,128]{2,1,0:T(8,128)(2,1)S(1)}, u32[]{:S(2)}, u32[]{:S(2)}) collective-permute-start(bf16[19,32,128]{2,1,0:T(8,128)(2,1)S(1)} %get-tuple-element.17), channel_id=1, source_target_pairs={{0,15},{1,0},{2,1},{3,2},{4,3},{5,4},{6,5},{7,6},{8,7},{9,8},{10,9... | collective-permute-start | bytes 466952 | tf_op jit(solution)/shard_map/ppermute | solution.py:25
